TPU v7x, 32 devices: a whole 2x2x4 slice. The times are simulated.
32 devices in a mesh: term: 2 (over x), sector: 16 (over z, y, core).
Axes of the slice: x: 2, y: 2, z: 4, core: 2. Of those that a mesh axis runs over, the one named last changes fastest.
Arguments:
- wave_tiles: bfloat16 [256, 2, 128, 128], P('sector'), may hold values from -6 to 6
- left_env: bfloat16 [2, 16, 128, 128], P('term', 'sector'), may hold values from -0.5 to 0.5
- right_env: bfloat16 [2, 16, 128, 128], P('term', 'sector'), may hold values from -0.5 to 0.5
- send_list: int32 [16, 32], P('sector'), may hold values from -1 to 15, as said below
- left_tasks: int32 [2, 16, 96, 3], P('term', 'sector'), may hold values from 0 to 31, as said below
- right_tasks: int32 [2, 16, 256, 3], P('term', 'sector'), may hold values from 0 to 31, as said below
Outputs:
- sigma: float32 [256, 2, 128, 128], P('sector', None, 'term')
Inputs may be any that keep to these rules, and one draw needn't show every extreme that they name: send_list[s, o * 2 + c] is a tile index local to sender s, or -1 for an empty slot; some owner drawn from the seed receives a full 2 tiles from every sender. `left_tasks`: entries 0, 1, 2 lie below 16, 32 and 32. `right_tasks`: entries 0, 1, 2 lie below 32, 16 and 16.
All inputs are finite; a program needn't handle non-finite values.
Results may differ from a plain program's by a relative error of at most 0.0029.
Values may be sent and summed in bfloat16 or wider, within the bound.
No kernel may reach another device: no remote copies, remote signals or barrier semaphores. Data moves between devices by JAX's collectives and lax.ppermute only.
A program may use at most 128 MiB of HBM per device.

v0:
```python
import math

import jax
import jax.numpy as jnp
from jax import lax
from jax.sharding import PartitionSpec as P

INTER_TILES = 32


def run_tasks(tasks, first_tiles, second_tiles, contract, count):
    block = math.gcd(tasks.shape[0], 32)
    shape = (count,) + tuple(contract(first_tiles[:1], second_tiles[:1]).shape[1:])

    def step(turn, total):
        rows = lax.dynamic_slice_in_dim(tasks, turn * block, block, 0)
        first = jnp.take(first_tiles, rows[:, 0], axis=0)
        second = jnp.take(second_tiles, rows[:, 1], axis=0)
        return total.at[rows[:, 2]].add(contract(first, second))

    return lax.fori_loop(0, tasks.shape[0] // block, step, jnp.zeros(shape, jnp.float32))


def left_product(env_part, wave_part):
    return jnp.einsum("bij,bvjk->bvik", env_part, wave_part, preferred_element_type=jnp.float32)


def right_product(inter_part, env_part):
    return jnp.einsum("bvij,bjk->bvik", inter_part, env_part, preferred_element_type=jnp.float32)


def shards(wave_tiles, left_env, right_env, send_list, left_tasks, right_tasks):
    env_left, env_right = (
        lax.all_gather(left_env, "sector", axis=1, tiled=True),
        lax.all_gather(right_env, "sector", axis=1, tiled=True),
    )
    env_left = env_left[0]
    env_right = env_right[0]
    slot_list = send_list[0]
    live = slot_list >= 0
    picked = jnp.take(wave_tiles, jnp.maximum(slot_list, 0), axis=0)
    outgoing = jnp.where(live[:, None, None, None], picked, jnp.zeros((), jnp.bfloat16))
    tile_dim = wave_tiles.shape[2]
    groups = lax.axis_size("term")
    share = tile_dim // groups
    received = lax.all_to_all(outgoing, "sector", split_axis=0, concat_axis=0, tiled=True)
    inter = run_tasks(left_tasks[0, 0], env_left, received, left_product, INTER_TILES).astype(
        jnp.bfloat16
    )
    partial_value = run_tasks(
        right_tasks[0, 0], inter, env_right, right_product, wave_tiles.shape[0]
    )
    summed = lax.psum(partial_value, "term")
    return lax.dynamic_slice_in_dim(summed, lax.axis_index("term") * share, share, 2)


def solution(mesh):
    in_specs = (
        P("sector", None, None, None),
        P("term", "sector", None, None),
        P("term", "sector", None, None),
        P("sector", None),
        P("term", "sector", None, None),
        P("term", "sector", None, None),
    )
    out_specs = P("sector", None, "term", None)
    return jax.shard_map(shards, mesh=mesh, in_specs=in_specs, out_specs=out_specs, check_vma=False)
```

profile of v0, /device:TPU:0, one launch (start us, length us, event | category | flops | bytes accessed | tf_op | source)
XLA Modules:
  0.0 398.8 jit_solution(8511671757382589006)
XLA Ops:
  6.5 0.7 compare_bitcast_fusion.1
  7.3 0.7 maximum_bitcast_fusion
  8.0 1.0 gather_fusion.4
  8.9 1.7 select_select_fusion
  10.6 7.5 %all-to-all-start = ((bf16[32,2,128,128]{3,2,1,0:T(8,128)(2,1)}), bf16[32,2,128,128]{3,2,1,0:T(8,128)(2,1)S(1)}, u32[]{:S(2)}, u32[]{:S(2)}) async-start(bf16[32,2,128,128]{3,2,1,0:T(8,128)(2,1)} %select_select_fusion), calls=%async_computation | async-start | bytes 4194304 | tf_op jit(solution)/shard_map/all_to_all | solution.py:46
  18.2 57.3 %all_gather.6 = bf16[1,16,128,128]{3,2,0,1:T(8,128)(2,1)} all-gather(bf16[1,1,128,128]{3,2,0,1:T(8,128)(2,1)S(1)} %bitcast.58), channel_id=1, replica_groups=mesh['term'=2,'sector'=16] {'sector'}, dimensions={1}, use_global_device_ids=true | all-gather | bytes 557056 | tf_op jit(solution)/shard_map/all_gather | solution.py:34
  75.6 26.1 %all_gather.7 = bf16[1,16,128,128]{3,2,0,1:T(8,128)(2,1)} all-gather(bf16[1,1,128,128]{3,2,0,1:T(8,128)(2,1)S(1)} %bitcast.59), channel_id=1, replica_groups=mesh['term'=2,'sector'=16] {'sector'}, dimensions={1}, use_global_device_ids=true | all-gather | bytes 557056 | tf_op jit(solution)/shard_map/all_gather | solution.py:35
  101.7 2.5 broadcast_in_dim.54
  104.2 78.6 %while.26 = (s32[]{:T(128)}, f32[32,2,128,128]{3,2,1,0:T(8,128)}, s32[96,3]{0,1:T(4,128)S(1)}, bf16[32,2,128,128]{3,2,1,0:T(8,128)(2,1)S(1)}, bf16[16,128,128]{2...) while((s32[]{:T(128)}, f32[32,2,128,128]{3,2,1,0:T(8,128)}, s32[96,3]{0,1:T(4,128)S(1)}, ...), condition=%wide.region_2.0_spmd, body=%wide.region_0.4_spmd.sunk | while | flops 271059424 | bytes 51390916 | solution.py:21
  104.3 1.2 copy-done.2
  105.5 2.5 gather_fusion
  108.0 2.7 gather_fusion.1
  110.7 4.0 %convolution_bitcast_fusion.2 = f32[32,2,128,128]{2,3,1,0:T(8,128)} fusion(bf16[32,2,128,128]{3,2,1,0:T(8,128)(2,1)S(1)} %gather_fusion, pred[32]{0:T(512)(128)(4,1)S(1)} %get-tuple-element.307, bf16[32,128,128]{2,1,0:T(8,128)(2,1)} %gather_fusion.1, pred[32]{0:T(512)(128)(4,1)S(1)} %get-tuple-element.309), kind=kOutput, calls=%fused_computation.7.clone.1 | convolution fusion | flops 270008320 | bytes 7340096 | tf_op jit(solution)/shard_map/while/body/eval_jaxpr/bij,bvjk->bvik/dot_general | solution.py:25
  114.8 5.6 %copy.23 = f32[32,2,128,128]{3,2,1,0:T(8,128)} copy(f32[32,2,128,128]{2,3,1,0:T(8,128)} %convolution_bitcast_fusion.2) | data formatting | bytes 8388608 | tf_op jit(solution)/shard_map/while/body/eval_jaxpr/bij,bvjk->bvik/transpose | solution.py:25
  120.4 10.0 %scatter_fusion = f32[32,2,128,128]{3,2,1,0:T(8,128)} fusion(f32[32,2,128,128]{3,2,1,0:T(8,128)} %get-tuple-element.331, s32[32]{0:T(128)S(1)} %fusion.28, f32[32,2,128,128]{3,2,1,0:T(8,128)} %copy.23), kind=kCustom, calls=%fused_computation.5.clone.1 | custom fusion | flops 1048576 | bytes 12583040 | tf_op jit(solution)/shard_map/while/body/eval_jaxpr/scatter-add | solution.py:19
  130.5 1.2 copy-done.2
  131.7 2.5 gather_fusion
  134.2 2.7 gather_fusion.1
  136.9 4.0 %convolution_bitcast_fusion.2 = f32[32,2,128,128]{2,3,1,0:T(8,128)} fusion(bf16[32,2,128,128]{3,2,1,0:T(8,128)(2,1)S(1)} %gather_fusion, pred[32]{0:T(512)(128)(4,1)S(1)} %get-tuple-element.307, bf16[32,128,128]{2,1,0:T(8,128)(2,1)} %gather_fusion.1, pred[32]{0:T(512)(128)(4,1)S(1)} %get-tuple-element.309), kind=kOutput, calls=%fused_computation.7.clone.1 | convolution fusion | flops 270008320 | bytes 7340096 | tf_op jit(solution)/shard_map/while/body/eval_jaxpr/bij,bvjk->bvik/dot_general | solution.py:25
  141.0 5.6 %copy.23 = f32[32,2,128,128]{3,2,1,0:T(8,128)} copy(f32[32,2,128,128]{2,3,1,0:T(8,128)} %convolution_bitcast_fusion.2) | data formatting | bytes 8388608 | tf_op jit(solution)/shard_map/while/body/eval_jaxpr/bij,bvjk->bvik/transpose | solution.py:25
  146.6 10.0 %scatter_fusion = f32[32,2,128,128]{3,2,1,0:T(8,128)} fusion(f32[32,2,128,128]{3,2,1,0:T(8,128)} %get-tuple-element.331, s32[32]{0:T(128)S(1)} %fusion.28, f32[32,2,128,128]{3,2,1,0:T(8,128)} %copy.23), kind=kCustom, calls=%fused_computation.5.clone.1 | custom fusion | flops 1048576 | bytes 12583040 | tf_op jit(solution)/shard_map/while/body/eval_jaxpr/scatter-add | solution.py:19
  156.7 1.2 copy-done.2
  157.9 2.5 gather_fusion
  160.5 2.7 gather_fusion.1
  163.2 4.0 %convolution_bitcast_fusion.2 = f32[32,2,128,128]{2,3,1,0:T(8,128)} fusion(bf16[32,2,128,128]{3,2,1,0:T(8,128)(2,1)S(1)} %gather_fusion, pred[32]{0:T(512)(128)(4,1)S(1)} %get-tuple-element.307, bf16[32,128,128]{2,1,0:T(8,128)(2,1)} %gather_fusion.1, pred[32]{0:T(512)(128)(4,1)S(1)} %get-tuple-element.309), kind=kOutput, calls=%fused_computation.7.clone.1 | convolution fusion | flops 270008320 | bytes 7340096 | tf_op jit(solution)/shard_map/while/body/eval_jaxpr/bij,bvjk->bvik/dot_general | solution.py:25
  167.2 5.6 %copy.23 = f32[32,2,128,128]{3,2,1,0:T(8,128)} copy(f32[32,2,128,128]{2,3,1,0:T(8,128)} %convolution_bitcast_fusion.2) | data formatting | bytes 8388608 | tf_op jit(solution)/shard_map/while/body/eval_jaxpr/bij,bvjk->bvik/transpose | solution.py:25
  172.8 10.0 %scatter_fusion = f32[32,2,128,128]{3,2,1,0:T(8,128)} fusion(f32[32,2,128,128]{3,2,1,0:T(8,128)} %get-tuple-element.331, s32[32]{0:T(128)S(1)} %fusion.28, f32[32,2,128,128]{3,2,1,0:T(8,128)} %copy.23), kind=kCustom, calls=%fused_computation.5.clone.1 | custom fusion | flops 1048576 | bytes 12583040 | tf_op jit(solution)/shard_map/while/body/eval_jaxpr/scatter-add | solution.py:19
  182.8 3.9 convert_element_type.3
  187.0 141.0 %while.27 = (s32[]{:T(128)}, f32[16,2,128,128]{3,2,1,0:T(8,128)S(1)}, s32[256,3]{0,1:T(4,128)S(1)}, bf16[32,2,128,128]{3,2,1,0:T(8,128)(2,1)}, bf16[16,128,128]{...) while((s32[]{:T(128)}, f32[16,2,128,128]{3,2,1,0:T(8,128)S(1)}, ...), condition=%wide.region_5.8_spmd, body=%wide.region_3.0_spmd.sunk | while | flops 271059424 | bytes 26225040 | solution.py:21
  187.1 3.7 gather_fusion.2
  190.8 2.7 gather_fusion.3
  193.5 4.6 %fusion.32 = f32[32,2,128,128]{3,2,1,0:T(8,128)} fusion(bf16[32,2,128,128]{3,2,1,0:T(8,128)(2,1)} %gather_fusion.2, pred[32]{0:T(512)(128)(4,1)S(1)} %get-tuple-element.318, bf16[32,128,128]{2,1,0:T(8,128)(2,1)} %gather_fusion.3, pred[32]{0:T(512)(128)(4,1)S(1)} %get-tuple-element.320), kind=kOutput, calls=%fused_computation.25.clone.1 | convolution fusion | flops 270008320 | bytes 7340096 | tf_op jit(solution)/shard_map/while/body/eval_jaxpr/bvij,bjk->bvik/dot_general | solution.py:29
  198.1 6.5 %scatter_fusion.1 = f32[16,2,128,128]{3,2,1,0:T(8,128)S(1)} fusion(f32[16,2,128,128]{3,2,1,0:T(8,128)S(1)} %get-tuple-element.358, s32[32]{0:T(128)S(1)} %fusion.31, f32[32,2,128,128]{3,2,1,0:T(8,128)} %fusion.32), kind=kCustom, calls=%fused_computation.6.clone.1 | custom fusion | flops 1048576 | bytes 12583040 | tf_op jit(solution)/shard_map/while/body/eval_jaxpr/scatter-add | solution.py:19
  204.7 3.7 gather_fusion.2
  208.5 2.7 gather_fusion.3
  211.1 4.6 %fusion.32 = f32[32,2,128,128]{3,2,1,0:T(8,128)} fusion(bf16[32,2,128,128]{3,2,1,0:T(8,128)(2,1)} %gather_fusion.2, pred[32]{0:T(512)(128)(4,1)S(1)} %get-tuple-element.318, bf16[32,128,128]{2,1,0:T(8,128)(2,1)} %gather_fusion.3, pred[32]{0:T(512)(128)(4,1)S(1)} %get-tuple-element.320), kind=kOutput, calls=%fused_computation.25.clone.1 | convolution fusion | flops 270008320 | bytes 7340096 | tf_op jit(solution)/shard_map/while/body/eval_jaxpr/bvij,bjk->bvik/dot_general | solution.py:29
  215.7 6.5 %scatter_fusion.1 = f32[16,2,128,128]{3,2,1,0:T(8,128)S(1)} fusion(f32[16,2,128,128]{3,2,1,0:T(8,128)S(1)} %get-tuple-element.358, s32[32]{0:T(128)S(1)} %fusion.31, f32[32,2,128,128]{3,2,1,0:T(8,128)} %fusion.32), kind=kCustom, calls=%fused_computation.6.clone.1 | custom fusion | flops 1048576 | bytes 12583040 | tf_op jit(solution)/shard_map/while/body/eval_jaxpr/scatter-add | solution.py:19
  222.4 3.7 gather_fusion.2
  226.1 2.7 gather_fusion.3
  228.8 4.6 %fusion.32 = f32[32,2,128,128]{3,2,1,0:T(8,128)} fusion(bf16[32,2,128,128]{3,2,1,0:T(8,128)(2,1)} %gather_fusion.2, pred[32]{0:T(512)(128)(4,1)S(1)} %get-tuple-element.318, bf16[32,128,128]{2,1,0:T(8,128)(2,1)} %gather_fusion.3, pred[32]{0:T(512)(128)(4,1)S(1)} %get-tuple-element.320), kind=kOutput, calls=%fused_computation.25.clone.1 | convolution fusion | flops 270008320 | bytes 7340096 | tf_op jit(solution)/shard_map/while/body/eval_jaxpr/bvij,bjk->bvik/dot_general | solution.py:29
  233.4 6.5 %scatter_fusion.1 = f32[16,2,128,128]{3,2,1,0:T(8,128)S(1)} fusion(f32[16,2,128,128]{3,2,1,0:T(8,128)S(1)} %get-tuple-element.358, s32[32]{0:T(128)S(1)} %fusion.31, f32[32,2,128,128]{3,2,1,0:T(8,128)} %fusion.32), kind=kCustom, calls=%fused_computation.6.clone.1 | custom fusion | flops 1048576 | bytes 12583040 | tf_op jit(solution)/shard_map/while/body/eval_jaxpr/scatter-add | solution.py:19
  240.0 3.7 gather_fusion.2
  243.7 2.7 gather_fusion.3
  246.4 4.6 %fusion.32 = f32[32,2,128,128]{3,2,1,0:T(8,128)} fusion(bf16[32,2,128,128]{3,2,1,0:T(8,128)(2,1)} %gather_fusion.2, pred[32]{0:T(512)(128)(4,1)S(1)} %get-tuple-element.318, bf16[32,128,128]{2,1,0:T(8,128)(2,1)} %gather_fusion.3, pred[32]{0:T(512)(128)(4,1)S(1)} %get-tuple-element.320), kind=kOutput, calls=%fused_computation.25.clone.1 | convolution fusion | flops 270008320 | bytes 7340096 | tf_op jit(solution)/shard_map/while/body/eval_jaxpr/bvij,bjk->bvik/dot_general | solution.py:29
  251.0 6.5 %scatter_fusion.1 = f32[16,2,128,128]{3,2,1,0:T(8,128)S(1)} fusion(f32[16,2,128,128]{3,2,1,0:T(8,128)S(1)} %get-tuple-element.358, s32[32]{0:T(128)S(1)} %fusion.31, f32[32,2,128,128]{3,2,1,0:T(8,128)} %fusion.32), kind=kCustom, calls=%fused_computation.6.clone.1 | custom fusion | flops 1048576 | bytes 12583040 | tf_op jit(solution)/shard_map/while/body/eval_jaxpr/scatter-add | solution.py:19
  257.6 3.7 gather_fusion.2
  261.4 2.7 gather_fusion.3
  264.1 4.6 %fusion.32 = f32[32,2,128,128]{3,2,1,0:T(8,128)} fusion(bf16[32,2,128,128]{3,2,1,0:T(8,128)(2,1)} %gather_fusion.2, pred[32]{0:T(512)(128)(4,1)S(1)} %get-tuple-element.318, bf16[32,128,128]{2,1,0:T(8,128)(2,1)} %gather_fusion.3, pred[32]{0:T(512)(128)(4,1)S(1)} %get-tuple-element.320), kind=kOutput, calls=%fused_computation.25.clone.1 | convolution fusion | flops 270008320 | bytes 7340096 | tf_op jit(solution)/shard_map/while/body/eval_jaxpr/bvij,bjk->bvik/dot_general | solution.py:29
  268.7 6.5 %scatter_fusion.1 = f32[16,2,128,128]{3,2,1,0:T(8,128)S(1)} fusion(f32[16,2,128,128]{3,2,1,0:T(8,128)S(1)} %get-tuple-element.358, s32[32]{0:T(128)S(1)} %fusion.31, f32[32,2,128,128]{3,2,1,0:T(8,128)} %fusion.32), kind=kCustom, calls=%fused_computation.6.clone.1 | custom fusion | flops 1048576 | bytes 12583040 | tf_op jit(solution)/shard_map/while/body/eval_jaxpr/scatter-add | solution.py:19
  275.3 3.7 gather_fusion.2
  279.0 2.7 gather_fusion.3
  281.7 4.6 %fusion.32 = f32[32,2,128,128]{3,2,1,0:T(8,128)} fusion(bf16[32,2,128,128]{3,2,1,0:T(8,128)(2,1)} %gather_fusion.2, pred[32]{0:T(512)(128)(4,1)S(1)} %get-tuple-element.318, bf16[32,128,128]{2,1,0:T(8,128)(2,1)} %gather_fusion.3, pred[32]{0:T(512)(128)(4,1)S(1)} %get-tuple-element.320), kind=kOutput, calls=%fused_computation.25.clone.1 | convolution fusion | flops 270008320 | bytes 7340096 | tf_op jit(solution)/shard_map/while/body/eval_jaxpr/bvij,bjk->bvik/dot_general | solution.py:29
  286.3 6.5 %scatter_fusion.1 = f32[16,2,128,128]{3,2,1,0:T(8,128)S(1)} fusion(f32[16,2,128,128]{3,2,1,0:T(8,128)S(1)} %get-tuple-element.358, s32[32]{0:T(128)S(1)} %fusion.31, f32[32,2,128,128]{3,2,1,0:T(8,128)} %fusion.32), kind=kCustom, calls=%fused_computation.6.clone.1 | custom fusion | flops 1048576 | bytes 12583040 | tf_op jit(solution)/shard_map/while/body/eval_jaxpr/scatter-add | solution.py:19
  292.9 3.7 gather_fusion.2
  296.6 2.7 gather_fusion.3
  299.3 4.6 %fusion.32 = f32[32,2,128,128]{3,2,1,0:T(8,128)} fusion(bf16[32,2,128,128]{3,2,1,0:T(8,128)(2,1)} %gather_fusion.2, pred[32]{0:T(512)(128)(4,1)S(1)} %get-tuple-element.318, bf16[32,128,128]{2,1,0:T(8,128)(2,1)} %gather_fusion.3, pred[32]{0:T(512)(128)(4,1)S(1)} %get-tuple-element.320), kind=kOutput, calls=%fused_computation.25.clone.1 | convolution fusion | flops 270008320 | bytes 7340096 | tf_op jit(solution)/shard_map/while/body/eval_jaxpr/bvij,bjk->bvik/dot_general | solution.py:29
  303.9 6.5 %scatter_fusion.1 = f32[16,2,128,128]{3,2,1,0:T(8,128)S(1)} fusion(f32[16,2,128,128]{3,2,1,0:T(8,128)S(1)} %get-tuple-element.358, s32[32]{0:T(128)S(1)} %fusion.31, f32[32,2,128,128]{3,2,1,0:T(8,128)} %fusion.32), kind=kCustom, calls=%fused_computation.6.clone.1 | custom fusion | flops 1048576 | bytes 12583040 | tf_op jit(solution)/shard_map/while/body/eval_jaxpr/scatter-add | solution.py:19
  310.5 3.7 gather_fusion.2
  314.2 2.7 gather_fusion.3
  316.9 4.6 %fusion.32 = f32[32,2,128,128]{3,2,1,0:T(8,128)} fusion(bf16[32,2,128,128]{3,2,1,0:T(8,128)(2,1)} %gather_fusion.2, pred[32]{0:T(512)(128)(4,1)S(1)} %get-tuple-element.318, bf16[32,128,128]{2,1,0:T(8,128)(2,1)} %gather_fusion.3, pred[32]{0:T(512)(128)(4,1)S(1)} %get-tuple-element.320), kind=kOutput, calls=%fused_computation.25.clone.1 | convolution fusion | flops 270008320 | bytes 7340096 | tf_op jit(solution)/shard_map/while/body/eval_jaxpr/bvij,bjk->bvik/dot_general | solution.py:29
  321.5 6.5 %scatter_fusion.1 = f32[16,2,128,128]{3,2,1,0:T(8,128)S(1)} fusion(f32[16,2,128,128]{3,2,1,0:T(8,128)S(1)} %get-tuple-element.358, s32[32]{0:T(128)S(1)} %fusion.31, f32[32,2,128,128]{3,2,1,0:T(8,128)} %fusion.32), kind=kCustom, calls=%fused_computation.6.clone.1 | custom fusion | flops 1048576 | bytes 12583040 | tf_op jit(solution)/shard_map/while/body/eval_jaxpr/scatter-add | solution.py:19
  328.0 1.3 copy-done.1
  329.3 60.3 %all-reduce.2.cloned.1.call-done = f32[16,2,128,128]{3,2,1,0:T(8,128)} async-done(((f32[16,2,128,128]{3,2,1,0:T(8,128)}), f32[16,2,128,128]{3,2,1,0:T(8,128)}) %all-reduce.2.cloned.1.call-update) | async-done | bytes 2097168 | tf_op jit(solution)/shard_map/psum | solution.py:53
  389.7 2.3 constant_dynamic-slice_fusion.2
  (71 shorter events, 1.4 us)
Async XLA Ops:
  6.5 1.4 copy-start
  10.6 7.6 %copy-start.7 = (s32[1,1,96,3]{2,1,3,0:T(1,128)S(1)}, s32[1,1,96,3]{2,1,3,0:T(1,128)}, u32[]{:S(2)}) copy-start(s32[1,1,96,3]{2,1,3,0:T(1,128)} %param.18) | copy-start | bytes 3460
  10.6 7.6 %copy-start.6 = (s32[1,1,256,3]{2,1,3,0:T(1,128)S(1)}, s32[1,1,256,3]{2,1,3,0:T(1,128)}, u32[]{:S(2)}) copy-start(s32[1,1,256,3]{2,1,3,0:T(1,128)} %param.19) | copy-start | bytes 9220
  10.6 7.6 %copy-start.4 = (bf16[1,1,128,128]{3,2,1,0:T(8,128)(2,1)S(1)}, bf16[1,1,128,128]{3,2,1,0:T(8,128)(2,1)}, u32[]{:S(2)}) copy-start(bf16[1,1,128,128]{3,2,1,0:T(8,128)(2,1)} %param.15) | copy-start | bytes 98308
  10.6 65.0 %copy-start.5 = (bf16[1,1,128,128]{3,2,1,0:T(8,128)(2,1)S(1)}, bf16[1,1,128,128]{3,2,1,0:T(8,128)(2,1)}, u32[]{:S(2)}) copy-start(bf16[1,1,128,128]{3,2,1,0:T(8,128)(2,1)} %param.16) | copy-start | bytes 98308
  10.6 91.1 %all-to-all-start = ((bf16[32,2,128,128]{3,2,1,0:T(8,128)(2,1)}), bf16[32,2,128,128]{3,2,1,0:T(8,128)(2,1)S(1)}, u32[]{:S(2)}, u32[]{:S(2)}) async-start(bf16[32,2,128,128]{3,2,1,0:T(8,128)(2,1)} %select_select_fusion), calls=%async_computation | async-start | bytes 4194304 | tf_op jit(solution)/shard_map/all_to_all | solution.py:46
  18.1 371.5 %all-reduce.2.cloned.1.call-start = ((), (), s32[]{:S(2)}) async-start(), calls=%async_computation.1 | async-start | bytes 4194304 | tf_op jit(solution)/shard_map/psum | solution.py:53
  104.2 1.3 copy-start.2
  120.4 10.0 %copy-start.3 = (bf16[32,2,128,128]{3,2,1,0:T(8,128)(2,1)S(1)}, bf16[32,2,128,128]{3,2,1,0:T(8,128)(2,1)}, u32[]{:S(2)}) copy-start(bf16[32,2,128,128]{3,2,1,0:T(8,128)(2,1)} %copy-done.2) | copy-start | bytes 6291460 | tf_op jit(solution)/shard_map/while
  130.4 1.3 copy-start.2
  146.6 10.0 %copy-start.3 = (bf16[32,2,128,128]{3,2,1,0:T(8,128)(2,1)S(1)}, bf16[32,2,128,128]{3,2,1,0:T(8,128)(2,1)}, u32[]{:S(2)}) copy-start(bf16[32,2,128,128]{3,2,1,0:T(8,128)(2,1)} %copy-done.2) | copy-start | bytes 6291460 | tf_op jit(solution)/shard_map/while
  156.6 1.3 copy-start.2
  172.8 10.0 %copy-start.3 = (bf16[32,2,128,128]{3,2,1,0:T(8,128)(2,1)S(1)}, bf16[32,2,128,128]{3,2,1,0:T(8,128)(2,1)}, u32[]{:S(2)}) copy-start(bf16[32,2,128,128]{3,2,1,0:T(8,128)(2,1)} %copy-done.2) | copy-start | bytes 6291460 | tf_op jit(solution)/shard_map/while
  328.0 1.3 copy-start.1
Sparse Core Ops, SparseCore 0:
  329.5 60.1 all-reduce.1
where the time goes:
time: 401 us; the launch traced here: 399 us
  local copies, waits for them, and re-layouts  95.7 us (24%)
  other arithmetic  89 us (22%)
  blocking collectives  83.4 us (21%)
  waiting for transfers between devices  60.3 us (15%)
  matrix products  48.8 us (12%)
  between operations  13.5 us (3%)
  starting transfers between devices  7.57 us (2%)
    scatter-add x11, other arithmetic, step(): return total.at[rows[:, 2]].add(contract(first, second))  81.8 us
    psum x1, waiting for transfers between devices, shards(): summed = lax.psum(partial_value, 'term')  60.3 us
    all_gather x1, blocking collectives, shards(): lax.all_gather(left_env, 'sector', axis=1, tiled=True)  57.3 us
    gather x11, local copies, waits for them, and re-layouts, step(): first = jnp.take(first_tiles, rows[:, 0], axis=0)  37.9 us
    dot_general x8, matrix products, right_product(): jnp.einsum('bvij,bjk->bvik', inter_part, env_part, preferred_element_type...  36.7 us
    gather x11, local copies, waits for them, and re-layouts, step(): second = jnp.take(second_tiles, rows[:, 1], axis=0)  29.1 us
    all_gather x1, blocking collectives, shards(): lax.all_gather(right_env, 'sector', axis=1, tiled=True)  26.1 us
    transpose x3, local copies, waits for them, and re-layouts, left_product(): jnp.einsum('bij,bvjk->bvik', env_part, wave_part, preferred_element_type=...  16.9 us
  transfers between devices with their start and end apart: 2, of which 1 were waited for; matrix products, arithmetic and copies ran while one was open for 0% of the time, Pallas kernels for 0%

commit v1 on v0

v1 whole, which is shorter than its diff:
```python
import functools

import jax
import jax.numpy as jnp
from jax import lax
from jax.experimental import pallas as pl
from jax.experimental.pallas import tpu as pltpu
from jax.sharding import PartitionSpec as P

INTER_TILES = 32
DEPTH = 8
LEFT_UNROLL = 8
RIGHT_UNROLL = 4


def round_up(value, step):
    return -(-value // step) * step


def butterfly_steps(sectors, terms):
    bits = [bit for bit in range(sectors.bit_length() - 1)]
    order = [("sector", bit) for bit in bits if bit >= 2]
    order += [("sector", bit) for bit in bits if bit == 1]
    order += [("term", bit) for bit in range(terms.bit_length() - 1)]
    order += [("sector", bit) for bit in bits if bit == 0]
    return order


def swap(value, axis, bit):
    size = lax.axis_size(axis)
    return lax.ppermute(value, axis, [(i, i ^ (1 << bit)) for i in range(size)])


def env_place(group, tile, steps):
    group = group ^ lax.axis_index("term")
    tile = tile ^ lax.axis_index("sector")
    place = jnp.zeros_like(tile)
    for turn, (axis, bit) in enumerate(steps):
        source = tile if axis == "sector" else group
        place = place + (((source >> bit) & 1) << turn)
    return place


def schedule(first, second, target, targets, depth, slots, idle):
    count = target.shape[0]
    index = jnp.arange(count, dtype=jnp.int32)
    same = target[:, None] == target[None, :]
    rank = jnp.sum(same & (index[None, :] < index[:, None]), axis=1, dtype=jnp.int32)
    names = jnp.arange(targets, dtype=jnp.int32)
    counts = jnp.sum(target[None, :] == names[:, None], axis=1, dtype=jnp.int32)
    padded = (counts + depth - 1) // depth * depth
    starts = jnp.sum(
        jnp.where(names[None, :] < target[:, None], padded[None, :], 0), axis=1, dtype=jnp.int32
    )
    place = starts + rank
    chosen = place[None, :] == jnp.arange(slots, dtype=jnp.int32)[:, None]

    def pick(values, rest):
        return rest + jnp.sum(jnp.where(chosen, values[None, :] - rest, 0), axis=1, dtype=jnp.int32)

    return jnp.concatenate([pick(first, idle), pick(second, 0), pick(target, 0)])


def products_kernel(
    left_count, slots, share, left, right, side, wave, env_left, env_right, keep, send, acc, inter, total
):
    inters = acc.shape[0]
    rows = acc.shape[1]
    acc[...] = jnp.zeros_like(acc)
    total[...] = jnp.zeros_like(total)

    @pl.loop(0, left_count // LEFT_UNROLL)
    def _(turn):
        done = []
        for step in range(LEFT_UNROLL):
            at = turn * LEFT_UNROLL + step
            product = jnp.dot(
                env_left[left[at]], wave[left[left_count + at]], preferred_element_type=jnp.float32
            )
            done.append((left[2 * left_count + at], product))
        for place, product in done:
            acc[place] += product

    @pl.loop(0, inters // 4)
    def _(turn):
        for step in range(4):
            inter[turn * 4 + step] = acc[turn * 4 + step].astype(jnp.bfloat16)

    inter[inters] = jnp.zeros((rows, inter.shape[2]), jnp.bfloat16)

    @pl.loop(0, slots // (DEPTH * RIGHT_UNROLL))
    def _(turn):
        done = []
        for step in range(RIGHT_UNROLL):
            base = (turn * RIGHT_UNROLL + step) * DEPTH
            first = [inter[right[base + i]] for i in range(DEPTH)]
            second = [env_right[right[slots + base + i]] for i in range(DEPTH)]
            product = jnp.dot(
                jnp.concatenate(first, axis=1),
                jnp.concatenate(second, axis=0),
                preferred_element_type=jnp.float32,
            )
            done.append((right[2 * slots + base], product))
        for place, product in done:
            total[place] += product

    parts = rows // share
    mine = side[0]
    keep[...] = total[:, pl.ds(pl.multiple_of(mine * share, share), share), :]
    for hop in range(1, parts):
        other = lax.rem(mine + hop, parts)
        send[hop - 1] = total[:, pl.ds(pl.multiple_of(other * share, share), share), :].astype(
            jnp.bfloat16
        )


def shards(wave_tiles, left_env, right_env, send_list, left_tasks, right_tasks):
    sectors, terms = lax.axis_size("sector"), lax.axis_size("term")
    tiles, vectors, dim, _ = wave_tiles.shape
    term = lax.axis_index("term")
    blocks = terms // vectors
    rows, share = dim // blocks, dim // terms
    vector, block = term % vectors, term // vectors

    slot_list = send_list[0]
    live = slot_list >= 0
    picked = jnp.take(
        wave_tiles.reshape(tiles * vectors, dim, dim),
        jnp.maximum(slot_list, 0) * vectors + vector,
        axis=0,
    )
    outgoing = jnp.where(live[:, None, None], picked, jnp.zeros((), jnp.bfloat16))
    received = lax.all_to_all(outgoing, "sector", split_axis=0, concat_axis=0, tiled=True)

    steps = butterfly_steps(sectors, terms)
    env = jnp.stack([left_env[0, 0], right_env[0, 0]])[:, None]
    for axis, bit in steps:
        env = jnp.concatenate([env, swap(env, axis, bit)], axis=1)
    env_left, env_right = env[0], env[1]
    env_left = lax.dynamic_slice_in_dim(env_left, block * rows, rows, 1)

    tasks = jnp.concatenate([left_tasks[0, 0], right_tasks[0, 0]], axis=0)
    tasks = lax.all_gather(tasks, "term", axis=0)
    left_rows, right_rows = tasks[:, : left_tasks.shape[2]], tasks[:, left_tasks.shape[2] :]
    groups = jnp.arange(terms, dtype=jnp.int32)[:, None]
    left_count = left_rows.shape[0] * left_rows.shape[1]
    right_count = right_rows.shape[0] * right_rows.shape[1]
    left = jnp.concatenate(
        [
            env_place(groups, left_rows[:, :, 0], steps).reshape(-1),
            left_rows[:, :, 1].reshape(-1),
            (groups * INTER_TILES + left_rows[:, :, 2]).reshape(-1),
        ]
    )
    slots = round_up(right_count + tiles * (DEPTH - 1), DEPTH * RIGHT_UNROLL)
    right = schedule(
        (groups * INTER_TILES + right_rows[:, :, 0]).reshape(-1),
        env_place(groups, right_rows[:, :, 1], steps).reshape(-1),
        right_rows[:, :, 2].reshape(-1),
        tiles,
        DEPTH,
        slots,
        terms * INTER_TILES,
    )
    vmem = pl.BlockSpec(memory_space=pltpu.VMEM)
    smem = pl.BlockSpec(memory_space=pltpu.SMEM)
    inters = terms * INTER_TILES
    keep, send = pl.pallas_call(
        functools.partial(products_kernel, left_count, slots, share),
        out_shape=(
            jax.ShapeDtypeStruct((tiles, share, dim), jnp.float32),
            jax.ShapeDtypeStruct((vectors - 1, tiles, share, dim), jnp.bfloat16),
        ),
        in_specs=[smem, smem, smem, vmem, vmem, vmem],
        out_specs=(vmem, vmem),
        scratch_shapes=[
            pltpu.VMEM((inters, rows, dim), jnp.float32),
            pltpu.VMEM((inters + 1, rows, dim), jnp.bfloat16),
            pltpu.VMEM((tiles, rows, dim), jnp.float32),
        ],
        compiler_params=pltpu.CompilerParams(vmem_limit_bytes=48 << 20),
        name="products",
    )(left, right, vector[None].astype(jnp.int32), received, env_left, env_right)

    pieces = [keep]
    for hop in range(1, vectors):
        pairs = [
            (i, i // vectors * vectors + (i % vectors + hop) % vectors) for i in range(terms)
        ]
        pieces.append(lax.ppermute(send[hop - 1], "term", pairs).astype(jnp.float32))
    result = []
    for place in range(vectors):
        hop = (vector - place) % vectors
        chosen = pieces[0]
        for other in range(1, vectors):
            chosen = jnp.where(hop == other, pieces[other], chosen)
        result.append(chosen)
    return jnp.stack(result, axis=1)


def solution(mesh):
    in_specs = (
        P("sector", None, None, None),
        P("term", "sector", None, None),
        P("term", "sector", None, None),
        P("sector", None),
        P("term", "sector", None, None),
        P("term", "sector", None, None),
    )
    out_specs = P("sector", None, "term", None)
    return jax.shard_map(shards, mesh=mesh, in_specs=in_specs, out_specs=out_specs, check_vma=False)
```

time: 401 us -> 99.6 us (0.25)
  local copies, waits for them, and re-layouts: 95.7 us -> 6.44 us
  other arithmetic: 89 us -> 7.58 us
  blocking collectives: 83.4 us -> 4.35 us
  matrix products: 48.8 us -> 0 us
  Pallas kernels: 0 us -> 15.4 us
  between operations: 13.5 us -> 0.25 us
  waiting for transfers between devices: 60.3 us -> 49.5 us
  starting transfers between devices: 7.57 us -> 15.7 us
    scatter-add x11 -> x0, other arithmetic: 81.8 us -> none  [step(): return total.at[rows[:, 2]].add(contract(first, second))]
    all_gather x2 -> x1, blocking collectives: 83.4 us -> 4.35 us  [shards(): tasks = lax.all_gather(tasks, 'term', axis=0)]
    gather x23 -> x1, local copies, waits for them, and re-layouts: 68 us -> 0.75 us  [shards(): jnp.take(wave_tiles.reshape(tiles * vectors, dim, dim), jnp.maximum(slot_...]
    psum x1 -> x0, waiting for transfers between devices: 60.3 us -> none  [shards(): summed = lax.psum(partial_value, 'term')]
    ppermute x0 -> x6, waiting for transfers between devices: none -> 49.5 us  [the longest x5 42.7 us: swap(): return lax.ppermute(value, axis, [(i, i ^ 1 << bit) for i in range(size)])]
    dot_general x11 -> x0, matrix products: 48.8 us -> none  [the longest x8 36.7 us: right_product(): jnp.einsum('bvij,bjk->bvik', inter_part, env_part, preferred_element_type...]
    transpose x3 -> x0, local copies, waits for them, and re-layouts: 16.9 us -> none  [left_product(): jnp.einsum('bij,bvjk->bvik', env_part, wave_part, preferred_element_type=...]
    pallas_call x0 -> x1, Pallas kernels: none -> 15.4 us  [shards(): pl.pallas_call(functools.partial(products_kernel, left_count, slots, shar...]
  transfers between devices with their start and end apart: 2 -> 7, of which waited for: 1 -> 5; matrix products, arithmetic and copies ran while one was open for 0% -> 9% of each run, Pallas kernels for 0% -> 0%
where the time goes in v1:
time: 99.6 us; the launch traced here: 99.2 us
  waiting for transfers between devices  49.5 us (50%)
  starting transfers between devices  15.7 us (16%)
  Pallas kernels  15.4 us (15%)
  other arithmetic  7.58 us (8%)
  local copies, waits for them, and re-layouts  6.44 us (6%)
  blocking collectives  4.35 us (4%)
    ppermute x5, waiting for transfers between devices, swap(): return lax.ppermute(value, axis, [(i, i ^ 1 << bit) for i in range(size)])  42.7 us
    pallas_call x1, Pallas kernels, shards(): pl.pallas_call(functools.partial(products_kernel, left_count, slots, shar...  15.4 us
    ppermute x5, starting transfers between devices, swap(): return lax.ppermute(value, axis, [(i, i ^ 1 << bit) for i in range(size)])  9.08 us
    ppermute x1, waiting for transfers between devices, shards(): lax.ppermute(send[hop - 1], 'term', pairs).astype(jnp.float32)  6.8 us
    all_to_all x1, starting transfers between devices, shards(): lax.all_to_all(outgoing, 'sector', split_axis=0, concat_axis=0, tiled=True)  5.06 us
    all_gather x1, blocking collectives, shards(): tasks = lax.all_gather(tasks, 'term', axis=0)  4.35 us
    unnamed x23, local copies, waits for them, and re-layouts  2.41 us
  transfers between devices with their start and end apart: 7, of which 5 were waited for; matrix products, arithmetic and copies ran while one was open for 9% of the time, Pallas kernels for 0%

profile of v1, /device:TPU:0, one launch (start us, length us, event | category | flops | bytes accessed | tf_op | source)
XLA Modules:
  0.0 99.2 jit_solution(17423826378255491883)
XLA Ops:
  0.0 0.0 copy-start
  0.0 0.9 maximum_bitcast_fusion
  0.9 3.1 %collective-permute-start = (bf16[2,1,128,128]{3,2,1,0:T(8,128)(2,1)S(1)}, bf16[2,1,128,128]{3,2,1,0:T(8,128)(2,1)S(1)}, u32[]{:S(2)}, u32[]{:S(2)}) collective-permute-start(bf16[2,1,128,128]{3,2,1,0:T(8,128)(2,1)S(1)} %maximum_bitcast_fusion), channel_id=1, source_target_pairs={{0,4},{1,5},{2,6},{3,7},{4,0},{5,1},{6,2},{7,3},{8,12},{9,13},{10,... | collective-permute-start | bytes 196616 | tf_op jit(solution)/shard_map/ppermute | solution.py:31
  4.0 0.7 fusion.3
  4.6 0.7 compare_and_fusion
  5.3 0.7 compare_bitcast_fusion
  5.9 0.0 copy-done
  6.0 0.7 gather_fusion
  6.7 0.0 copy-start.5
  6.7 0.0 copy-start.6
  6.7 1.2 %select_select_fusion = bf16[32,128,128]{2,1,0:T(8,128)(2,1)} fusion(bf16[32,128,128]{2,1,0:T(8,128)(2,1)S(1)} %gather_fusion, pred[32]{0:T(512)(128)(4,1)S(1)} %compare_and_fusion, pred[32]{0:T(512)(128)(4,1)S(1)} %compare_bitcast_fusion), kind=kLoop, calls=%fused_computation.8 | loop fusion | flops 1048576 | bytes 2097216 | tf_op jit(solution)/shard_map/jit(_where)/select_n | solution.py:132
  7.9 0.0 copy-start.3
  7.9 0.0 copy-start.4
  7.9 5.1 %all-to-all-start = ((bf16[32,128,128]{2,1,0:T(8,128)(2,1)}), bf16[32,128,128]{2,1,0:T(8,128)(2,1)S(1)}, u32[]{:S(2)}, u32[]{:S(2)}) async-start(bf16[32,128,128]{2,1,0:T(8,128)(2,1)} %select_select_fusion), calls=%async_computation | async-start | bytes 2097152 | tf_op jit(solution)/shard_map/all_to_all | solution.py:133
  13.0 0.0 copy-done.5
  13.0 0.0 copy-done.6
  13.0 0.1 add_bitcast_fusion
  13.1 4.4 %all-gather.1 = s32[2,352,3]{1,2,0:T(4,128)S(1)} all-gather(s32[1,352,3]{1,2,0:T(4,128)S(1)} %add_bitcast_fusion), channel_id=2, replica_groups=mesh['term'=2,'sector'=16] {'term'}, dimensions={0}, use_global_device_ids=true | all-gather | bytes 12672 | tf_op jit(solution)/shard_map/all_gather | solution.py:143
  17.5 0.1 add_add_fusion
  17.5 0.1 convert_reduce_fusion.1
  17.7 0.1 broadcast_bitcast_fusion
  17.7 0.1 select_reduce_fusion.3
  17.8 0.0 collective-permute-done
  17.9 2.9 %collective-permute-start.1 = (bf16[2,2,128,128]{3,2,1,0:T(8,128)(2,1)S(1)}, bf16[2,2,128,128]{3,2,1,0:T(8,128)(2,1)S(1)}, u32[]{:S(2)}, u32[]{:S(2)}) collective-permute-start(bf16[2,2,128,128]{3,2,1,0:T(8,128)(2,1)S(1)} %pad_maximum_fusion.3), channel_id=1, source_target_pairs={{0,8},{1,9},{2,10},{3,11},{4,12},{5,13},{6,14},{7,15},{8,0},{9,1},... | collective-permute-start | bytes 393224 | tf_op jit(solution)/shard_map/ppermute | solution.py:31
  20.7 0.2 convert_reduce_fusion
  21.0 24.1 %collective-permute-done.1 = bf16[2,2,128,128]{3,2,1,0:T(8,128)(2,1)S(1)} collective-permute-done((bf16[2,2,128,128]{3,2,1,0:T(8,128)(2,1)S(1)}, bf16[2,2,128,128]{3,2,1,0:T(8,128)(2,1)S(1)}, u32[]{:S(2)}, u32[]{:S(2)}) %collective-permute-start.1) | collective-permute-done | bytes 131104 | tf_op jit(solution)/shard_map/ppermute | solution.py:31
  45.2 1.5 %collective-permute-start.2 = (bf16[2,4,128,128]{3,2,1,0:T(8,128)(2,1)S(1)}, bf16[2,4,128,128]{3,2,1,0:T(8,128)(2,1)S(1)}, u32[]{:S(2)}, u32[]{:S(2)}) collective-permute-start(bf16[2,4,128,128]{3,2,1,0:T(8,128)(2,1)S(1)} %pad_maximum_fusion.2), channel_id=1, source_target_pairs={{0,2},{1,3},{2,0},{3,1},{4,6},{5,7},{6,4},{7,5},{8,10},{9,11},{10,... | collective-permute-start | bytes 786440 | tf_op jit(solution)/shard_map/ppermute | solution.py:31
  46.7 0.1 broadcast_bitcast_fusion.1
  46.8 6.3 %collective-permute-done.2 = bf16[2,4,128,128]{3,2,1,0:T(8,128)(2,1)S(1)} collective-permute-done((bf16[2,4,128,128]{3,2,1,0:T(8,128)(2,1)S(1)}, bf16[2,4,128,128]{3,2,1,0:T(8,128)(2,1)S(1)}, u32[]{:S(2)}, u32[]{:S(2)}) %collective-permute-start.2) | collective-permute-done | bytes 262176 | tf_op jit(solution)/shard_map/ppermute | solution.py:31
  53.1 0.8 pad_maximum_fusion.1
  53.9 1.5 %collective-permute-start.3 = (bf16[2,8,128,128]{3,2,1,0:T(8,128)(2,1)}, bf16[2,8,128,128]{3,2,1,0:T(8,128)(2,1)S(1)}, u32[]{:S(2)}, u32[]{:S(2)}) collective-permute-start(bf16[2,8,128,128]{3,2,1,0:T(8,128)(2,1)} %pad_maximum_fusion.1), channel_id=1, source_target_pairs={{0,16},{16,0},{1,17},{17,1},{2,18},{18,2},{3,19},{19,3},{4,20},{20... | collective-permute-start | bytes 1572872 | tf_op jit(solution)/shard_map/ppermute | solution.py:31
  55.5 0.1 reshape.197
  55.6 0.1 shift_left.92
  55.6 0.1 add.176
  55.7 0.1 add.177
  55.8 0.1 squeeze.26
  55.9 0.1 add.180
  55.9 0.1 add.181
  56.0 0.1 reshape_squeeze.3
  56.1 0.0 copy-done.3
  56.1 0.0 copy-done.4
  56.2 0.1 constant_dynamic-update-slice_fusion.2
  56.3 0.1 constant_dynamic-update-slice_fusion.1
  56.4 10.3 %collective-permute-done.3 = bf16[2,8,128,128]{3,2,1,0:T(8,128)(2,1)S(1)} collective-permute-done((bf16[2,8,128,128]{3,2,1,0:T(8,128)(2,1)}, bf16[2,8,128,128]{3,2,1,0:T(8,128)(2,1)S(1)}, u32[]{:S(2)}, u32[]{:S(2)}) %collective-permute-start.3) | collective-permute-done | bytes 524320 | tf_op jit(solution)/shard_map/ppermute | solution.py:31
  66.7 0.3 constant_dynamic-update-slice_fusion
  67.0 0.1 collective-permute-start.4
  67.1 0.1 pad_add_fusion.1.left
  67.2 0.6 select_reduce_fusion.2
  67.8 1.9 %collective-permute-done.4 = bf16[2,16,128,128]{3,2,1,0:T(8,128)(2,1)S(1)} collective-permute-done((bf16[2,16,128,128]{3,2,1,0:T(8,128)(2,1)S(1)}, bf16[2,16,128,128]{3,2,1,0:T(8,128)(2,1)S(1)}, u32[]{:S(2)}, u32[]{:S(2)}) %collective-permute-start.4) | collective-permute-done | bytes 1048608 | tf_op jit(solution)/shard_map/ppermute | solution.py:31
  69.7 0.1 constant_dynamic-update-slice_fusion.5
  69.9 1.1 %slice_bitcast_fusion = (bf16[32,128,128]{2,1,0:T(8,128)(2,1)S(1)}, bf16[32,128,128]{2,1,0:T(8,128)(2,1)}) fusion(bf16[2,32,128,128]{3,2,1,0:T(8,128)(2,1)S(1)} %constant_dynamic-update-slice_fusion.5), kind=kLoop, calls=%fused_computation.5 | loop fusion | bytes 4194304 | tf_op jit(solution)/shard_map/squeeze | solution.py:139
  71.0 0.0 all-to-all-done.wave
  71.0 0.0 copy-start.1
  71.0 1.2 %copy-done.1 = bf16[32,128,128]{2,1,0:T(8,128)(2,1)S(1)} copy-done((bf16[32,128,128]{2,1,0:T(8,128)(2,1)S(1)}, bf16[32,128,128]{2,1,0:T(8,128)(2,1)}, u32[]{:S(2)}) %copy-start.1) | copy-done | bytes 1048600
  72.2 15.4 %products.1 = (f32[16,64,128]{2,1,0:T(8,128)S(1)}, bf16[1,16,64,128]{3,2,1,0:T(8,128)(2,1)S(1)}) custom-call(s32[576]{0:T(1024)S(1)} %pad_add_fusion.1.left, s32[1920]{0:T(1024)S(1)} %pad_add_fusion.right, s32[1]{0:T(128)} %bitcast.5.side, bf16[32,128,128]{2,1,0:T(8,128)(2,1)S(1)} %all-to-all-done.wave, bf16[32,128,128]{2,1,0:T(8,128)(2,1)S(1)} %copy-done.1, ...), custom_call_target="tpu_custom_call" | custom-call | tf_op jit(solution)/shard_map/products/pallas_call | solution.py:168
  87.6 0.0 copy-start.2
  87.7 0.8 copy-done.2
  88.4 1.6 %collective-permute-start.5 = (bf16[16,64,128]{2,1,0:T(8,128)(2,1)S(1)}, bf16[16,64,128]{2,1,0:T(8,128)(2,1)S(1)}, u32[]{:S(2)}, u32[]{:S(2)}) collective-permute-start(bf16[16,64,128]{2,1,0:T(8,128)(2,1)S(1)} %bitcast.46), channel_id=1, source_target_pairs={{0,16},{16,0},{1,17},{17,1},{2,18},{18,2},{3,19},{19,3},{4,20},{20... | collective-permute-start | bytes 786440 | tf_op jit(solution)/shard_map/ppermute | solution.py:190
  90.0 6.8 %collective-permute-done.5 = bf16[16,64,128]{2,1,0:T(8,128)(2,1)S(1)} collective-permute-done((bf16[16,64,128]{2,1,0:T(8,128)(2,1)S(1)}, bf16[16,64,128]{2,1,0:T(8,128)(2,1)S(1)}, u32[]{:S(2)}, u32[]{:S(2)}) %collective-permute-start.5) | collective-permute-done | bytes 262176 | tf_op jit(solution)/shard_map/ppermute | solution.py:190
  96.8 1.2 %fusion.1 = (f32[16,1,64,128]{3,2,0,1:T(8,128)S(1)}, f32[16,1,64,128]{3,2,0,1:T(8,128)S(1)}) fusion(f32[16,64,128]{2,1,0:T(8,128)} %copy-done.2, bf16[16,64,128]{2,1,0:T(8,128)(2,1)S(1)} %collective-permute-done.5, pred[]{:T(512)S(6)} %eq.49, pred[]{:T(512)S(6)} %eq.59), kind=kLoop, calls=%fused_computation.14 | loop fusion | flops 393216 | bytes 1835010 | tf_op jit(solution)/shard_map/stack | solution.py:198
  98.0 0.1 pad_maximum_fusion
  98.1 1.1 %copy.9 = f32[16,2,64,128]{3,2,1,0:T(8,128)} copy(f32[16,2,64,128]{3,2,0,1:T(8,128)S(1)} %pad_maximum_fusion) | data formatting | bytes 2097152 | tf_op jit(solution)/shard_map/stack | solution.py:198
  (19 shorter events, 0.2 us)
Async XLA Ops:
  0.0 5.9 %copy-start = (bf16[16,2,128,128]{3,2,1,0:T(8,128)(2,1)S(1)}, bf16[16,2,128,128]{3,2,1,0:T(8,128)(2,1)}, u32[]{:S(2)}) copy-start(bf16[16,2,128,128]{3,2,1,0:T(8,128)(2,1)} %param.6) | copy-start | bytes 3145732
  0.9 17.0 %collective-permute-start = (bf16[2,1,128,128]{3,2,1,0:T(8,128)(2,1)S(1)}, bf16[2,1,128,128]{3,2,1,0:T(8,128)(2,1)S(1)}, u32[]{:S(2)}, u32[]{:S(2)}) collective-permute-start(bf16[2,1,128,128]{3,2,1,0:T(8,128)(2,1)S(1)} %maximum_bitcast_fusion), channel_id=1, source_target_pairs={{0,4},{1,5},{2,6},{3,7},{4,0},{5,1},{6,2},{7,3},{8,12},{9,13},{10,... | collective-permute-start | bytes 196616 | tf_op jit(solution)/shard_map/ppermute | solution.py:31
  6.7 6.3 %copy-start.5 = (s32[1,1,256,3]{2,1,3,0:T(1,128)S(1)}, s32[1,1,256,3]{2,1,3,0:T(1,128)}, u32[]{:S(2)}) copy-start(s32[1,1,256,3]{2,1,3,0:T(1,128)} %param.11) | copy-start | bytes 9220
  6.7 6.3 %copy-start.6 = (s32[1,1,96,3]{2,1,3,0:T(1,128)S(1)}, s32[1,1,96,3]{2,1,3,0:T(1,128)}, u32[]{:S(2)}) copy-start(s32[1,1,96,3]{2,1,3,0:T(1,128)} %param.10) | copy-start | bytes 3460
  7.9 48.2 %copy-start.3 = (bf16[1,1,128,128]{3,2,1,0:T(8,128)(2,1)S(1)}, bf16[1,1,128,128]{3,2,1,0:T(8,128)(2,1)}, u32[]{:S(2)}) copy-start(bf16[1,1,128,128]{3,2,1,0:T(8,128)(2,1)} %param.8) | copy-start | bytes 98308
  7.9 48.2 %copy-start.4 = (bf16[1,1,128,128]{3,2,1,0:T(8,128)(2,1)S(1)}, bf16[1,1,128,128]{3,2,1,0:T(8,128)(2,1)}, u32[]{:S(2)}) copy-start(bf16[1,1,128,128]{3,2,1,0:T(8,128)(2,1)} %param.7) | copy-start | bytes 98308
  7.9 63.1 %all-to-all-start = ((bf16[32,128,128]{2,1,0:T(8,128)(2,1)}), bf16[32,128,128]{2,1,0:T(8,128)(2,1)S(1)}, u32[]{:S(2)}, u32[]{:S(2)}) async-start(bf16[32,128,128]{2,1,0:T(8,128)(2,1)} %select_select_fusion), calls=%async_computation | async-start | bytes 2097152 | tf_op jit(solution)/shard_map/all_to_all | solution.py:133
  17.9 27.3 %collective-permute-start.1 = (bf16[2,2,128,128]{3,2,1,0:T(8,128)(2,1)S(1)}, bf16[2,2,128,128]{3,2,1,0:T(8,128)(2,1)S(1)}, u32[]{:S(2)}, u32[]{:S(2)}) collective-permute-start(bf16[2,2,128,128]{3,2,1,0:T(8,128)(2,1)S(1)} %pad_maximum_fusion.3), channel_id=1, source_target_pairs={{0,8},{1,9},{2,10},{3,11},{4,12},{5,13},{6,14},{7,15},{8,0},{9,1},... | collective-permute-start | bytes 393224 | tf_op jit(solution)/shard_map/ppermute | solution.py:31
  45.2 7.9 %collective-permute-start.2 = (bf16[2,4,128,128]{3,2,1,0:T(8,128)(2,1)S(1)}, bf16[2,4,128,128]{3,2,1,0:T(8,128)(2,1)S(1)}, u32[]{:S(2)}, u32[]{:S(2)}) collective-permute-start(bf16[2,4,128,128]{3,2,1,0:T(8,128)(2,1)S(1)} %pad_maximum_fusion.2), channel_id=1, source_target_pairs={{0,2},{1,3},{2,0},{3,1},{4,6},{5,7},{6,4},{7,5},{8,10},{9,11},{10,... | collective-permute-start | bytes 786440 | tf_op jit(solution)/shard_map/ppermute | solution.py:31
  53.9 12.8 %collective-permute-start.3 = (bf16[2,8,128,128]{3,2,1,0:T(8,128)(2,1)}, bf16[2,8,128,128]{3,2,1,0:T(8,128)(2,1)S(1)}, u32[]{:S(2)}, u32[]{:S(2)}) collective-permute-start(bf16[2,8,128,128]{3,2,1,0:T(8,128)(2,1)} %pad_maximum_fusion.1), channel_id=1, source_target_pairs={{0,16},{16,0},{1,17},{17,1},{2,18},{18,2},{3,19},{19,3},{4,20},{20... | collective-permute-start | bytes 1572872 | tf_op jit(solution)/shard_map/ppermute | solution.py:31
  67.0 2.7 %collective-permute-start.4 = (bf16[2,16,128,128]{3,2,1,0:T(8,128)(2,1)S(1)}, bf16[2,16,128,128]{3,2,1,0:T(8,128)(2,1)S(1)}, u32[]{:S(2)}, u32[]{:S(2)}) collective-permute-start(bf16[2,16,128,128]{3,2,1,0:T(8,128)(2,1)S(1)} %get-tuple-element.20), channel_id=1, source_target_pairs={{0,1},{1,0},{2,3},{3,2},{4,5},{5,4},{6,7},{7,6},{8,9},{9,8},{10,11... | collective-permute-start | bytes 3145736 | tf_op jit(solution)/shard_map/ppermute | solution.py:31
  71.0 1.2 %copy-start.1 = (bf16[32,128,128]{2,1,0:T(8,128)(2,1)S(1)}, bf16[32,128,128]{2,1,0:T(8,128)(2,1)}, u32[]{:S(2)}) copy-start(bf16[32,128,128]{2,1,0:T(8,128)(2,1)} %get-tuple-element.17.env_left) | copy-start | bytes 3145732
  87.6 0.8 copy-start.2
  88.4 8.4 %collective-permute-start.5 = (bf16[16,64,128]{2,1,0:T(8,128)(2,1)S(1)}, bf16[16,64,128]{2,1,0:T(8,128)(2,1)S(1)}, u32[]{:S(2)}, u32[]{:S(2)}) collective-permute-start(bf16[16,64,128]{2,1,0:T(8,128)(2,1)S(1)} %bitcast.46), channel_id=1, source_target_pairs={{0,16},{16,0},{1,17},{17,1},{2,18},{18,2},{3,19},{19,3},{4,20},{20... | collective-permute-start | bytes 786440 | tf_op jit(solution)/shard_map/ppermute | solution.py:190

commit v2 on v1

v2 whole, which is shorter than its diff:
```python
import functools

import jax
import jax.numpy as jnp
from jax import lax
from jax.experimental import pallas as pl
from jax.experimental.pallas import tpu as pltpu
from jax.sharding import PartitionSpec as P

INTER_TILES = 32
DEPTH = 8
PACK_UNROLL = 8
LEFT_UNROLL = 16
RIGHT_UNROLL = 8


def round_up(value, step):
    return -(-value // step) * step


def swap(value, axis, mask):
    size = lax.axis_size(axis)
    return lax.ppermute(value, axis, [(i, i ^ mask) for i in range(size)])


def env_place(group, tile, side):
    sectors, terms = lax.axis_size("sector"), lax.axis_size("term")
    group = group ^ lax.axis_index("term")
    tile = tile ^ lax.axis_index("sector")
    far = sectors // 4
    place = (tile >> 2) + far * (((tile >> 1) & 1) + 2 * group)
    return place + far * 2 * terms * (side + 2 * (tile & 1))


def gather_env(env):
    sectors, terms = lax.axis_size("sector"), lax.axis_size("term")
    far = [env] + [swap(env, "sector", mask << 2) for mask in range(1, sectors // 4)]
    column = jnp.stack(far, axis=1)
    across, over = swap(column, "sector", 2), swap(column, "term", 1)
    corner = jnp.stack([swap(over[0], "sector", 2), swap(across[1], "term", 1)])
    plane = jnp.concatenate([column, across, over, corner], axis=1)
    bit = 2
    while bit < terms:
        plane = jnp.concatenate([plane, swap(plane, "term", bit)], axis=1)
        bit *= 2
    both = jnp.stack([plane, swap(plane, "sector", 1)])
    return both.reshape((-1,) + env.shape[1:])


def pack_kernel(vectors, picks, wave, left, right, out, env, held, sems):
    vector = lax.rem(lax.axis_index("term"), vectors)
    copies = [
        pltpu.make_async_copy(wave.at[:, vector], held, sems.at[0]),
        pltpu.make_async_copy(left.at[0, 0], env.at[0], sems.at[1]),
        pltpu.make_async_copy(right.at[0, 0], env.at[1], sems.at[2]),
    ]
    for copy in copies:
        copy.start()
    for copy in copies:
        copy.wait()

    @pl.loop(0, out.shape[0] // PACK_UNROLL)
    def _(turn):
        for step in range(PACK_UNROLL):
            slot = turn * PACK_UNROLL + step
            tile = picks[0, slot]
            picked = held[jnp.maximum(tile, 0)]
            out[slot] = jnp.where(tile >= 0, picked, jnp.zeros_like(picked))


def schedule(first, second, target, targets, depth, slots, idle):
    count = target.shape[0]
    index = jnp.arange(count, dtype=jnp.int32)
    same = target[:, None] == target[None, :]
    rank = jnp.sum(same & (index[None, :] < index[:, None]), axis=1, dtype=jnp.int32)
    names = jnp.arange(targets, dtype=jnp.int32)
    counts = jnp.sum(target[None, :] == names[:, None], axis=1, dtype=jnp.int32)
    padded = (counts + depth - 1) // depth * depth
    starts = jnp.sum(
        jnp.where(names[None, :] < target[:, None], padded[None, :], 0), axis=1, dtype=jnp.int32
    )
    place = starts + rank
    chosen = place[None, :] == jnp.arange(slots, dtype=jnp.int32)[:, None]

    def pick(values, rest):
        return rest + jnp.sum(jnp.where(chosen, values[None, :] - rest, 0), axis=1, dtype=jnp.int32)

    return jnp.concatenate([pick(first, idle), pick(second, 0), pick(target, 0)])


def products_kernel(left_count, slots, share, left, right, side, wave, env, keep, send, acc, inter, total):
    inters, rows, dim = acc.shape
    mine, block = side[0], side[1]
    row = 0 if rows == dim else pl.multiple_of(block * rows, rows)
    acc[...] = jnp.zeros_like(acc)
    total[...] = jnp.zeros_like(total)

    @pl.loop(0, left_count // LEFT_UNROLL)
    def _(turn):
        done = []
        for step in range(LEFT_UNROLL):
            at = turn * LEFT_UNROLL + step
            product = jnp.dot(
                env[left[at], pl.ds(row, rows), :],
                wave[left[left_count + at]],
                preferred_element_type=jnp.float32,
            )
            done.append((left[2 * left_count + at], product))
        for place, product in done:
            acc[place] += product

    @pl.loop(0, inters // 8)
    def _(turn):
        for step in range(8):
            inter[turn * 8 + step] = acc[turn * 8 + step].astype(jnp.bfloat16)

    inter[inters] = jnp.zeros((rows, dim), jnp.bfloat16)

    @pl.loop(0, slots // (DEPTH * RIGHT_UNROLL))
    def _(turn):
        done = []
        for step in range(RIGHT_UNROLL):
            base = (turn * RIGHT_UNROLL + step) * DEPTH
            first = [inter[right[base + i]] for i in range(DEPTH)]
            second = [env[right[slots + base + i]] for i in range(DEPTH)]
            product = jnp.dot(
                jnp.concatenate(first, axis=1),
                jnp.concatenate(second, axis=0),
                preferred_element_type=jnp.float32,
            )
            done.append((right[2 * slots + base], product))
        for place, product in done:
            total[place] += product

    parts = rows // share
    keep[...] = total[:, pl.ds(pl.multiple_of(mine * share, share), share), :]
    for hop in range(1, parts):
        other = lax.rem(mine + hop, parts)
        send[hop - 1] = total[:, pl.ds(pl.multiple_of(other * share, share), share), :].astype(
            jnp.bfloat16
        )


def shards(wave_tiles, left_env, right_env, send_list, left_tasks, right_tasks):
    sectors, terms = lax.axis_size("sector"), lax.axis_size("term")
    tiles, vectors, dim, _ = wave_tiles.shape
    term = lax.axis_index("term")
    blocks = terms // vectors
    rows, share = dim // blocks, dim // terms
    vector, block = term % vectors, term // vectors

    vmem = pl.BlockSpec(memory_space=pltpu.VMEM)
    smem = pl.BlockSpec(memory_space=pltpu.SMEM)
    hbm = pl.BlockSpec(memory_space=pl.ANY)
    send_slots = send_list.shape[1]
    outgoing, env = pl.pallas_call(
        functools.partial(pack_kernel, vectors),
        out_shape=(
            jax.ShapeDtypeStruct((send_slots, dim, dim), jnp.bfloat16),
            jax.ShapeDtypeStruct((2, dim, dim), jnp.bfloat16),
        ),
        in_specs=[smem, hbm, hbm, hbm],
        out_specs=(vmem, vmem),
        scratch_shapes=[
            pltpu.VMEM((tiles, dim, dim), jnp.bfloat16),
            pltpu.SemaphoreType.DMA((3,)),
        ],
        name="pack",
    )(send_list, wave_tiles, left_env, right_env)
    env = gather_env(env)
    received = lax.all_to_all(outgoing, "sector", split_axis=0, concat_axis=0, tiled=True)

    tasks = jnp.concatenate([left_tasks[0, 0], right_tasks[0, 0]], axis=0)[None]
    bit = 1
    while bit < terms:
        tasks = jnp.concatenate([tasks, swap(tasks, "term", bit)], axis=0)
        bit *= 2
    left_rows, right_rows = tasks[:, : left_tasks.shape[2]], tasks[:, left_tasks.shape[2] :]
    groups = jnp.arange(terms, dtype=jnp.int32)[:, None] ^ term
    left_count = left_rows.shape[0] * left_rows.shape[1]
    right_count = right_rows.shape[0] * right_rows.shape[1]
    left = jnp.concatenate(
        [
            env_place(groups, left_rows[:, :, 0], 0).reshape(-1),
            left_rows[:, :, 1].reshape(-1),
            (groups * INTER_TILES + left_rows[:, :, 2]).reshape(-1),
        ]
    )
    slots = round_up(right_count + tiles * (DEPTH - 1), DEPTH * RIGHT_UNROLL)
    right = schedule(
        (groups * INTER_TILES + right_rows[:, :, 0]).reshape(-1),
        env_place(groups, right_rows[:, :, 1], 1).reshape(-1),
        right_rows[:, :, 2].reshape(-1),
        tiles,
        DEPTH,
        slots,
        terms * INTER_TILES,
    )
    inters = terms * INTER_TILES
    keep, send = pl.pallas_call(
        functools.partial(products_kernel, left_count, slots, share),
        out_shape=(
            jax.ShapeDtypeStruct((tiles, share, dim), jnp.float32),
            jax.ShapeDtypeStruct((vectors - 1, tiles, share, dim), jnp.bfloat16),
        ),
        in_specs=[smem, smem, smem, vmem, vmem],
        out_specs=(vmem, vmem),
        scratch_shapes=[
            pltpu.VMEM((inters, rows, dim), jnp.float32),
            pltpu.VMEM((inters + 1, rows, dim), jnp.bfloat16),
            pltpu.VMEM((tiles, rows, dim), jnp.float32),
        ],
        compiler_params=pltpu.CompilerParams(vmem_limit_bytes=48 << 20),
        name="products",
    )(left, right, jnp.stack([vector, block]).astype(jnp.int32), received, env)

    pieces = [keep]
    for hop in range(1, vectors):
        pairs = [
            (i, i // vectors * vectors + (i % vectors + hop) % vectors) for i in range(terms)
        ]
        pieces.append(lax.ppermute(send[hop - 1], "term", pairs).astype(jnp.float32))
    hops = (vector - jnp.arange(vectors)[None, :, None, None]) % vectors
    result = pieces[0][:, None]
    for hop in range(1, vectors):
        result = jnp.where(hops == hop, pieces[hop][:, None], result)
    return result


def solution(mesh):
    in_specs = (
        P("sector", None, None, None),
        P("term", "sector", None, None),
        P("term", "sector", None, None),
        P("sector", None),
        P("term", "sector", None, None),
        P("term", "sector", None, None),
    )
    out_specs = P("sector", None, "term", None)
    return jax.shard_map(shards, mesh=mesh, in_specs=in_specs, out_specs=out_specs, check_vma=False)
```

time: 99.6 us -> 68 us (0.68)
  waiting for transfers between devices: 49.5 us -> 27.7 us
  other arithmetic: 7.58 us -> 2.98 us
  blocking collectives: 4.35 us -> 0 us
  local copies, waits for them, and re-layouts: 6.44 us -> 2.52 us
  starting transfers between devices: 15.7 us -> 19.2 us
    ppermute x5 -> x9, waiting for transfers between devices: 42.7 us -> 19.9 us  [swap(): return lax.ppermute(value, axis, [(i, i ^ mask) for i in range(size)])]
    ppermute x5 -> x9, starting transfers between devices: 9.08 us -> 13.4 us  [swap(): return lax.ppermute(value, axis, [(i, i ^ mask) for i in range(size)])]
    all_gather x1 -> x0, blocking collectives: 4.35 us -> none  [shards(): tasks = lax.all_gather(tasks, 'term', axis=0)]
    pallas_call x1, Pallas kernels: 15.4 us -> 12 us  [shards(): pl.pallas_call(functools.partial(products_kernel, left_count, slots, shar...]
    pallas_call x0 -> x1, Pallas kernels: none -> 3.02 us  [shards(): pl.pallas_call(functools.partial(pack_kernel, vectors), out_shape=(jax.Sh...]
    squeeze x1 -> x2, local copies, waits for them, and re-layouts: 1.13 us -> 0.02 us  [gather_env(): corner = jnp.stack([swap(over[0], 'sector', 2), swap(across[1], 'term', 1)])]
    ppermute x1, waiting for transfers between devices: 6.8 us -> 7.85 us  [shards(): lax.ppermute(send[hop - 1], 'term', pairs).astype(jnp.float32)]
    ppermute x1, starting transfers between devices: 1.56 us -> 0.55 us  [shards(): lax.ppermute(send[hop - 1], 'term', pairs).astype(jnp.float32)]
  transfers between devices with their start and end apart: 7 -> 11, of which waited for: 5 -> 5; matrix products, arithmetic and copies ran while one was open for 9% -> 6% of each run, Pallas kernels for 0% -> 0%
where the time goes in v2:
time: 68 us; the launch traced here: 67.8 us
  waiting for transfers between devices  27.7 us (41%)
  starting transfers between devices  19.2 us (28%)
  Pallas kernels  15 us (22%)
  other arithmetic  2.98 us (4%)
  local copies, waits for them, and re-layouts  2.52 us (4%)
    ppermute x9, waiting for transfers between devices, swap(): return lax.ppermute(value, axis, [(i, i ^ mask) for i in range(size)])  19.9 us
    ppermute x9, starting transfers between devices, swap(): return lax.ppermute(value, axis, [(i, i ^ mask) for i in range(size)])  13.4 us
    pallas_call x1, Pallas kernels, shards(): pl.pallas_call(functools.partial(products_kernel, left_count, slots, shar...  12 us
    ppermute x1, waiting for transfers between devices, shards(): lax.ppermute(send[hop - 1], 'term', pairs).astype(jnp.float32)  7.85 us
    all_to_all x1, starting transfers between devices, shards(): lax.all_to_all(outgoing, 'sector', split_axis=0, concat_axis=0, tiled=True)  5.26 us
    pallas_call x1, Pallas kernels, shards(): pl.pallas_call(functools.partial(pack_kernel, vectors), out_shape=(jax.Sh...  3.02 us
    unnamed x14, local copies, waits for them, and re-layouts  1.63 us
  transfers between devices with their start and end apart: 11, of which 5 were waited for; matrix products, arithmetic and copies ran while one was open for 6% of the time, Pallas kernels for 0%

profile of v2, /device:TPU:0, one launch (start us, length us, event | category | flops | bytes accessed | tf_op | source)
XLA Modules:
  0.0 67.8 jit_solution(16616215350535840759)
XLA Ops:
  0.0 3.0 %pack.1 = (bf16[32,128,128]{2,1,0:T(8,128)(2,1)}, bf16[2,128,128]{2,1,0:T(8,128)(2,1)}) custom-call(s32[1,32]{1,0:T(1,128)} %picks.1, bf16[16,2,128,128]{3,2,1,0:T(8,128)(2,1)} %wave.1, bf16[1,1,128,128]{3,2,1,0:T(8,128)(2,1)} %left.1, bf16[1,1,128,128]{3,2,1,0:T(8,128)(2,1)} %right.1), custom_call_target="tpu_custom_call" | custom-call | tf_op jit(solution)/shard_map/pack/pallas_call | solution.py:156
  3.0 0.0 copy-start
  3.0 4.1 %collective-permute-start.2 = (bf16[2,128,128]{2,1,0:T(8,128)(2,1)}, bf16[2,128,128]{2,1,0:T(8,128)(2,1)S(1)}, u32[]{:S(2)}, u32[]{:S(2)}) collective-permute-start(bf16[2,128,128]{2,1,0:T(8,128)(2,1)} %get-tuple-element.10), channel_id=1, source_target_pairs={{0,8},{1,9},{2,10},{3,11},{4,12},{5,13},{6,14},{7,15},{8,0},{9,1},... | collective-permute-start | bytes 196616 | tf_op jit(solution)/shard_map/ppermute | solution.py:23
  7.1 1.3 %collective-permute-start.3 = (bf16[2,128,128]{2,1,0:T(8,128)(2,1)}, bf16[2,128,128]{2,1,0:T(8,128)(2,1)S(1)}, u32[]{:S(2)}, u32[]{:S(2)}) collective-permute-start(bf16[2,128,128]{2,1,0:T(8,128)(2,1)} %get-tuple-element.10), channel_id=1, source_target_pairs={{0,12},{1,13},{2,14},{3,15},{4,8},{5,9},{6,10},{7,11},{8,4},{9,5},... | collective-permute-start | bytes 196616 | tf_op jit(solution)/shard_map/ppermute | solution.py:23
  8.5 0.2 collective-permute-start.1
  8.7 0.7 %copy.23 = s32[1,1,256,3]{2,3,1,0:T(4,128)S(1)} copy(s32[1,1,256,3]{2,1,3,0:T(1,128)} %param.11) | data formatting | bytes 6144
  9.4 0.7 %copy.24 = s32[1,1,96,3]{2,3,1,0:T(4,128)S(1)} copy(s32[1,1,96,3]{2,1,3,0:T(1,128)} %param.10) | data formatting | bytes 2304
  10.1 0.1 add_bitcast_fusion
  10.2 1.5 %collective-permute-start = (s32[1,352,3]{1,2,0:T(4,128)S(1)}, s32[1,352,3]{1,2,0:T(4,128)S(1)}, u32[]{:S(2)}, u32[]{:S(2)}) collective-permute-start(s32[1,352,3]{1,2,0:T(4,128)S(1)} %add_bitcast_fusion), channel_id=1, source_target_pairs={{0,16},{16,0},{1,17},{17,1},{2,18},{18,2},{3,19},{19,3},{4,20},{20... | collective-permute-start | bytes 12680 | tf_op jit(solution)/shard_map/ppermute | solution.py:23
  11.7 5.3 %all-to-all-start = ((bf16[32,128,128]{2,1,0:T(8,128)(2,1)}), bf16[32,128,128]{2,1,0:T(8,128)(2,1)S(1)}, u32[]{:S(2)}, u32[]{:S(2)}) async-start(bf16[32,128,128]{2,1,0:T(8,128)(2,1)} %get-tuple-element.9), calls=%async_computation | async-start | bytes 2097152 | tf_op jit(solution)/shard_map/all_to_all | solution.py:171
  16.9 0.0 copy-done
  17.0 0.1 broadcast_bitcast_fusion
  17.0 0.1 broadcast_bitcast_fusion.1
  17.1 0.1 pad_add_fusion.5.side
  17.2 0.1 add.134
  17.3 0.1 add.135
  17.4 0.1 add.139
  17.4 0.1 add.140
  17.5 0.0 collective-permute-done
  17.5 0.1 shift-right-arithmetic_and_fusion
  17.6 0.1 convert_reduce_fusion.1
  17.7 0.3 convert_reduce_fusion
  18.0 0.1 and.74
  18.1 0.1 mul.76
  18.2 0.1 shift_right_arithmetic.31
  18.3 0.1 squeeze.25
  18.4 0.1 reshape_squeeze.3
  18.5 0.1 select_reduce_fusion.3
  18.6 0.0 collective-permute-done.2
  18.6 0.0 collective-permute-done.3
  18.6 0.0 collective-permute-done.1
  18.7 0.6 collective-permute-start.5
  19.3 1.9 %collective-permute-start.4 = (bf16[2,4,128,128]{3,2,1,0:T(8,128)(2,1)S(1)}, bf16[2,4,128,128]{3,2,1,0:T(8,128)(2,1)S(1)}, u32[]{:S(2)}, u32[]{:S(2)}) collective-permute-start(bf16[2,4,128,128]{3,2,1,0:T(8,128)(2,1)S(1)} %copy.11), channel_id=1, source_target_pairs={{0,2},{1,3},{2,0},{3,1},{4,6},{5,7},{6,4},{7,5},{8,10},{9,11},{10,... | collective-permute-start | bytes 786440 | tf_op jit(solution)/shard_map/ppermute | solution.py:23
  21.2 12.8 %collective-permute-done.4 = bf16[2,4,128,128]{3,2,1,0:T(8,128)(2,1)S(1)} collective-permute-done((bf16[2,4,128,128]{3,2,1,0:T(8,128)(2,1)S(1)}, bf16[2,4,128,128]{3,2,1,0:T(8,128)(2,1)S(1)}, u32[]{:S(2)}, u32[]{:S(2)}) %collective-permute-start.4) | collective-permute-done | bytes 262176 | tf_op jit(solution)/shard_map/ppermute | solution.py:23
  34.1 1.1 %collective-permute-start.7 = (bf16[4,128,128]{2,1,0:T(8,128)(2,1)S(1)}, bf16[4,128,128]{2,1,0:T(8,128)(2,1)S(1)}, u32[]{:S(2)}, u32[]{:S(2)}) collective-permute-start(bf16[4,128,128]{2,1,0:T(8,128)(2,1)S(1)} %slice_bitcast_fusion), channel_id=1, source_target_pairs={{0,16},{16,0},{1,17},{17,1},{2,18},{18,2},{3,19},{19,3},{4,20},{20... | collective-permute-start | bytes 393224 | tf_op jit(solution)/shard_map/ppermute | solution.py:23
  35.2 0.0 collective-permute-done.5
  35.2 2.5 %collective-permute-start.6 = (bf16[4,128,128]{2,1,0:T(8,128)(2,1)S(1)}, bf16[4,128,128]{2,1,0:T(8,128)(2,1)S(1)}, u32[]{:S(2)}, u32[]{:S(2)}) collective-permute-start(bf16[4,128,128]{2,1,0:T(8,128)(2,1)S(1)} %slice_bitcast_fusion.1), channel_id=1, source_target_pairs={{0,2},{1,3},{2,0},{3,1},{4,6},{5,7},{6,4},{7,5},{8,10},{9,11},{10,... | collective-permute-start | bytes 393224 | tf_op jit(solution)/shard_map/ppermute | solution.py:23
  37.9 1.3 %collective-permute-done.7 = bf16[4,128,128]{2,1,0:T(8,128)(2,1)S(1)} collective-permute-done((bf16[4,128,128]{2,1,0:T(8,128)(2,1)S(1)}, bf16[4,128,128]{2,1,0:T(8,128)(2,1)S(1)}, u32[]{:S(2)}, u32[]{:S(2)}) %collective-permute-start.7) | collective-permute-done | bytes 131104 | tf_op jit(solution)/shard_map/ppermute | solution.py:23
  39.2 3.8 %collective-permute-done.6 = bf16[4,128,128]{2,1,0:T(8,128)(2,1)S(1)} collective-permute-done((bf16[4,128,128]{2,1,0:T(8,128)(2,1)S(1)}, bf16[4,128,128]{2,1,0:T(8,128)(2,1)S(1)}, u32[]{:S(2)}, u32[]{:S(2)}) %collective-permute-start.6) | collective-permute-done | bytes 131104 | tf_op jit(solution)/shard_map/ppermute | solution.py:23
  43.0 0.1 collective-permute-start.8
  43.1 0.1 pad_add_fusion.1.left
  43.2 0.6 select_reduce_fusion.2
  43.8 1.9 %collective-permute-done.8 = bf16[2,16,128,128]{3,2,0,1:T(8,128)(2,1)S(1)} collective-permute-done((bf16[2,16,128,128]{3,2,0,1:T(8,128)(2,1)S(1)}, bf16[2,16,128,128]{3,2,0,1:T(8,128)(2,1)S(1)}, u32[]{:S(2)}, u32[]{:S(2)}) %collective-permute-start.8) | collective-permute-done | bytes 1048608 | tf_op jit(solution)/shard_map/ppermute | solution.py:23
  45.8 0.2 pad_maximum_fusion
  46.0 0.1 copy.14
  46.1 0.0 all-to-all-done.wave
  46.1 12.0 %products.1 = (f32[16,64,128]{2,1,0:T(8,128)S(1)}, bf16[1,16,64,128]{3,2,1,0:T(8,128)(2,1)S(1)}) custom-call(s32[576]{0:T(1024)S(1)} %pad_add_fusion.1.left, s32[1920]{0:T(1024)S(1)} %pad_add_fusion.right, s32[2]{0:T(128)S(1)} %pad_add_fusion.5.side, bf16[32,128,128]{2,1,0:T(8,128)(2,1)S(1)} %all-to-all-done.wave, bf16[64,128,128]{2,1,0:T(8,128)(2,1)S(1)} %bitcast.41), custom_call_target="tpu_custom_call" | custom-call | tf_op jit(solution)/shard_map/products/pallas_call | solution.py:200
  58.1 0.6 collective-permute-start.9
  58.7 7.8 %collective-permute-done.9 = bf16[16,64,128]{2,1,0:T(8,128)(2,1)S(1)} collective-permute-done((bf16[16,64,128]{2,1,0:T(8,128)(2,1)S(1)}, bf16[16,64,128]{2,1,0:T(8,128)(2,1)S(1)}, u32[]{:S(2)}, u32[]{:S(2)}) %collective-permute-start.9) | collective-permute-done | bytes 262176 | tf_op jit(solution)/shard_map/ppermute | solution.py:222
  66.6 1.2 %broadcast_select_fusion = f32[16,2,64,128]{3,2,1,0:T(8,128)} fusion(f32[16,64,128]{2,1,0:T(8,128)S(1)} %get-tuple-element.12, f32[16,64,128]{2,1,0:T(8,128)S(1)} %convert_element_type.11, pred[2]{0:T(512)(128)(4,1)S(1)} %fusion.2), kind=kLoop, calls=%fused_computation.8 | loop fusion | flops 262144 | bytes 2097154 | tf_op jit(solution)/shard_map/jit(_where)/select_n | solution.py:226
  (27 shorter events, 0.4 us)
Async XLA Ops:
  3.0 13.9 %copy-start = (bf16[2,128,128]{2,1,0:T(8,128)(2,1)S(1)}, bf16[2,128,128]{2,1,0:T(8,128)(2,1)}, u32[]{:S(2)}) copy-start(bf16[2,128,128]{2,1,0:T(8,128)(2,1)} %get-tuple-element.10) | copy-start | bytes 196612
  3.0 15.5 %collective-permute-start.2 = (bf16[2,128,128]{2,1,0:T(8,128)(2,1)}, bf16[2,128,128]{2,1,0:T(8,128)(2,1)S(1)}, u32[]{:S(2)}, u32[]{:S(2)}) collective-permute-start(bf16[2,128,128]{2,1,0:T(8,128)(2,1)} %get-tuple-element.10), channel_id=1, source_target_pairs={{0,8},{1,9},{2,10},{3,11},{4,12},{5,13},{6,14},{7,15},{8,0},{9,1},... | collective-permute-start | bytes 196616 | tf_op jit(solution)/shard_map/ppermute | solution.py:23
  7.1 11.4 %collective-permute-start.3 = (bf16[2,128,128]{2,1,0:T(8,128)(2,1)}, bf16[2,128,128]{2,1,0:T(8,128)(2,1)S(1)}, u32[]{:S(2)}, u32[]{:S(2)}) collective-permute-start(bf16[2,128,128]{2,1,0:T(8,128)(2,1)} %get-tuple-element.10), channel_id=1, source_target_pairs={{0,12},{1,13},{2,14},{3,15},{4,8},{5,9},{6,10},{7,11},{8,4},{9,5},... | collective-permute-start | bytes 196616 | tf_op jit(solution)/shard_map/ppermute | solution.py:23
  8.5 10.1 %collective-permute-start.1 = (bf16[2,128,128]{2,1,0:T(8,128)(2,1)}, bf16[2,128,128]{2,1,0:T(8,128)(2,1)S(1)}, u32[]{:S(2)}, u32[]{:S(2)}) collective-permute-start(bf16[2,128,128]{2,1,0:T(8,128)(2,1)} %get-tuple-element.10), channel_id=1, source_target_pairs={{0,4},{1,5},{2,6},{3,7},{4,0},{5,1},{6,2},{7,3},{8,12},{9,13},{10,... | collective-permute-start | bytes 196616 | tf_op jit(solution)/shard_map/ppermute | solution.py:23
  10.2 7.3 %collective-permute-start = (s32[1,352,3]{1,2,0:T(4,128)S(1)}, s32[1,352,3]{1,2,0:T(4,128)S(1)}, u32[]{:S(2)}, u32[]{:S(2)}) collective-permute-start(s32[1,352,3]{1,2,0:T(4,128)S(1)} %add_bitcast_fusion), channel_id=1, source_target_pairs={{0,16},{16,0},{1,17},{17,1},{2,18},{18,2},{3,19},{19,3},{4,20},{20... | collective-permute-start | bytes 12680 | tf_op jit(solution)/shard_map/ppermute | solution.py:23
  11.7 34.4 %all-to-all-start = ((bf16[32,128,128]{2,1,0:T(8,128)(2,1)}), bf16[32,128,128]{2,1,0:T(8,128)(2,1)S(1)}, u32[]{:S(2)}, u32[]{:S(2)}) async-start(bf16[32,128,128]{2,1,0:T(8,128)(2,1)} %get-tuple-element.9), calls=%async_computation | async-start | bytes 2097152 | tf_op jit(solution)/shard_map/all_to_all | solution.py:171
  18.7 16.6 %collective-permute-start.5 = (bf16[2,4,128,128]{3,2,0,1:T(8,128)(2,1)S(1)}, bf16[2,4,128,128]{3,2,0,1:T(8,128)(2,1)S(1)}, u32[]{:S(2)}, u32[]{:S(2)}) collective-permute-start(bf16[2,4,128,128]{3,2,0,1:T(8,128)(2,1)S(1)} %pad_maximum_fusion.1), channel_id=1, source_target_pairs={{0,16},{16,0},{1,17},{17,1},{2,18},{18,2},{3,19},{19,3},{4,20},{20... | collective-permute-start | bytes 786440 | tf_op jit(solution)/shard_map/ppermute | solution.py:23
  19.3 14.8 %collective-permute-start.4 = (bf16[2,4,128,128]{3,2,1,0:T(8,128)(2,1)S(1)}, bf16[2,4,128,128]{3,2,1,0:T(8,128)(2,1)S(1)}, u32[]{:S(2)}, u32[]{:S(2)}) collective-permute-start(bf16[2,4,128,128]{3,2,1,0:T(8,128)(2,1)S(1)} %copy.11), channel_id=1, source_target_pairs={{0,2},{1,3},{2,0},{3,1},{4,6},{5,7},{6,4},{7,5},{8,10},{9,11},{10,... | collective-permute-start | bytes 786440 | tf_op jit(solution)/shard_map/ppermute | solution.py:23
  34.1 5.1 %collective-permute-start.7 = (bf16[4,128,128]{2,1,0:T(8,128)(2,1)S(1)}, bf16[4,128,128]{2,1,0:T(8,128)(2,1)S(1)}, u32[]{:S(2)}, u32[]{:S(2)}) collective-permute-start(bf16[4,128,128]{2,1,0:T(8,128)(2,1)S(1)} %slice_bitcast_fusion), channel_id=1, source_target_pairs={{0,16},{16,0},{1,17},{17,1},{2,18},{18,2},{3,19},{19,3},{4,20},{20... | collective-permute-start | bytes 393224 | tf_op jit(solution)/shard_map/ppermute | solution.py:23
  35.2 7.7 %collective-permute-start.6 = (bf16[4,128,128]{2,1,0:T(8,128)(2,1)S(1)}, bf16[4,128,128]{2,1,0:T(8,128)(2,1)S(1)}, u32[]{:S(2)}, u32[]{:S(2)}) collective-permute-start(bf16[4,128,128]{2,1,0:T(8,128)(2,1)S(1)} %slice_bitcast_fusion.1), channel_id=1, source_target_pairs={{0,2},{1,3},{2,0},{3,1},{4,6},{5,7},{6,4},{7,5},{8,10},{9,11},{10,... | collective-permute-start | bytes 393224 | tf_op jit(solution)/shard_map/ppermute | solution.py:23
  43.0 2.7 %collective-permute-start.8 = (bf16[2,16,128,128]{3,2,0,1:T(8,128)(2,1)S(1)}, bf16[2,16,128,128]{3,2,0,1:T(8,128)(2,1)S(1)}, u32[]{:S(2)}, u32[]{:S(2)}) collective-permute-start(bf16[2,16,128,128]{3,2,0,1:T(8,128)(2,1)S(1)} %maximum_dynamic-update-slice_fusion), channel_id=1, source_target_pairs={{0,1},{1,0},{2,3},{3,2},{4,5},{5,4},{6,7},{7,6},{8,9},{9,8},{10,11... | collective-permute-start | bytes 3145736 | tf_op jit(solution)/shard_map/ppermute | solution.py:23
  58.1 8.4 %collective-permute-start.9 = (bf16[16,64,128]{2,1,0:T(8,128)(2,1)S(1)}, bf16[16,64,128]{2,1,0:T(8,128)(2,1)S(1)}, u32[]{:S(2)}, u32[]{:S(2)}) collective-permute-start(bf16[16,64,128]{2,1,0:T(8,128)(2,1)S(1)} %bitcast.42), channel_id=1, source_target_pairs={{0,16},{16,0},{1,17},{17,1},{2,18},{18,2},{3,19},{19,3},{4,20},{20... | collective-permute-start | bytes 786440 | tf_op jit(solution)/shard_map/ppermute | solution.py:222

commit v3 on v2

v3 whole, which is shorter than its diff:
```python
import functools

import jax
import jax.numpy as jnp
from jax import lax
from jax.experimental import pallas as pl
from jax.experimental.pallas import tpu as pltpu
from jax.sharding import PartitionSpec as P

INTER_TILES = 32
PACK_UNROLL = 8
DEPTH = 8
LEFT_UNROLL = 32
RIGHT_UNROLL = 8


def vmem_params(size):
    return pltpu.CompilerParams(vmem_limit_bytes=min(size + (6 << 20), 60 << 20))


def round_up(value, step):
    return -(-value // step) * step


def swap(value, axis, mask):
    size = lax.axis_size(axis)
    return lax.ppermute(value, axis, [(i, i ^ mask) for i in range(size)])


def env_place(group, tile):
    sectors, terms = lax.axis_size("sector"), lax.axis_size("term")
    group = group ^ lax.axis_index("term")
    tile = tile ^ lax.axis_index("sector")
    far = sectors // 4
    place = (tile >> 2) + far * (((tile >> 1) & 1) + 2 * group)
    return place + far * 2 * terms * (tile & 1)


def gather_far(env):
    far = [env]
    far += [swap(env, "sector", mask << 2) for mask in range(1, lax.axis_size("sector") // 4)]
    return jnp.stack(far, axis=1)


def gather_env(column):
    terms = lax.axis_size("term")
    across, over = swap(column, "sector", 2), swap(column, "term", 1)
    corner = jnp.stack([swap(over[0], "sector", 2), swap(across[1], "term", 1)])
    plane = jnp.concatenate([column, across, over, corner], axis=1)
    bit = 2
    while bit < terms:
        plane = jnp.concatenate([plane, swap(plane, "term", bit)], axis=1)
        bit *= 2
    return plane, swap(plane, "sector", 1)


def pack_kernel(vectors, picks, wave, left, right, out, env, held, sems):
    vector = lax.rem(lax.axis_index("term"), vectors)
    copies = [
        pltpu.make_async_copy(wave.at[:, vector], held, sems.at[0]),
        pltpu.make_async_copy(left.at[0, 0], env.at[0], sems.at[1]),
        pltpu.make_async_copy(right.at[0, 0], env.at[1], sems.at[2]),
    ]
    for copy in copies:
        copy.start()
    for copy in copies:
        copy.wait()

    @pl.loop(0, out.shape[0] // PACK_UNROLL)
    def _(turn):
        for step in range(PACK_UNROLL):
            slot = turn * PACK_UNROLL + step
            tile = picks[0, slot]
            picked = held[jnp.maximum(tile, 0)]
            out[slot] = jnp.where(tile >= 0, picked, jnp.zeros_like(picked))


def schedule(first, second, target, targets, depth, turn, slots, idle):
    count = target.shape[0]
    index = jnp.arange(count, dtype=jnp.int32)
    same = target[:, None] == target[None, :]
    rank = jnp.sum(same & (index[None, :] < index[:, None]), axis=1, dtype=jnp.int32)
    names = jnp.arange(targets, dtype=jnp.int32)
    counts = jnp.sum(target[None, :] == names[:, None], axis=1, dtype=jnp.int32)
    padded = (counts + depth - 1) // depth * depth
    starts = jnp.sum(
        jnp.where(names[None, :] < target[:, None], padded[None, :], 0), axis=1, dtype=jnp.int32
    )
    place = starts + rank
    chosen = place[None, :] == jnp.arange(slots, dtype=jnp.int32)[:, None]

    def pick(values, rest):
        return rest + jnp.sum(jnp.where(chosen, values[None, :] - rest, 0), axis=1, dtype=jnp.int32)

    ends = [jnp.sum(padded[: targets // 2]), jnp.sum(padded)]
    turns = [(end + turn - 1) // turn for end in ends]
    return jnp.concatenate([pick(first, idle), pick(second, 0), pick(target, 0)]), turns


def tasks_kernel(left, right, after, out):
    out[...] = jnp.zeros_like(out)
    out[0 : left.shape[0], 0 : left.shape[1]] = left[...]
    out[3 : 3 + right.shape[0], 0 : right.shape[1]] = right[...]


def right_products(right, slots, first_turn, last_turn, inter, env, total):
    @pl.loop(first_turn, last_turn)
    def _(turn):
        done = []
        for step in range(RIGHT_UNROLL):
            base = (turn * RIGHT_UNROLL + step) * DEPTH
            first = [inter[right[base + i]] for i in range(DEPTH)]
            second = [env[right[slots + base + i]] for i in range(DEPTH)]
            product = jnp.dot(
                jnp.concatenate(first, axis=1),
                jnp.concatenate(second, axis=0),
                preferred_element_type=jnp.float32,
            )
            done.append((right[2 * slots + base], product))
        for place, product in done:
            total[place] += product


def give(total, first, count, mine, share, keep, send):
    parts = total.shape[1] // share
    own = pl.ds(pl.multiple_of(mine * share, share), share)
    keep[...] = total[pl.ds(first, count), own, :]
    for hop in range(1, parts):
        other = lax.rem(mine + hop, parts)
        theirs = pl.ds(pl.multiple_of(other * share, share), share)
        send[hop - 1] = total[pl.ds(first, count), theirs, :].astype(jnp.bfloat16)


def first_kernel(
    left_count,
    slots,
    share,
    near,
    left,
    right,
    side,
    wave,
    here,
    there,
    keep,
    send,
    inter,
    env_right,
    rest,
    env_left,
    acc,
    total,
    sems,
):
    inters, rows, dim = acc.shape
    mine, block, middle = side[0], side[1], side[2]
    own = here.shape[1]
    row = pl.ds(0 if rows == dim else pl.multiple_of(block * rows, rows), rows)
    acc[...] = jnp.zeros_like(acc)
    total[...] = jnp.zeros_like(total)
    copies = []
    for place, source in enumerate((here, there)):
        span = pl.ds(place * own, own)
        if near:
            env_left[span] = source[0, :, row]
            env_right[span] = source[1]
            continue
        copies.append(
            pltpu.make_async_copy(source.at[0, :, row], env_left.at[span], sems.at[2 * place])
        )
        copies.append(
            pltpu.make_async_copy(source.at[1], env_right.at[span], sems.at[2 * place + 1])
        )
    for copy in copies:
        copy.start()
    for copy in copies:
        copy.wait()

    @pl.loop(0, left_count // LEFT_UNROLL)
    def _(turn):
        done = []
        for step in range(LEFT_UNROLL):
            at = turn * LEFT_UNROLL + step
            product = jnp.dot(
                env_left[left[at]],
                wave[left[left_count + at]],
                preferred_element_type=jnp.float32,
            )
            done.append((left[2 * left_count + at], product))
        for place, product in done:
            acc[place] += product

    @pl.loop(0, inters // 8)
    def _(turn):
        for step in range(8):
            inter[turn * 8 + step] = acc[turn * 8 + step].astype(jnp.bfloat16)

    inter[inters] = jnp.zeros((rows, dim), jnp.bfloat16)
    right_products(right, slots, 0, middle, inter, env_right, total)
    half = total.shape[0] // 2
    give(total, 0, half, mine, share, keep, send)
    rest[...] = total[half:]


def second_kernel(slots, share, right, side, inter, env, rest, keep, send, total):
    half = rest.shape[0]
    total[half:] = rest[...]
    right_products(right, slots, side[2], side[3], inter, env, total)
    give(total, half, half, side[0], share, keep, send)


def finish_kernel(vectors, first, keep, *rest):
    received, (out, held, sems) = rest[: vectors - 1], rest[-3:]
    count = keep.shape[0]
    vector = lax.rem(lax.axis_index("term"), vectors)
    held[vector] = keep[...]
    for hop in range(1, vectors):
        place = lax.rem(vector + vectors - hop, vectors)
        held[place] = received[hop - 1][...].astype(jnp.float32)
    copies = [
        pltpu.make_async_copy(held.at[i], out.at[pl.ds(first, count), i], sems.at[i])
        for i in range(vectors)
    ]
    for copy in copies:
        copy.start()
    for copy in copies:
        copy.wait()


def finish(keep, received, tiles, first, before=None):
    vectors = len(received) + 1
    count, share, dim = keep.shape
    vmem = pl.BlockSpec(memory_space=pltpu.VMEM)
    hbm = pl.BlockSpec(memory_space=pl.ANY)
    operands = [keep] + received + ([] if before is None else [before])
    return pl.pallas_call(
        functools.partial(finish_kernel, vectors, first),
        out_shape=jax.ShapeDtypeStruct((tiles, vectors, share, dim), jnp.float32),
        in_specs=[vmem] * vectors + ([] if before is None else [hbm]),
        out_specs=hbm,
        scratch_shapes=[
            pltpu.VMEM((vectors, count, share, dim), jnp.float32),
            pltpu.SemaphoreType.DMA((vectors,)),
        ],
        compiler_params=vmem_params(3 * vectors * count * share * dim * 4),
        input_output_aliases={} if before is None else {vectors: 0},
        name="finish",
    )(*operands)


def shards(wave_tiles, left_env, right_env, send_list, left_tasks, right_tasks):
    sectors, terms = lax.axis_size("sector"), lax.axis_size("term")
    tiles, vectors, dim, _ = wave_tiles.shape
    term = lax.axis_index("term")
    blocks = terms // vectors
    rows, share = dim // blocks, dim // terms
    vector, block = term % vectors, term // vectors

    vmem = pl.BlockSpec(memory_space=pltpu.VMEM)
    smem = pl.BlockSpec(memory_space=pltpu.SMEM)
    hbm = pl.BlockSpec(memory_space=pl.ANY)
    send_slots = send_list.shape[1]
    tile_bytes = dim * dim * 2
    outgoing, env = pl.pallas_call(
        functools.partial(pack_kernel, vectors),
        out_shape=(
            jax.ShapeDtypeStruct((send_slots, dim, dim), jnp.bfloat16),
            jax.ShapeDtypeStruct((2, dim, dim), jnp.bfloat16),
        ),
        in_specs=[smem, hbm, hbm, hbm],
        out_specs=(vmem, vmem),
        scratch_shapes=[
            pltpu.VMEM((tiles, dim, dim), jnp.bfloat16),
            pltpu.SemaphoreType.DMA((3,)),
        ],
        compiler_params=vmem_params(54 << 20),
        name="pack",
    )(send_list, wave_tiles, left_env, right_env)
    column = gather_far(env)
    received = lax.all_to_all(outgoing, "sector", split_axis=0, concat_axis=0, tiled=True)
    here, there = gather_env(column)

    left_count, right_count = left_tasks.shape[2], right_tasks.shape[2]
    tasks = pl.pallas_call(
        tasks_kernel,
        out_shape=jax.ShapeDtypeStruct((8, max(left_count, right_count)), jnp.int32),
        in_specs=[vmem, vmem, hbm],
        out_specs=vmem,
        compiler_params=vmem_params(0),
        name="tasks",
    )(left_tasks[0, 0].T, right_tasks[0, 0].T, column)[None]
    bit = 1
    while bit < terms:
        tasks = jnp.concatenate([tasks, swap(tasks, "term", bit)], axis=0)
        bit *= 2
    left_rows, right_rows = tasks[:, 0:3, :left_count], tasks[:, 3:6, :right_count]
    groups = jnp.arange(terms, dtype=jnp.int32)[:, None] ^ term
    left_count, right_count = terms * left_count, terms * right_count
    left = jnp.concatenate(
        [
            env_place(groups, left_rows[:, 0]).reshape(-1),
            left_rows[:, 1].reshape(-1),
            (groups * INTER_TILES + left_rows[:, 2]).reshape(-1),
        ]
    )
    turn = DEPTH * RIGHT_UNROLL
    slots = round_up(right_count + tiles * (DEPTH - 1), turn)
    inters = terms * INTER_TILES
    right, turns = schedule(
        (groups * INTER_TILES + right_rows[:, 0]).reshape(-1),
        env_place(groups, right_rows[:, 1]).reshape(-1),
        right_rows[:, 2].reshape(-1),
        tiles,
        DEPTH,
        turn,
        slots,
        inters,
    )
    side = jnp.stack([vector, block] + turns).astype(jnp.int32)
    half = tiles // 2
    block_bytes = rows * dim * 2
    env_bytes = here.size * 2
    near = env_bytes <= 4 << 20
    rest_bytes = (tiles * 6 + inters) * block_bytes + env_bytes
    first_bytes = rest_bytes + (inters * 2 + here.shape[1] * 2) * block_bytes
    first_bytes += send_slots * tile_bytes + (2 * env_bytes if near else 0)
    keep_shape = jax.ShapeDtypeStruct((half, share, dim), jnp.float32)
    send_shape = jax.ShapeDtypeStruct((vectors - 1, half, share, dim), jnp.bfloat16)
    keep_one, send_one, inter, env_right, rest = pl.pallas_call(
        functools.partial(first_kernel, left_count, slots, share, near),
        out_shape=(
            keep_shape,
            send_shape,
            jax.ShapeDtypeStruct((inters + 1, rows, dim), jnp.bfloat16),
            jax.ShapeDtypeStruct((2 * here.shape[1], dim, dim), jnp.bfloat16),
            jax.ShapeDtypeStruct((tiles - half, rows, dim), jnp.float32),
        ),
        in_specs=[smem, smem, smem, vmem] + [vmem if near else hbm] * 2,
        out_specs=(vmem, vmem, vmem, vmem, vmem),
        scratch_shapes=[
            pltpu.VMEM((2 * here.shape[1], rows, dim), jnp.bfloat16),
            pltpu.VMEM((inters, rows, dim), jnp.float32),
            pltpu.VMEM((tiles, rows, dim), jnp.float32),
            pltpu.SemaphoreType.DMA((4,)),
        ],
        compiler_params=vmem_params(first_bytes),
        name="first_products",
    )(left, right, side, received, here, there)
    keep_two, send_two = pl.pallas_call(
        functools.partial(second_kernel, slots, share),
        out_shape=(keep_shape, send_shape),
        in_specs=[smem, smem, vmem, vmem, vmem],
        out_specs=(vmem, vmem),
        scratch_shapes=[pltpu.VMEM((tiles, rows, dim), jnp.float32)],
        compiler_params=vmem_params(rest_bytes),
        cost_estimate=pl.CostEstimate(
            flops=right_count * rows * dim * dim, bytes_accessed=12 << 20, transcendentals=0
        ),
        name="second_products",
    )(right, side, inter, env_right, rest)

    def exchange(send):
        moved = []
        for hop in range(1, vectors):
            pairs = [
                (i, i // vectors * vectors + (i % vectors + hop) % vectors) for i in range(terms)
            ]
            moved.append(lax.ppermute(send[hop - 1], "term", pairs))
        return moved

    result = finish(keep_one, exchange(send_one), tiles, 0)
    return finish(keep_two, exchange(send_two), tiles, half, result)


def solution(mesh):
    in_specs = (
        P("sector", None, None, None),
        P("term", "sector", None, None),
        P("term", "sector", None, None),
        P("sector", None),
        P("term", "sector", None, None),
        P("term", "sector", None, None),
    )
    out_specs = P("sector", None, "term", None)
    return jax.shard_map(shards, mesh=mesh, in_specs=in_specs, out_specs=out_specs, check_vma=False)
```

time: 68 us -> 59.8 us (0.88)
  waiting for transfers between devices: 27.7 us -> 16.7 us
  starting transfers between devices: 19.2 us -> 21.3 us
  local copies, waits for them, and re-layouts: 2.52 us -> 1.02 us
  between operations: 0.23 us -> 1.56 us
  Pallas kernels: 15 us -> 16.2 us
    ppermute x9, waiting for transfers between devices: 19.9 us -> 12.9 us  [swap(): return lax.ppermute(value, axis, [(i, i ^ mask) for i in range(size)])]
    ppermute x1 -> x2, waiting for transfers between devices: 7.85 us -> 3.85 us  [exchange(): moved.append(lax.ppermute(send[hop - 1], 'term', pairs))]
    ppermute x1 -> x2, starting transfers between devices: 0.55 us -> 2.16 us  [exchange(): moved.append(lax.ppermute(send[hop - 1], 'term', pairs))]
    reduce_sum x0 -> x2, other arithmetic: none -> 1.35 us  [schedule(): ends = [jnp.sum(padded[:targets // 2]), jnp.sum(padded)]]
    unnamed x14 -> x18, local copies, waits for them, and re-layouts: 1.63 us -> 0.28 us
    pallas_call x1 -> x5, Pallas kernels: 12 us -> 13.2 us  [the longest x1 7.19 us: shards(): pl.pallas_call(functools.partial(first_kernel, left_count, slots, share,...]
    select_n x1 -> x0, other arithmetic: 1.16 us -> none  [shards(): result = jnp.where(hops == hop, pieces[hop][:, None], result)]
    all_to_all x1, starting transfers between devices: 5.26 us -> 6.08 us  [shards(): lax.all_to_all(outgoing, 'sector', split_axis=0, concat_axis=0, tiled=True)]
  transfers between devices with their start and end apart: 11 -> 12, of which waited for: 5 -> 6; matrix products, arithmetic and copies ran while one was open for 6% -> 6% of each run, Pallas kernels for 0% -> 9%
where the time goes in v3:
time: 59.8 us; the launch traced here: 59.6 us
  starting transfers between devices  21.3 us (36%)
  waiting for transfers between devices  16.7 us (28%)
  Pallas kernels  16.2 us (27%)
  other arithmetic  2.75 us (5%)
  between operations  1.56 us (3%)
  local copies, waits for them, and re-layouts  1.02 us (2%)
    ppermute x9, starting transfers between devices, swap(): return lax.ppermute(value, axis, [(i, i ^ mask) for i in range(size)])  13.1 us
    ppermute x9, waiting for transfers between devices, swap(): return lax.ppermute(value, axis, [(i, i ^ mask) for i in range(size)])  12.9 us
    pallas_call x1, Pallas kernels, shards(): pl.pallas_call(functools.partial(first_kernel, left_count, slots, share,...  7.19 us
    all_to_all x1, starting transfers between devices, shards(): lax.all_to_all(outgoing, 'sector', split_axis=0, concat_axis=0, tiled=True)  6.08 us
    pallas_call x1, Pallas kernels, shards(): pl.pallas_call(functools.partial(second_kernel, slots, share), out_shape=...  4.29 us
    ppermute x2, waiting for transfers between devices, exchange(): moved.append(lax.ppermute(send[hop - 1], 'term', pairs))  3.85 us
    pallas_call x1, Pallas kernels, shards(): pl.pallas_call(functools.partial(pack_kernel, vectors), out_shape=(jax.Sh...  3.02 us
    ppermute x2, starting transfers between devices, exchange(): moved.append(lax.ppermute(send[hop - 1], 'term', pairs))  2.16 us
  transfers between devices with their start and end apart: 12, of which 6 were waited for; matrix products, arithmetic and copies ran while one was open for 6% of the time, Pallas kernels for 9%

profile of v3, /device:TPU:0, one launch (start us, length us, event | category | flops | bytes accessed | tf_op | source)
XLA Modules:
  0.0 59.6 jit_solution(10461380273839126650)
XLA Ops:
  0.0 3.0 %pack.1 = (bf16[32,128,128]{2,1,0:T(8,128)(2,1)}, bf16[2,128,128]{2,1,0:T(8,128)(2,1)}) custom-call(s32[1,32]{1,0:T(1,128)} %picks.1, bf16[16,2,128,128]{3,2,1,0:T(8,128)(2,1)} %wave.1, bf16[1,1,128,128]{3,2,1,0:T(8,128)(2,1)} %left.1, bf16[1,1,128,128]{3,2,1,0:T(8,128)(2,1)} %right.1), custom_call_target="tpu_custom_call" | custom-call | tf_op jit(solution)/shard_map/pack/pallas_call | solution.py:264
  3.0 0.0 copy-start
  3.0 0.0 copy-start.2
  3.0 0.0 copy-start.1
  3.1 5.1 %collective-permute-start.2 = (bf16[2,128,128]{2,1,0:T(8,128)(2,1)}, bf16[2,128,128]{2,1,0:T(8,128)(2,1)S(1)}, u32[]{:S(2)}, u32[]{:S(2)}) collective-permute-start(bf16[2,128,128]{2,1,0:T(8,128)(2,1)} %get-tuple-element.14), channel_id=1, source_target_pairs={{0,12},{1,13},{2,14},{3,15},{4,8},{5,9},{6,10},{7,11},{8,4},{9,5},... | collective-permute-start | bytes 196616 | tf_op jit(solution)/shard_map/ppermute | solution.py:27
  8.2 0.0 collective-permute-start.1
  8.2 0.6 %collective-permute-start = (bf16[2,128,128]{2,1,0:T(8,128)(2,1)}, bf16[2,128,128]{2,1,0:T(8,128)(2,1)S(1)}, u32[]{:S(2)}, u32[]{:S(2)}) collective-permute-start(bf16[2,128,128]{2,1,0:T(8,128)(2,1)} %get-tuple-element.14), channel_id=1, source_target_pairs={{0,4},{1,5},{2,6},{3,7},{4,0},{5,1},{6,2},{7,3},{8,12},{9,13},{10,... | collective-permute-start | bytes 196616 | tf_op jit(solution)/shard_map/ppermute | solution.py:27
  8.8 6.1 %all-to-all-start = ((bf16[32,128,128]{2,1,0:T(8,128)(2,1)}), bf16[32,128,128]{2,1,0:T(8,128)(2,1)S(1)}, u32[]{:S(2)}, u32[]{:S(2)}) async-start(bf16[32,128,128]{2,1,0:T(8,128)(2,1)} %get-tuple-element.15), calls=%async_computation | async-start | bytes 2097152 | tf_op jit(solution)/shard_map/all_to_all | solution.py:280
  14.9 0.0 copy-done
  15.0 0.1 broadcast_bitcast_fusion.1
  15.0 0.1 broadcast_bitcast_fusion
  15.1 0.1 add.135
  15.2 0.1 add.136
  15.2 0.1 add.140
  15.3 0.1 add.141
  15.4 0.0 copy-done.2
  15.4 0.0 copy-done.1
  15.5 0.0 collective-permute-done.2
  15.5 0.0 collective-permute-done.1
  15.5 0.0 collective-permute-done
  15.5 1.6 %collective-permute-start.5 = (bf16[2,4,128,128]{3,2,1,0:T(8,128)(2,1)S(1)}, bf16[2,4,128,128]{3,2,1,0:T(8,128)(2,1)S(1)}, u32[]{:S(2)}, u32[]{:S(2)}) collective-permute-start(bf16[2,4,128,128]{3,2,1,0:T(8,128)(2,1)S(1)} %pad_maximum_fusion.after), channel_id=1, source_target_pairs={{0,16},{16,0},{1,17},{17,1},{2,18},{18,2},{3,19},{19,3},{4,20},{20... | collective-permute-start | bytes 786440 | tf_op jit(solution)/shard_map/ppermute | solution.py:27
  17.1 1.9 %collective-permute-start.4 = (bf16[2,4,128,128]{3,2,1,0:T(8,128)(2,1)S(1)}, bf16[2,4,128,128]{3,2,1,0:T(8,128)(2,1)S(1)}, u32[]{:S(2)}, u32[]{:S(2)}) collective-permute-start(bf16[2,4,128,128]{3,2,1,0:T(8,128)(2,1)S(1)} %pad_maximum_fusion.after), channel_id=1, source_target_pairs={{0,2},{1,3},{2,0},{3,1},{4,6},{5,7},{6,4},{7,5},{8,10},{9,11},{10,... | collective-permute-start | bytes 786440 | tf_op jit(solution)/shard_map/ppermute | solution.py:27
  19.0 0.5 collective-permute-start.3
  19.6 4.8 %collective-permute-done.3 = s32[1,8,256]{2,1,0:T(8,128)S(1)} collective-permute-done((s32[1,8,256]{2,1,0:T(8,128)S(1)}, s32[1,8,256]{2,1,0:T(8,128)S(1)}, u32[]{:S(2)}, u32[]{:S(2)}) %collective-permute-start.3) | collective-permute-done | bytes 8224 | tf_op jit(solution)/shard_map/ppermute | solution.py:27
  24.4 0.1 reshape_squeeze.3
  24.5 0.1 convert_reduce_fusion.1
  24.6 0.7 %fusion.4 = (s32[]{:T(128)}, s32[16]{0:T(128)S(1)}) fusion(s32[16]{0:T(128)S(1)} %convert_reduce_fusion.1), kind=kLoop, calls=%fused_computation.54 | loop fusion | flops 287 | bytes 132 | tf_op jit(solution)/shard_map/reduce_sum | solution.py:95
  25.4 0.1 squeeze.29
  25.5 0.1 select_reduce_fusion.3
  25.6 0.1 and.76
  25.6 0.1 mul.77
  25.7 0.1 shift_right_arithmetic.42
  25.8 0.1 pad_add_fusion.1.left
  25.9 0.2 convert_reduce_fusion
  26.2 0.6 %slice_reduce_fusion = s32[]{:T(128)} fusion(s32[16]{0:T(128)S(1)} %get-tuple-element.32), kind=kLoop, calls=%fused_computation.49 | loop fusion | flops 7 | bytes 36 | tf_op jit(solution)/shard_map/reduce_sum | solution.py:95
  28.1 0.0 collective-permute-done.5
  28.1 1.7 %collective-permute-start.6 = (bf16[4,128,128]{2,1,0:T(8,128)(2,1)S(1)}, bf16[4,128,128]{2,1,0:T(8,128)(2,1)S(1)}, u32[]{:S(2)}, u32[]{:S(2)}) collective-permute-start(bf16[4,128,128]{2,1,0:T(8,128)(2,1)S(1)} %slice_bitcast_fusion.1), channel_id=1, source_target_pairs={{0,2},{1,3},{2,0},{3,1},{4,6},{5,7},{6,4},{7,5},{8,10},{9,11},{10,... | collective-permute-start | bytes 393224 | tf_op jit(solution)/shard_map/ppermute | solution.py:27
  29.8 2.7 %collective-permute-done.4 = bf16[2,4,128,128]{3,2,1,0:T(8,128)(2,1)S(1)} collective-permute-done((bf16[2,4,128,128]{3,2,1,0:T(8,128)(2,1)S(1)}, bf16[2,4,128,128]{3,2,1,0:T(8,128)(2,1)S(1)}, u32[]{:S(2)}, u32[]{:S(2)}) %collective-permute-start.4) | collective-permute-done | bytes 262176 | tf_op jit(solution)/shard_map/ppermute | solution.py:27
  32.6 1.6 %collective-permute-start.7 = (bf16[4,128,128]{2,1,0:T(8,128)(2,1)S(1)}, bf16[4,128,128]{2,1,0:T(8,128)(2,1)S(1)}, u32[]{:S(2)}, u32[]{:S(2)}) collective-permute-start(bf16[4,128,128]{2,1,0:T(8,128)(2,1)S(1)} %slice_bitcast_fusion), channel_id=1, source_target_pairs={{0,16},{16,0},{1,17},{17,1},{2,18},{18,2},{3,19},{19,3},{4,20},{20... | collective-permute-start | bytes 393224 | tf_op jit(solution)/shard_map/ppermute | solution.py:27
  34.2 0.7 %collective-permute-done.6 = bf16[4,128,128]{2,1,0:T(8,128)(2,1)S(1)} collective-permute-done((bf16[4,128,128]{2,1,0:T(8,128)(2,1)S(1)}, bf16[4,128,128]{2,1,0:T(8,128)(2,1)S(1)}, u32[]{:S(2)}, u32[]{:S(2)}) %collective-permute-start.6) | collective-permute-done | bytes 131104 | tf_op jit(solution)/shard_map/ppermute | solution.py:27
  34.9 2.7 %collective-permute-done.7 = bf16[4,128,128]{2,1,0:T(8,128)(2,1)S(1)} collective-permute-done((bf16[4,128,128]{2,1,0:T(8,128)(2,1)S(1)}, bf16[4,128,128]{2,1,0:T(8,128)(2,1)S(1)}, u32[]{:S(2)}, u32[]{:S(2)}) %collective-permute-start.7) | collective-permute-done | bytes 131104 | tf_op jit(solution)/shard_map/ppermute | solution.py:27
  37.6 0.1 collective-permute-start.8
  37.7 0.1 pad_add_fusion.5.side
  37.8 0.6 %select_reduce_fusion.2 = (s32[640]{0:T(1024)S(1)}, s32[640]{0:T(1024)S(1)}, s32[640]{0:T(1024)S(1)}) fusion(s32[512]{0:T(512)S(1)} %add_add_fusion.1, s32[512]{0:T(512)S(1)} %add.123, s32[512]{0:T(512)S(1)} %bitcast.58, s32[512]{0:T(512)S(1)} %add_add_fusion), kind=kLoop, calls=%fused_computation.2 | loop fusion | flops 2291840 | bytes 15872 | tf_op jit(solution)/shard_map/reduce_sum | solution.py:93
  38.4 1.9 %collective-permute-done.8.there = bf16[2,16,128,128]{3,2,1,0:T(8,128)(2,1)S(1)} collective-permute-done((bf16[2,16,128,128]{3,2,1,0:T(8,128)(2,1)S(1)}, bf16[2,16,128,128]{3,2,1,0:T(8,128)(2,1)S(1)}, u32[]{:S(2)}, u32[]{:S(2)}) %collective-permute-start.8) | collective-permute-done | bytes 1048608 | tf_op jit(solution)/shard_map/ppermute | solution.py:27
  40.4 0.0 all-to-all-done.wave
  40.4 7.2 %first_products.1 = (f32[8,64,128]{2,1,0:T(8,128)S(1)}, bf16[1,8,64,128]{3,2,1,0:T(8,128)(2,1)S(1)}, bf16[65,128,128]{2,1,0:T(8,128)(2,1)S(1)}, bf16[32,128,128]{2,1,0:T(8,128)(2,1)S(1)}, f32[8,128,128]{2,1,0:T(8,128)S(1)}) custom-call(s32[576]{0:T(1024)S(1)} %pad_add_fusion.1.left, s32[1920]{0:T(1024)S(1)} %pad_add_fusion.right, s32[4]{0:T(128)S(1)} %pad_add_fusion.5.side, ...), custom_call_target="tpu_custom_call" | custom-call | tf_op jit(solution)/shard_map/first_products/pallas_call | solution.py:329
  47.6 1.6 %collective-permute-start.10 = (bf16[8,64,128]{2,1,0:T(8,128)(2,1)S(1)}, bf16[8,64,128]{2,1,0:T(8,128)(2,1)S(1)}, u32[]{:S(2)}, u32[]{:S(2)}) collective-permute-start(bf16[8,64,128]{2,1,0:T(8,128)(2,1)S(1)} %bitcast.47), channel_id=1, source_target_pairs={{0,16},{16,0},{1,17},{17,1},{2,18},{18,2},{3,19},{19,3},{4,20},{20... | collective-permute-start | bytes 393224 | tf_op jit(solution)/shard_map/ppermute | solution.py:368
  49.1 4.3 %second_products.1 = (f32[8,64,128]{2,1,0:T(8,128)S(1)}, bf16[1,8,64,128]{3,2,1,0:T(8,128)(2,1)S(1)}) custom-call(s32[1920]{0:T(1024)S(1)} %pad_add_fusion.right, s32[4]{0:T(128)S(1)} %pad_add_fusion.5.side, bf16[65,128,128]{2,1,0:T(8,128)(2,1)S(1)} %get-tuple-element.16.inter, bf16[32,128,128]{2,1,0:T(8,128)(2,1)S(1)} %get-tuple-element.17.env, ...), custom_call_target="tpu_custom_call" | custom-call | flops 1073741824 | bytes 12582912 | tf_op jit(solution)/shard_map/second_products/pallas_call | solution.py:349
  53.4 0.6 %collective-permute-start.9 = (bf16[8,64,128]{2,1,0:T(8,128)(2,1)S(1)}, bf16[8,64,128]{2,1,0:T(8,128)(2,1)S(1)}, u32[]{:S(2)}, u32[]{:S(2)}) collective-permute-start(bf16[8,64,128]{2,1,0:T(8,128)(2,1)S(1)} %bitcast.48), channel_id=1, source_target_pairs={{0,16},{16,0},{1,17},{17,1},{2,18},{18,2},{3,19},{19,3},{4,20},{20... | collective-permute-start | bytes 393224 | tf_op jit(solution)/shard_map/ppermute | solution.py:368
  54.0 0.0 collective-permute-done.10.rest_0_
  54.0 0.9 %finish.2.rest_1_ = f32[16,2,64,128]{3,2,1,0:T(8,128)} custom-call(f32[8,64,128]{2,1,0:T(8,128)S(1)} %get-tuple-element.21.keep, bf16[8,64,128]{2,1,0:T(8,128)(2,1)S(1)} %collective-permute-done.10.rest_0_), custom_call_target="tpu_custom_call" | custom-call | tf_op jit(solution)/shard_map/finish/pallas_call | solution.py:236
  54.9 3.8 %collective-permute-done.9.rest_0_ = bf16[8,64,128]{2,1,0:T(8,128)(2,1)S(1)} collective-permute-done((bf16[8,64,128]{2,1,0:T(8,128)(2,1)S(1)}, bf16[8,64,128]{2,1,0:T(8,128)(2,1)S(1)}, u32[]{:S(2)}, u32[]{:S(2)}) %collective-permute-start.9) | collective-permute-done | bytes 131104 | tf_op jit(solution)/shard_map/ppermute | solution.py:368
  58.7 0.9 %finish.3 = f32[16,2,64,128]{3,2,1,0:T(8,128)} custom-call(f32[8,64,128]{2,1,0:T(8,128)S(1)} %get-tuple-element.19.keep, bf16[8,64,128]{2,1,0:T(8,128)(2,1)S(1)} %collective-permute-done.9.rest_0_, f32[16,2,64,128]{3,2,1,0:T(8,128)} %finish.2.rest_1_), custom_call_target="tpu_custom_call", output_to_operand_aliasing={{}: (2, {})} | custom-call | tf_op jit(solution)/shard_map/finish/pallas_call | solution.py:236
  (27 shorter events, 0.3 us)
Async XLA Ops:
  3.0 11.9 %copy-start = (bf16[2,128,128]{2,1,0:T(8,128)(2,1)S(1)}, bf16[2,128,128]{2,1,0:T(8,128)(2,1)}, u32[]{:S(2)}) copy-start(bf16[2,128,128]{2,1,0:T(8,128)(2,1)} %get-tuple-element.14) | copy-start | bytes 196612
  3.0 12.4 %copy-start.2 = (s32[1,1,96,3]{2,1,3,0:T(1,128)S(1)}, s32[1,1,96,3]{2,1,3,0:T(1,128)}, u32[]{:S(2)}) copy-start(s32[1,1,96,3]{2,1,3,0:T(1,128)} %param.10) | copy-start | bytes 3460
  3.0 12.4 %copy-start.1 = (s32[1,1,256,3]{2,1,3,0:T(1,128)S(1)}, s32[1,1,256,3]{2,1,3,0:T(1,128)}, u32[]{:S(2)}) copy-start(s32[1,1,256,3]{2,1,3,0:T(1,128)} %param.11) | copy-start | bytes 9220
  3.1 12.4 %collective-permute-start.2 = (bf16[2,128,128]{2,1,0:T(8,128)(2,1)}, bf16[2,128,128]{2,1,0:T(8,128)(2,1)S(1)}, u32[]{:S(2)}, u32[]{:S(2)}) collective-permute-start(bf16[2,128,128]{2,1,0:T(8,128)(2,1)} %get-tuple-element.14), channel_id=1, source_target_pairs={{0,12},{1,13},{2,14},{3,15},{4,8},{5,9},{6,10},{7,11},{8,4},{9,5},... | collective-permute-start | bytes 196616 | tf_op jit(solution)/shard_map/ppermute | solution.py:27
  8.2 7.3 %collective-permute-start.1 = (bf16[2,128,128]{2,1,0:T(8,128)(2,1)}, bf16[2,128,128]{2,1,0:T(8,128)(2,1)S(1)}, u32[]{:S(2)}, u32[]{:S(2)}) collective-permute-start(bf16[2,128,128]{2,1,0:T(8,128)(2,1)} %get-tuple-element.14), channel_id=1, source_target_pairs={{0,8},{1,9},{2,10},{3,11},{4,12},{5,13},{6,14},{7,15},{8,0},{9,1},... | collective-permute-start | bytes 196616 | tf_op jit(solution)/shard_map/ppermute | solution.py:27
  8.2 7.3 %collective-permute-start = (bf16[2,128,128]{2,1,0:T(8,128)(2,1)}, bf16[2,128,128]{2,1,0:T(8,128)(2,1)S(1)}, u32[]{:S(2)}, u32[]{:S(2)}) collective-permute-start(bf16[2,128,128]{2,1,0:T(8,128)(2,1)} %get-tuple-element.14), channel_id=1, source_target_pairs={{0,4},{1,5},{2,6},{3,7},{4,0},{5,1},{6,2},{7,3},{8,12},{9,13},{10,... | collective-permute-start | bytes 196616 | tf_op jit(solution)/shard_map/ppermute | solution.py:27
  8.8 31.5 %all-to-all-start = ((bf16[32,128,128]{2,1,0:T(8,128)(2,1)}), bf16[32,128,128]{2,1,0:T(8,128)(2,1)S(1)}, u32[]{:S(2)}, u32[]{:S(2)}) async-start(bf16[32,128,128]{2,1,0:T(8,128)(2,1)} %get-tuple-element.15), calls=%async_computation | async-start | bytes 2097152 | tf_op jit(solution)/shard_map/all_to_all | solution.py:280
  15.5 12.6 %collective-permute-start.5 = (bf16[2,4,128,128]{3,2,1,0:T(8,128)(2,1)S(1)}, bf16[2,4,128,128]{3,2,1,0:T(8,128)(2,1)S(1)}, u32[]{:S(2)}, u32[]{:S(2)}) collective-permute-start(bf16[2,4,128,128]{3,2,1,0:T(8,128)(2,1)S(1)} %pad_maximum_fusion.after), channel_id=1, source_target_pairs={{0,16},{16,0},{1,17},{17,1},{2,18},{18,2},{3,19},{19,3},{4,20},{20... | collective-permute-start | bytes 786440 | tf_op jit(solution)/shard_map/ppermute | solution.py:27
  17.1 15.5 %collective-permute-start.4 = (bf16[2,4,128,128]{3,2,1,0:T(8,128)(2,1)S(1)}, bf16[2,4,128,128]{3,2,1,0:T(8,128)(2,1)S(1)}, u32[]{:S(2)}, u32[]{:S(2)}) collective-permute-start(bf16[2,4,128,128]{3,2,1,0:T(8,128)(2,1)S(1)} %pad_maximum_fusion.after), channel_id=1, source_target_pairs={{0,2},{1,3},{2,0},{3,1},{4,6},{5,7},{6,4},{7,5},{8,10},{9,11},{10,... | collective-permute-start | bytes 786440 | tf_op jit(solution)/shard_map/ppermute | solution.py:27
  19.0 5.4 %collective-permute-start.3 = (s32[1,8,256]{2,1,0:T(8,128)S(1)}, s32[1,8,256]{2,1,0:T(8,128)S(1)}, u32[]{:S(2)}, u32[]{:S(2)}) collective-permute-start(s32[1,8,256]{2,1,0:T(8,128)S(1)} %bitcast.42), channel_id=1, source_target_pairs={{0,16},{16,0},{1,17},{17,1},{2,18},{18,2},{3,19},{19,3},{4,20},{20... | collective-permute-start | bytes 24584 | tf_op jit(solution)/shard_map/ppermute | solution.py:27
  28.1 6.8 %collective-permute-start.6 = (bf16[4,128,128]{2,1,0:T(8,128)(2,1)S(1)}, bf16[4,128,128]{2,1,0:T(8,128)(2,1)S(1)}, u32[]{:S(2)}, u32[]{:S(2)}) collective-permute-start(bf16[4,128,128]{2,1,0:T(8,128)(2,1)S(1)} %slice_bitcast_fusion.1), channel_id=1, source_target_pairs={{0,2},{1,3},{2,0},{3,1},{4,6},{5,7},{6,4},{7,5},{8,10},{9,11},{10,... | collective-permute-start | bytes 393224 | tf_op jit(solution)/shard_map/ppermute | solution.py:27
  32.6 5.0 %collective-permute-start.7 = (bf16[4,128,128]{2,1,0:T(8,128)(2,1)S(1)}, bf16[4,128,128]{2,1,0:T(8,128)(2,1)S(1)}, u32[]{:S(2)}, u32[]{:S(2)}) collective-permute-start(bf16[4,128,128]{2,1,0:T(8,128)(2,1)S(1)} %slice_bitcast_fusion), channel_id=1, source_target_pairs={{0,16},{16,0},{1,17},{17,1},{2,18},{18,2},{3,19},{19,3},{4,20},{20... | collective-permute-start | bytes 393224 | tf_op jit(solution)/shard_map/ppermute | solution.py:27
  37.6 2.7 %collective-permute-start.8 = (bf16[2,16,128,128]{3,2,1,0:T(8,128)(2,1)S(1)}, bf16[2,16,128,128]{3,2,1,0:T(8,128)(2,1)S(1)}, u32[]{:S(2)}, u32[]{:S(2)}) collective-permute-start(bf16[2,16,128,128]{3,2,1,0:T(8,128)(2,1)S(1)} %maximum_dynamic-update-slice_fusion.here), channel_id=1, source_target_pairs={{0,1},{1,0},{2,3},{3,2},{4,5},{5,4},{6,7},{7,6},{8,9},{9,8},{10,11... | collective-permute-start | bytes 3145736 | tf_op jit(solution)/shard_map/ppermute | solution.py:27
  47.6 6.5 %collective-permute-start.10 = (bf16[8,64,128]{2,1,0:T(8,128)(2,1)S(1)}, bf16[8,64,128]{2,1,0:T(8,128)(2,1)S(1)}, u32[]{:S(2)}, u32[]{:S(2)}) collective-permute-start(bf16[8,64,128]{2,1,0:T(8,128)(2,1)S(1)} %bitcast.47), channel_id=1, source_target_pairs={{0,16},{16,0},{1,17},{17,1},{2,18},{18,2},{3,19},{19,3},{4,20},{20... | collective-permute-start | bytes 393224 | tf_op jit(solution)/shard_map/ppermute | solution.py:368
  53.4 5.3 %collective-permute-start.9 = (bf16[8,64,128]{2,1,0:T(8,128)(2,1)S(1)}, bf16[8,64,128]{2,1,0:T(8,128)(2,1)S(1)}, u32[]{:S(2)}, u32[]{:S(2)}) collective-permute-start(bf16[8,64,128]{2,1,0:T(8,128)(2,1)S(1)} %bitcast.48), channel_id=1, source_target_pairs={{0,16},{16,0},{1,17},{17,1},{2,18},{18,2},{3,19},{19,3},{4,20},{20... | collective-permute-start | bytes 393224 | tf_op jit(solution)/shard_map/ppermute | solution.py:368

commit v4 on v3

--- a/solution.py
+++ b/solution.py
@@ -36,22 +36,38 @@
     return place + far * 2 * terms * (tile & 1)
 
 
+def column_kernel(count, *refs):
+    tiles, sides = refs[:count], refs[count:]
+    for place in range(count):
+        for side in range(2):
+            sides[side][place] = tiles[place][side]
+
+
 def gather_far(env):
-    far = [env]
-    far += [swap(env, "sector", mask << 2) for mask in range(1, lax.axis_size("sector") // 4)]
-    return jnp.stack(far, axis=1)
+    count = lax.axis_size("sector") // 4
+    vmem = pl.BlockSpec(memory_space=pltpu.VMEM)
+    return pl.pallas_call(
+        functools.partial(column_kernel, count),
+        out_shape=[jax.ShapeDtypeStruct((count,) + env.shape[1:], env.dtype)] * 2,
+        in_specs=[vmem] * count,
+        out_specs=[vmem] * 2,
+        compiler_params=vmem_params(4 * count * env.size),
+        name="column",
+    )(env, *[swap(env, "sector", mask << 2) for mask in range(1, count)])
 
 
 def gather_env(column):
     terms = lax.axis_size("term")
-    across, over = swap(column, "sector", 2), swap(column, "term", 1)
-    corner = jnp.stack([swap(over[0], "sector", 2), swap(across[1], "term", 1)])
-    plane = jnp.concatenate([column, across, over, corner], axis=1)
-    bit = 2
-    while bit < terms:
-        plane = jnp.concatenate([plane, swap(plane, "term", bit)], axis=1)
-        bit *= 2
-    return plane, swap(plane, "sector", 1)
+    sides = []
+    for side in range(2):
+        across, over = swap(column[side], "sector", 2), swap(column[side], "term", 1)
+        plane = jnp.concatenate([column[side], across, over, swap(across, "term", 1)])
+        bit = 2
+        while bit < terms:
+            plane = jnp.concatenate([plane, swap(plane, "term", bit)])
+            bit *= 2
+        sides.append((plane, swap(plane, "sector", 1)))
+    return sides
 
 
 def pack_kernel(vectors, picks, wave, left, right, out, env, held, sems):
@@ -75,7 +91,7 @@
             out[slot] = jnp.where(tile >= 0, picked, jnp.zeros_like(picked))
 
 
-def schedule(first, second, target, targets, depth, turn, slots, idle):
+def schedule(first, second, target, targets, middle, depth, turn, slots, idle):
     count = target.shape[0]
     index = jnp.arange(count, dtype=jnp.int32)
     same = target[:, None] == target[None, :]
@@ -92,7 +108,7 @@
     def pick(values, rest):
         return rest + jnp.sum(jnp.where(chosen, values[None, :] - rest, 0), axis=1, dtype=jnp.int32)
 
-    ends = [jnp.sum(padded[: targets // 2]), jnp.sum(padded)]
+    ends = [jnp.sum(padded[:middle]), jnp.sum(padded)]
     turns = [(end + turn - 1) // turn for end in ends]
     return jnp.concatenate([pick(first, idle), pick(second, 0), pick(target, 0)]), turns
 
@@ -131,62 +147,35 @@
         send[hop - 1] = total[pl.ds(first, count), theirs, :].astype(jnp.bfloat16)
 
 
-def first_kernel(
-    left_count,
-    slots,
-    share,
-    near,
-    left,
-    right,
-    side,
-    wave,
-    here,
-    there,
-    keep,
-    send,
-    inter,
-    env_right,
-    rest,
-    env_left,
-    acc,
-    total,
-    sems,
-):
+def join(near, pieces, row, out, sems):
+    copies = []
+    for place, piece in enumerate(pieces):
+        span = pl.ds(place * piece.shape[0], piece.shape[0])
+        if near:
+            out[span] = piece[:, row]
+        else:
+            copies.append(pltpu.make_async_copy(piece.at[:, row], out.at[span], sems.at[place]))
+    for copy in copies:
+        copy.start()
+    for copy in copies:
+        copy.wait()
+
+
+def left_kernel(count, near, left, side, wave, here, there, inter, env, acc, sems):
     inters, rows, dim = acc.shape
-    mine, block, middle = side[0], side[1], side[2]
-    own = here.shape[1]
-    row = pl.ds(0 if rows == dim else pl.multiple_of(block * rows, rows), rows)
+    first_row = 0 if rows == dim else pl.multiple_of(side[1] * rows, rows)
     acc[...] = jnp.zeros_like(acc)
-    total[...] = jnp.zeros_like(total)
-    copies = []
-    for place, source in enumerate((here, there)):
-        span = pl.ds(place * own, own)
-        if near:
-            env_left[span] = source[0, :, row]
-            env_right[span] = source[1]
-            continue
-        copies.append(
-            pltpu.make_async_copy(source.at[0, :, row], env_left.at[span], sems.at[2 * place])
-        )
-        copies.append(
-            pltpu.make_async_copy(source.at[1], env_right.at[span], sems.at[2 * place + 1])
-        )
-    for copy in copies:
-        copy.start()
-    for copy in copies:
-        copy.wait()
-
-    @pl.loop(0, left_count // LEFT_UNROLL)
+    join(near, (here, there), pl.ds(first_row, rows), env, sems)
+
+    @pl.loop(0, count // LEFT_UNROLL)
     def _(turn):
         done = []
         for step in range(LEFT_UNROLL):
             at = turn * LEFT_UNROLL + step
             product = jnp.dot(
-                env_left[left[at]],
-                wave[left[left_count + at]],
-                preferred_element_type=jnp.float32,
+                env[left[at]], wave[left[count + at]], preferred_element_type=jnp.float32
             )
-            done.append((left[2 * left_count + at], product))
+            done.append((left[2 * count + at], product))
         for place, product in done:
             acc[place] += product
 
@@ -196,17 +185,25 @@
             inter[turn * 8 + step] = acc[turn * 8 + step].astype(jnp.bfloat16)
 
     inter[inters] = jnp.zeros((rows, dim), jnp.bfloat16)
-    right_products(right, slots, 0, middle, inter, env_right, total)
-    half = total.shape[0] // 2
-    give(total, 0, half, mine, share, keep, send)
-    rest[...] = total[half:]
+
+
+def first_kernel(
+    slots, share, near, right, side, inter, here, there, keep, send, env, rest, total, sems
+):
+    total[...] = jnp.zeros_like(total)
+    join(near, (here, there), pl.ds(0, here.shape[1]), env, sems)
+    right_products(right, slots, 0, side[2], inter, env, total)
+    middle = keep.shape[0]
+    give(total, 0, middle, side[0], share, keep, send)
+    rest[...] = total[middle:]
 
 
 def second_kernel(slots, share, right, side, inter, env, rest, keep, send, total):
-    half = rest.shape[0]
-    total[half:] = rest[...]
+    count = rest.shape[0]
+    middle = total.shape[0] - count
+    total[middle:] = rest[...]
     right_products(right, slots, side[2], side[3], inter, env, total)
-    give(total, half, half, side[0], share, keep, send)
+    give(total, middle, count, side[0], share, keep, send)
 
 
 def finish_kernel(vectors, first, keep, *rest):
@@ -278,7 +275,7 @@
     )(send_list, wave_tiles, left_env, right_env)
     column = gather_far(env)
     received = lax.all_to_all(outgoing, "sector", split_axis=0, concat_axis=0, tiled=True)
-    here, there = gather_env(column)
+    sides = gather_env(column)
 
     left_count, right_count = left_tasks.shape[2], right_tasks.shape[2]
     tasks = pl.pallas_call(
@@ -288,7 +285,7 @@
         out_specs=vmem,
         compiler_params=vmem_params(0),
         name="tasks",
-    )(left_tasks[0, 0].T, right_tasks[0, 0].T, column)[None]
+    )(left_tasks[0, 0].T, right_tasks[0, 0].T, column[0])[None]
     bit = 1
     while bit < terms:
         tasks = jnp.concatenate([tasks, swap(tasks, "term", bit)], axis=0)
@@ -304,6 +301,7 @@
         ]
     )
     turn = DEPTH * RIGHT_UNROLL
+    middle = tiles * 3 // 4
     slots = round_up(right_count + tiles * (DEPTH - 1), turn)
     inters = terms * INTER_TILES
     right, turns = schedule(
@@ -311,48 +309,66 @@
         env_place(groups, right_rows[:, 1]).reshape(-1),
         right_rows[:, 2].reshape(-1),
         tiles,
+        middle,
         DEPTH,
         turn,
         slots,
         inters,
     )
     side = jnp.stack([vector, block] + turns).astype(jnp.int32)
-    half = tiles // 2
     block_bytes = rows * dim * 2
-    env_bytes = here.size * 2
-    near = env_bytes <= 4 << 20
-    rest_bytes = (tiles * 6 + inters) * block_bytes + env_bytes
-    first_bytes = rest_bytes + (inters * 2 + here.shape[1] * 2) * block_bytes
-    first_bytes += send_slots * tile_bytes + (2 * env_bytes if near else 0)
-    keep_shape = jax.ShapeDtypeStruct((half, share, dim), jnp.float32)
-    send_shape = jax.ShapeDtypeStruct((vectors - 1, half, share, dim), jnp.bfloat16)
-    keep_one, send_one, inter, env_right, rest = pl.pallas_call(
-        functools.partial(first_kernel, left_count, slots, share, near),
-        out_shape=(
-            keep_shape,
-            send_shape,
-            jax.ShapeDtypeStruct((inters + 1, rows, dim), jnp.bfloat16),
-            jax.ShapeDtypeStruct((2 * here.shape[1], dim, dim), jnp.bfloat16),
-            jax.ShapeDtypeStruct((tiles - half, rows, dim), jnp.float32),
+    env_tiles = terms * sectors
+    env_bytes = env_tiles * tile_bytes
+    near = env_bytes <= 2 << 20
+    env_spec = vmem if near else hbm
+    left_bytes = send_slots * tile_bytes + (3 * inters + env_tiles) * block_bytes
+    right_bytes = (tiles * 6 + inters) * block_bytes + env_bytes
+    inter = pl.pallas_call(
+        functools.partial(left_kernel, left_count, near),
+        out_shape=jax.ShapeDtypeStruct((inters + 1, rows, dim), jnp.bfloat16),
+        in_specs=[smem, smem, vmem, env_spec, env_spec],
+        out_specs=vmem,
+        scratch_shapes=[
+            pltpu.VMEM((env_tiles, rows, dim), jnp.bfloat16),
+            pltpu.VMEM((inters, rows, dim), jnp.float32),
+            pltpu.SemaphoreType.DMA((2,)),
+        ],
+        compiler_params=vmem_params(left_bytes + near * env_bytes),
+        cost_estimate=pl.CostEstimate(
+            flops=2 * left_count * rows * dim * dim, bytes_accessed=8 << 20, transcendentals=0
         ),
-        in_specs=[smem, smem, smem, vmem] + [vmem if near else hbm] * 2,
-        out_specs=(vmem, vmem, vmem, vmem, vmem),
+        name="left_products",
+    )(left, side, received, *sides[0])
+
+    def sigma_shapes(count):
+        return (
+            jax.ShapeDtypeStruct((count, share, dim), jnp.float32),
+            jax.ShapeDtypeStruct((vectors - 1, count, share, dim), jnp.bfloat16),
+        )
+
+    keep_one, send_one, env_right, rest = pl.pallas_call(
+        functools.partial(first_kernel, slots, share, near),
+        out_shape=sigma_shapes(middle)
+        + (
+            jax.ShapeDtypeStruct((env_tiles, dim, dim), jnp.bfloat16),
+            jax.ShapeDtypeStruct((tiles - middle, rows, dim), jnp.float32),
+        ),
+        in_specs=[smem, smem, vmem, env_spec, env_spec],
+        out_specs=(vmem, vmem, vmem, vmem),
         scratch_shapes=[
-            pltpu.VMEM((2 * here.shape[1], rows, dim), jnp.bfloat16),
-            pltpu.VMEM((inters, rows, dim), jnp.float32),
             pltpu.VMEM((tiles, rows, dim), jnp.float32),
-            pltpu.SemaphoreType.DMA((4,)),
+            pltpu.SemaphoreType.DMA((2,)),
         ],
-        compiler_params=vmem_params(first_bytes),
+        compiler_params=vmem_params(right_bytes + near * env_bytes),
         name="first_products",
-    )(left, right, side, received, here, there)
+    )(right, side, inter, *sides[1])
     keep_two, send_two = pl.pallas_call(
         functools.partial(second_kernel, slots, share),
-        out_shape=(keep_shape, send_shape),
+        out_shape=sigma_shapes(tiles - middle),
         in_specs=[smem, smem, vmem, vmem, vmem],
         out_specs=(vmem, vmem),
         scratch_shapes=[pltpu.VMEM((tiles, rows, dim), jnp.float32)],
-        compiler_params=vmem_params(rest_bytes),
+        compiler_params=vmem_params(right_bytes),
         cost_estimate=pl.CostEstimate(
             flops=right_count * rows * dim * dim, bytes_accessed=12 << 20, transcendentals=0
         ),
@@ -369,7 +385,7 @@
         return moved
 
     result = finish(keep_one, exchange(send_one), tiles, 0)
-    return finish(keep_two, exchange(send_two), tiles, half, result)
+    return finish(keep_two, exchange(send_two), tiles, middle, result)
 
 
 def solution(mesh):

time: 59.8 us -> 58.2 us (0.973); the launches traced: 59.6 us -> 57.3 us
  waiting for transfers between devices: 16.7 us -> 12.6 us
  starting transfers between devices: 21.3 us -> 22.8 us
    ppermute x9 -> x12, waiting for transfers between devices: 12.9 us -> 8.69 us  [swap(): return lax.ppermute(value, axis, [(i, i ^ mask) for i in range(size)])]
    pallas_call x1 -> x3, Pallas kernels: 7.19 us -> 9.86 us  [the longest x1 5.84 us: shards(): pl.pallas_call(functools.partial(first_kernel, slots, share, near), out_s...]
    pallas_call x1, Pallas kernels: 4.29 us -> 2.12 us  [shards(): pl.pallas_call(functools.partial(second_kernel, slots, share), out_shape=...]
    ppermute x9 -> x12, starting transfers between devices: 13.1 us -> 14.5 us  [swap(): return lax.ppermute(value, axis, [(i, i ^ mask) for i in range(size)])]
  transfers between devices with their start and end apart: 12 -> 15, of which waited for: 6 -> 8; matrix products, arithmetic and copies ran while one was open for 6% -> 6% of each run, Pallas kernels for 9% -> 12%
where the time goes in v4:
time: 58.2 us; the launch traced here: 57.3 us
  starting transfers between devices  22.8 us (39%)
  Pallas kernels  16.7 us (29%)
  waiting for transfers between devices  12.6 us (22%)
  other arithmetic  2.68 us (5%)
  between operations  1.55 us (3%)
  local copies, waits for them, and re-layouts  1.01 us (2%)
    ppermute x12, starting transfers between devices, swap(): return lax.ppermute(value, axis, [(i, i ^ mask) for i in range(size)])  14.5 us
    ppermute x12, waiting for transfers between devices, swap(): return lax.ppermute(value, axis, [(i, i ^ mask) for i in range(size)])  8.69 us
    all_to_all x1, starting transfers between devices, shards(): lax.all_to_all(outgoing, 'sector', split_axis=0, concat_axis=0, tiled=True)  6.16 us
    pallas_call x1, Pallas kernels, shards(): pl.pallas_call(functools.partial(first_kernel, slots, share, near), out_s...  5.84 us
    pallas_call x1, Pallas kernels, shards(): pl.pallas_call(functools.partial(left_kernel, left_count, near), out_shap...  4 us
    ppermute x2, waiting for transfers between devices, exchange(): moved.append(lax.ppermute(send[hop - 1], 'term', pairs))  3.63 us
    pallas_call x1, Pallas kernels, shards(): pl.pallas_call(functools.partial(pack_kernel, vectors), out_shape=(jax.Sh...  3.02 us
    ppermute x2, starting transfers between devices, exchange(): moved.append(lax.ppermute(send[hop - 1], 'term', pairs))  2.16 us
  transfers between devices with their start and end apart: 15, of which 8 were waited for; matrix products, arithmetic and copies ran while one was open for 6% of the time, Pallas kernels for 12%

profile of v4, /device:TPU:0, one launch (start us, length us, event | category | flops | bytes accessed | tf_op | source)
XLA Modules:
  0.0 57.3 jit_solution(14063017367053352368)
XLA Ops:
  0.0 3.0 %pack.1 = (bf16[32,128,128]{2,1,0:T(8,128)(2,1)}, bf16[2,128,128]{2,1,0:T(8,128)(2,1)}) custom-call(s32[1,32]{1,0:T(1,128)} %picks.1, bf16[16,2,128,128]{3,2,1,0:T(8,128)(2,1)} %wave.1, bf16[1,1,128,128]{3,2,1,0:T(8,128)(2,1)} %left.1, bf16[1,1,128,128]{3,2,1,0:T(8,128)(2,1)} %right.1), custom_call_target="tpu_custom_call" | custom-call | tf_op jit(solution)/shard_map/pack/pallas_call | solution.py:261
  3.0 0.0 copy-start.1
  3.0 0.0 copy-start.2
  3.1 0.0 copy-start
  3.1 3.1 %collective-permute-start = (bf16[2,128,128]{2,1,0:T(8,128)(2,1)}, bf16[2,128,128]{2,1,0:T(8,128)(2,1)S(1)}, u32[]{:S(2)}, u32[]{:S(2)}) collective-permute-start(bf16[2,128,128]{2,1,0:T(8,128)(2,1)} %get-tuple-element.15.refs_0_), channel_id=1, source_target_pairs={{0,4},{1,5},{2,6},{3,7},{4,0},{5,1},{6,2},{7,3},{8,12},{9,13},{10,... | collective-permute-start | bytes 196616 | tf_op jit(solution)/shard_map/ppermute | solution.py:27
  6.2 2.6 %collective-permute-start.1 = (bf16[2,128,128]{2,1,0:T(8,128)(2,1)}, bf16[2,128,128]{2,1,0:T(8,128)(2,1)S(1)}, u32[]{:S(2)}, u32[]{:S(2)}) collective-permute-start(bf16[2,128,128]{2,1,0:T(8,128)(2,1)} %get-tuple-element.15.refs_0_), channel_id=1, source_target_pairs={{0,8},{1,9},{2,10},{3,11},{4,12},{5,13},{6,14},{7,15},{8,0},{9,1},... | collective-permute-start | bytes 196616 | tf_op jit(solution)/shard_map/ppermute | solution.py:27
  8.7 0.0 collective-permute-start.2
  8.7 6.2 %all-to-all-start = ((bf16[32,128,128]{2,1,0:T(8,128)(2,1)}), bf16[32,128,128]{2,1,0:T(8,128)(2,1)S(1)}, u32[]{:S(2)}, u32[]{:S(2)}) async-start(bf16[32,128,128]{2,1,0:T(8,128)(2,1)} %get-tuple-element.17), calls=%async_computation | async-start | bytes 2097152 | tf_op jit(solution)/shard_map/all_to_all | solution.py:277
  14.9 0.1 broadcast_bitcast_fusion
  15.0 0.1 broadcast_bitcast_fusion.1
  15.1 0.0 copy-done.1
  15.1 0.0 copy-done.2
  15.1 0.1 add.135
  15.1 0.1 add.136
  15.2 0.1 add.140
  15.3 0.1 add.141
  15.4 0.0 collective-permute-done.refs_1_
  15.4 0.0 collective-permute-done.1.refs_2_
  15.4 0.0 collective-permute-done.2.refs_3_
  15.4 0.0 copy-done
  15.5 2.0 %collective-permute-start.4 = (bf16[4,128,128]{2,1,0:T(8,128)(2,1)S(1)}, bf16[4,128,128]{2,1,0:T(8,128)(2,1)S(1)}, u32[]{:S(2)}, u32[]{:S(2)}) collective-permute-start(bf16[4,128,128]{2,1,0:T(8,128)(2,1)S(1)} %get-tuple-element.16.after), channel_id=1, source_target_pairs={{0,2},{1,3},{2,0},{3,1},{4,6},{5,7},{6,4},{7,5},{8,10},{9,11},{10,... | collective-permute-start | bytes 393224 | tf_op jit(solution)/shard_map/ppermute | solution.py:27
  17.4 1.5 %collective-permute-start.5 = (bf16[4,128,128]{2,1,0:T(8,128)(2,1)S(1)}, bf16[4,128,128]{2,1,0:T(8,128)(2,1)S(1)}, u32[]{:S(2)}, u32[]{:S(2)}) collective-permute-start(bf16[4,128,128]{2,1,0:T(8,128)(2,1)S(1)} %get-tuple-element.16.after), channel_id=1, source_target_pairs={{0,16},{16,0},{1,17},{17,1},{2,18},{18,2},{3,19},{19,3},{4,20},{20... | collective-permute-start | bytes 393224 | tf_op jit(solution)/shard_map/ppermute | solution.py:27
  18.9 0.5 collective-permute-start.3
  19.5 0.2 collective-permute-start.8
  19.7 1.5 %collective-permute-start.9 = (bf16[4,128,128]{2,1,0:T(8,128)(2,1)S(1)}, bf16[4,128,128]{2,1,0:T(8,128)(2,1)S(1)}, u32[]{:S(2)}, u32[]{:S(2)}) collective-permute-start(bf16[4,128,128]{2,1,0:T(8,128)(2,1)S(1)} %get-tuple-element.18), channel_id=1, source_target_pairs={{0,16},{16,0},{1,17},{17,1},{2,18},{18,2},{3,19},{19,3},{4,20},{20... | collective-permute-start | bytes 393224 | tf_op jit(solution)/shard_map/ppermute | solution.py:27
  21.2 2.8 %collective-permute-done.3 = s32[1,8,256]{2,1,0:T(8,128)S(1)} collective-permute-done((s32[1,8,256]{2,1,0:T(8,128)S(1)}, s32[1,8,256]{2,1,0:T(8,128)S(1)}, u32[]{:S(2)}, u32[]{:S(2)}) %collective-permute-start.3) | collective-permute-done | bytes 8224 | tf_op jit(solution)/shard_map/ppermute | solution.py:27
  24.0 0.1 convert_reduce_fusion.1
  24.1 0.3 convert_reduce_fusion
  24.4 0.1 and.76
  24.5 0.1 mul.77
  24.6 0.1 shift_right_arithmetic.42
  24.7 0.1 squeeze.23
  24.8 0.1 reshape_squeeze.3
  24.8 0.7 %fusion.4 = (s32[]{:T(128)}, s32[16]{0:T(128)S(1)}) fusion(s32[16]{0:T(128)S(1)} %convert_reduce_fusion.1), kind=kLoop, calls=%fused_computation.52 | loop fusion | flops 287 | bytes 132 | tf_op jit(solution)/shard_map/reduce_sum | solution.py:111
  25.6 0.1 select_reduce_fusion.3
  25.7 0.6 %select_reduce_fusion.2 = (s32[640]{0:T(1024)S(1)}, s32[640]{0:T(1024)S(1)}, s32[640]{0:T(1024)S(1)}) fusion(s32[512]{0:T(512)S(1)} %add_add_fusion.1, s32[512]{0:T(512)S(1)} %add.123, s32[512]{0:T(512)S(1)} %bitcast.38, s32[512]{0:T(512)S(1)} %add_add_fusion), kind=kLoop, calls=%fused_computation.2 | loop fusion | flops 2291840 | bytes 15872 | tf_op jit(solution)/shard_map/reduce_sum | solution.py:109
  26.3 0.1 pad_add_fusion.1.left
  26.4 0.6 %slice_reduce_fusion = s32[]{:T(128)} fusion(s32[16]{0:T(128)S(1)} %get-tuple-element.34), kind=kLoop, calls=%fused_computation.47 | loop fusion | flops 11 | bytes 52 | tf_op jit(solution)/shard_map/reduce_sum | solution.py:111
  28.3 1.3 %collective-permute-done.4 = bf16[4,128,128]{2,1,0:T(8,128)(2,1)S(1)} collective-permute-done((bf16[4,128,128]{2,1,0:T(8,128)(2,1)S(1)}, bf16[4,128,128]{2,1,0:T(8,128)(2,1)S(1)}, u32[]{:S(2)}, u32[]{:S(2)}) %collective-permute-start.4) | collective-permute-done | bytes 131104 | tf_op jit(solution)/shard_map/ppermute | solution.py:27
  29.6 1.5 %collective-permute-start.6 = (bf16[4,128,128]{2,1,0:T(8,128)(2,1)S(1)}, bf16[4,128,128]{2,1,0:T(8,128)(2,1)S(1)}, u32[]{:S(2)}, u32[]{:S(2)}) collective-permute-start(bf16[4,128,128]{2,1,0:T(8,128)(2,1)S(1)} %collective-permute-done.4), channel_id=1, source_target_pairs={{0,16},{16,0},{1,17},{17,1},{2,18},{18,2},{3,19},{19,3},{4,20},{20... | collective-permute-start | bytes 393224 | tf_op jit(solution)/shard_map/ppermute | solution.py:27
  31.1 1.0 %collective-permute-done.8 = bf16[4,128,128]{2,1,0:T(8,128)(2,1)S(1)} collective-permute-done((bf16[4,128,128]{2,1,0:T(8,128)(2,1)S(1)}, bf16[4,128,128]{2,1,0:T(8,128)(2,1)S(1)}, u32[]{:S(2)}, u32[]{:S(2)}) %collective-permute-start.8) | collective-permute-done | bytes 131104 | tf_op jit(solution)/shard_map/ppermute | solution.py:27
  32.1 1.5 %collective-permute-start.10 = (bf16[4,128,128]{2,1,0:T(8,128)(2,1)S(1)}, bf16[4,128,128]{2,1,0:T(8,128)(2,1)S(1)}, u32[]{:S(2)}, u32[]{:S(2)}) collective-permute-start(bf16[4,128,128]{2,1,0:T(8,128)(2,1)S(1)} %collective-permute-done.8), channel_id=1, source_target_pairs={{0,16},{16,0},{1,17},{17,1},{2,18},{18,2},{3,19},{19,3},{4,20},{20... | collective-permute-start | bytes 393224 | tf_op jit(solution)/shard_map/ppermute | solution.py:27
  33.6 0.0 collective-permute-done.5
  33.6 0.0 collective-permute-done.9
  33.7 1.1 %collective-permute-done.6 = bf16[4,128,128]{2,1,0:T(8,128)(2,1)S(1)} collective-permute-done((bf16[4,128,128]{2,1,0:T(8,128)(2,1)S(1)}, bf16[4,128,128]{2,1,0:T(8,128)(2,1)S(1)}, u32[]{:S(2)}, u32[]{:S(2)}) %collective-permute-start.6) | collective-permute-done | bytes 131104 | tf_op jit(solution)/shard_map/ppermute | solution.py:27
  34.8 0.1 collective-permute-start.7
  34.9 2.5 %collective-permute-done.10 = bf16[4,128,128]{2,1,0:T(8,128)(2,1)S(1)} collective-permute-done((bf16[4,128,128]{2,1,0:T(8,128)(2,1)S(1)}, bf16[4,128,128]{2,1,0:T(8,128)(2,1)S(1)}, u32[]{:S(2)}, u32[]{:S(2)}) %collective-permute-start.10) | collective-permute-done | bytes 131104 | tf_op jit(solution)/shard_map/ppermute | solution.py:27
  37.4 0.1 collective-permute-start.11
  37.5 0.1 pad_add_fusion.5.side
  37.5 0.0 collective-permute-done.7.there
  37.6 0.3 all-to-all-done.wave
  37.9 4.0 %left_products.1.inter = bf16[65,128,128]{2,1,0:T(8,128)(2,1)S(1)} custom-call(s32[576]{0:T(1024)S(1)} %pad_add_fusion.1.left, s32[4]{0:T(128)S(1)} %pad_add_fusion.5.side, bf16[32,128,128]{2,1,0:T(8,128)(2,1)S(1)} %all-to-all-done.wave, bf16[16,128,128]{2,1,0:T(8,128)(2,1)S(1)} %constant_dynamic-update-slice_fusion.here, ...), custom_call_target="tpu_custom_call" | custom-call | flops 805306368 | bytes 8388608 | tf_op jit(solution)/shard_map/left_products/pallas_call | solution.py:326
  41.9 0.0 collective-permute-done.11.there
  41.9 5.8 %first_products.1 = (f32[12,64,128]{2,1,0:T(8,128)S(1)}, bf16[1,12,64,128]{3,2,1,0:T(8,128)(2,1)S(1)}, bf16[32,128,128]{2,1,0:T(8,128)(2,1)S(1)}, f32[4,128,128]{2,1,0:T(8,128)S(1)}) custom-call(s32[1920]{0:T(1024)S(1)} %pad_add_fusion.right, s32[4]{0:T(128)S(1)} %pad_add_fusion.5.side, bf16[65,128,128]{2,1,0:T(8,128)(2,1)S(1)} %left_products.1.inter, ...), custom_call_target="tpu_custom_call" | custom-call | tf_op jit(solution)/shard_map/first_products/pallas_call | solution.py:349
  47.7 1.6 %collective-permute-start.13 = (bf16[12,64,128]{2,1,0:T(8,128)(2,1)S(1)}, bf16[12,64,128]{2,1,0:T(8,128)(2,1)S(1)}, u32[]{:S(2)}, u32[]{:S(2)}) collective-permute-start(bf16[12,64,128]{2,1,0:T(8,128)(2,1)S(1)} %bitcast.33), channel_id=1, source_target_pairs={{0,16},{16,0},{1,17},{17,1},{2,18},{18,2},{3,19},{19,3},{4,20},{20... | collective-permute-start | bytes 589832 | tf_op jit(solution)/shard_map/ppermute | solution.py:384
  49.3 2.1 %second_products.1 = (f32[4,64,128]{2,1,0:T(8,128)S(1)}, bf16[1,4,64,128]{3,2,1,0:T(8,128)(2,1)S(1)}) custom-call(s32[1920]{0:T(1024)S(1)} %pad_add_fusion.right, s32[4]{0:T(128)S(1)} %pad_add_fusion.5.side, bf16[65,128,128]{2,1,0:T(8,128)(2,1)S(1)} %left_products.1.inter, bf16[32,128,128]{2,1,0:T(8,128)(2,1)S(1)} %get-tuple-element.19.env, ...), custom_call_target="tpu_custom_call" | custom-call | flops 1073741824 | bytes 12582912 | tf_op jit(solution)/shard_map/second_products/pallas_call | solution.py:365
  51.4 0.6 %collective-permute-start.12 = (bf16[4,64,128]{2,1,0:T(8,128)(2,1)S(1)}, bf16[4,64,128]{2,1,0:T(8,128)(2,1)S(1)}, u32[]{:S(2)}, u32[]{:S(2)}) collective-permute-start(bf16[4,64,128]{2,1,0:T(8,128)(2,1)S(1)} %bitcast.34), channel_id=1, source_target_pairs={{0,16},{16,0},{1,17},{17,1},{2,18},{18,2},{3,19},{19,3},{4,20},{20... | collective-permute-start | bytes 196616 | tf_op jit(solution)/shard_map/ppermute | solution.py:384
  52.0 3.5 %collective-permute-done.13.rest_0_ = bf16[12,64,128]{2,1,0:T(8,128)(2,1)S(1)} collective-permute-done((bf16[12,64,128]{2,1,0:T(8,128)(2,1)S(1)}, bf16[12,64,128]{2,1,0:T(8,128)(2,1)S(1)}, u32[]{:S(2)}, u32[]{:S(2)}) %collective-permute-start.13) | collective-permute-done | bytes 196640 | tf_op jit(solution)/shard_map/ppermute | solution.py:384
  55.5 1.0 %finish.2.rest_1_ = f32[16,2,64,128]{3,2,1,0:T(8,128)} custom-call(f32[12,64,128]{2,1,0:T(8,128)S(1)} %get-tuple-element.23.keep, bf16[12,64,128]{2,1,0:T(8,128)(2,1)S(1)} %collective-permute-done.13.rest_0_), custom_call_target="tpu_custom_call" | custom-call | tf_op jit(solution)/shard_map/finish/pallas_call | solution.py:233
  56.4 0.2 collective-permute-done.12.rest_0_
  56.6 0.7 %finish.3 = f32[16,2,64,128]{3,2,1,0:T(8,128)} custom-call(f32[4,64,128]{2,1,0:T(8,128)S(1)} %get-tuple-element.21.keep, bf16[4,64,128]{2,1,0:T(8,128)(2,1)S(1)} %collective-permute-done.12.rest_0_, f32[16,2,64,128]{3,2,1,0:T(8,128)} %finish.2.rest_1_), custom_call_target="tpu_custom_call", output_to_operand_aliasing={{}: (2, {})} | custom-call | tf_op jit(solution)/shard_map/finish/pallas_call | solution.py:233
  (25 shorter events, 0.3 us)
Async XLA Ops:
  3.0 12.0 %copy-start.1 = (s32[1,1,256,3]{2,1,3,0:T(1,128)S(1)}, s32[1,1,256,3]{2,1,3,0:T(1,128)}, u32[]{:S(2)}) copy-start(s32[1,1,256,3]{2,1,3,0:T(1,128)} %param.11) | copy-start | bytes 9220
  3.0 12.0 %copy-start.2 = (s32[1,1,96,3]{2,1,3,0:T(1,128)S(1)}, s32[1,1,96,3]{2,1,3,0:T(1,128)}, u32[]{:S(2)}) copy-start(s32[1,1,96,3]{2,1,3,0:T(1,128)} %param.10) | copy-start | bytes 3460
  3.1 12.4 %copy-start = (bf16[2,128,128]{2,1,0:T(8,128)(2,1)S(1)}, bf16[2,128,128]{2,1,0:T(8,128)(2,1)}, u32[]{:S(2)}) copy-start(bf16[2,128,128]{2,1,0:T(8,128)(2,1)} %get-tuple-element.15.refs_0_) | copy-start | bytes 196612
  3.1 12.3 %collective-permute-start = (bf16[2,128,128]{2,1,0:T(8,128)(2,1)}, bf16[2,128,128]{2,1,0:T(8,128)(2,1)S(1)}, u32[]{:S(2)}, u32[]{:S(2)}) collective-permute-start(bf16[2,128,128]{2,1,0:T(8,128)(2,1)} %get-tuple-element.15.refs_0_), channel_id=1, source_target_pairs={{0,4},{1,5},{2,6},{3,7},{4,0},{5,1},{6,2},{7,3},{8,12},{9,13},{10,... | collective-permute-start | bytes 196616 | tf_op jit(solution)/shard_map/ppermute | solution.py:27
  6.2 9.2 %collective-permute-start.1 = (bf16[2,128,128]{2,1,0:T(8,128)(2,1)}, bf16[2,128,128]{2,1,0:T(8,128)(2,1)S(1)}, u32[]{:S(2)}, u32[]{:S(2)}) collective-permute-start(bf16[2,128,128]{2,1,0:T(8,128)(2,1)} %get-tuple-element.15.refs_0_), channel_id=1, source_target_pairs={{0,8},{1,9},{2,10},{3,11},{4,12},{5,13},{6,14},{7,15},{8,0},{9,1},... | collective-permute-start | bytes 196616 | tf_op jit(solution)/shard_map/ppermute | solution.py:27
  8.7 6.7 %collective-permute-start.2 = (bf16[2,128,128]{2,1,0:T(8,128)(2,1)}, bf16[2,128,128]{2,1,0:T(8,128)(2,1)S(1)}, u32[]{:S(2)}, u32[]{:S(2)}) collective-permute-start(bf16[2,128,128]{2,1,0:T(8,128)(2,1)} %get-tuple-element.15.refs_0_), channel_id=1, source_target_pairs={{0,12},{1,13},{2,14},{3,15},{4,8},{5,9},{6,10},{7,11},{8,4},{9,5},... | collective-permute-start | bytes 196616 | tf_op jit(solution)/shard_map/ppermute | solution.py:27
  8.7 29.1 %all-to-all-start = ((bf16[32,128,128]{2,1,0:T(8,128)(2,1)}), bf16[32,128,128]{2,1,0:T(8,128)(2,1)S(1)}, u32[]{:S(2)}, u32[]{:S(2)}) async-start(bf16[32,128,128]{2,1,0:T(8,128)(2,1)} %get-tuple-element.17), calls=%async_computation | async-start | bytes 2097152 | tf_op jit(solution)/shard_map/all_to_all | solution.py:277
  15.5 14.1 %collective-permute-start.4 = (bf16[4,128,128]{2,1,0:T(8,128)(2,1)S(1)}, bf16[4,128,128]{2,1,0:T(8,128)(2,1)S(1)}, u32[]{:S(2)}, u32[]{:S(2)}) collective-permute-start(bf16[4,128,128]{2,1,0:T(8,128)(2,1)S(1)} %get-tuple-element.16.after), channel_id=1, source_target_pairs={{0,2},{1,3},{2,0},{3,1},{4,6},{5,7},{6,4},{7,5},{8,10},{9,11},{10,... | collective-permute-start | bytes 393224 | tf_op jit(solution)/shard_map/ppermute | solution.py:27
  17.4 16.2 %collective-permute-start.5 = (bf16[4,128,128]{2,1,0:T(8,128)(2,1)S(1)}, bf16[4,128,128]{2,1,0:T(8,128)(2,1)S(1)}, u32[]{:S(2)}, u32[]{:S(2)}) collective-permute-start(bf16[4,128,128]{2,1,0:T(8,128)(2,1)S(1)} %get-tuple-element.16.after), channel_id=1, source_target_pairs={{0,16},{16,0},{1,17},{17,1},{2,18},{18,2},{3,19},{19,3},{4,20},{20... | collective-permute-start | bytes 393224 | tf_op jit(solution)/shard_map/ppermute | solution.py:27
  18.9 5.1 %collective-permute-start.3 = (s32[1,8,256]{2,1,0:T(8,128)S(1)}, s32[1,8,256]{2,1,0:T(8,128)S(1)}, u32[]{:S(2)}, u32[]{:S(2)}) collective-permute-start(s32[1,8,256]{2,1,0:T(8,128)S(1)} %bitcast.28), channel_id=1, source_target_pairs={{0,16},{16,0},{1,17},{17,1},{2,18},{18,2},{3,19},{19,3},{4,20},{20... | collective-permute-start | bytes 24584 | tf_op jit(solution)/shard_map/ppermute | solution.py:27
  19.5 12.6 %collective-permute-start.8 = (bf16[4,128,128]{2,1,0:T(8,128)(2,1)S(1)}, bf16[4,128,128]{2,1,0:T(8,128)(2,1)S(1)}, u32[]{:S(2)}, u32[]{:S(2)}) collective-permute-start(bf16[4,128,128]{2,1,0:T(8,128)(2,1)S(1)} %get-tuple-element.18), channel_id=1, source_target_pairs={{0,2},{1,3},{2,0},{3,1},{4,6},{5,7},{6,4},{7,5},{8,10},{9,11},{10,... | collective-permute-start | bytes 393224 | tf_op jit(solution)/shard_map/ppermute | solution.py:27
  19.7 14.0 %collective-permute-start.9 = (bf16[4,128,128]{2,1,0:T(8,128)(2,1)S(1)}, bf16[4,128,128]{2,1,0:T(8,128)(2,1)S(1)}, u32[]{:S(2)}, u32[]{:S(2)}) collective-permute-start(bf16[4,128,128]{2,1,0:T(8,128)(2,1)S(1)} %get-tuple-element.18), channel_id=1, source_target_pairs={{0,16},{16,0},{1,17},{17,1},{2,18},{18,2},{3,19},{19,3},{4,20},{20... | collective-permute-start | bytes 393224 | tf_op jit(solution)/shard_map/ppermute | solution.py:27
  29.6 5.2 %collective-permute-start.6 = (bf16[4,128,128]{2,1,0:T(8,128)(2,1)S(1)}, bf16[4,128,128]{2,1,0:T(8,128)(2,1)S(1)}, u32[]{:S(2)}, u32[]{:S(2)}) collective-permute-start(bf16[4,128,128]{2,1,0:T(8,128)(2,1)S(1)} %collective-permute-done.4), channel_id=1, source_target_pairs={{0,16},{16,0},{1,17},{17,1},{2,18},{18,2},{3,19},{19,3},{4,20},{20... | collective-permute-start | bytes 393224 | tf_op jit(solution)/shard_map/ppermute | solution.py:27
  32.1 5.3 %collective-permute-start.10 = (bf16[4,128,128]{2,1,0:T(8,128)(2,1)S(1)}, bf16[4,128,128]{2,1,0:T(8,128)(2,1)S(1)}, u32[]{:S(2)}, u32[]{:S(2)}) collective-permute-start(bf16[4,128,128]{2,1,0:T(8,128)(2,1)S(1)} %collective-permute-done.8), channel_id=1, source_target_pairs={{0,16},{16,0},{1,17},{17,1},{2,18},{18,2},{3,19},{19,3},{4,20},{20... | collective-permute-start | bytes 393224 | tf_op jit(solution)/shard_map/ppermute | solution.py:27
  34.8 2.8 %collective-permute-start.7 = (bf16[16,128,128]{2,1,0:T(8,128)(2,1)S(1)}, bf16[16,128,128]{2,1,0:T(8,128)(2,1)S(1)}, u32[]{:S(2)}, u32[]{:S(2)}) collective-permute-start(bf16[16,128,128]{2,1,0:T(8,128)(2,1)S(1)} %constant_dynamic-update-slice_fusion.here), channel_id=1, source_target_pairs={{0,1},{1,0},{2,3},{3,2},{4,5},{5,4},{6,7},{7,6},{8,9},{9,8},{10,11... | collective-permute-start | bytes 1572872 | tf_op jit(solution)/shard_map/ppermute | solution.py:27
  37.4 4.5 %collective-permute-start.11 = (bf16[16,128,128]{2,1,0:T(8,128)(2,1)S(1)}, bf16[16,128,128]{2,1,0:T(8,128)(2,1)S(1)}, u32[]{:S(2)}, u32[]{:S(2)}) collective-permute-start(bf16[16,128,128]{2,1,0:T(8,128)(2,1)S(1)} %constant_dynamic-update-slice_fusion.4.here), channel_id=1, source_target_pairs={{0,1},{1,0},{2,3},{3,2},{4,5},{5,4},{6,7},{7,6},{8,9},{9,8},{10,11... | collective-permute-start | bytes 1572872 | tf_op jit(solution)/shard_map/ppermute | solution.py:27
  47.7 7.7 %collective-permute-start.13 = (bf16[12,64,128]{2,1,0:T(8,128)(2,1)S(1)}, bf16[12,64,128]{2,1,0:T(8,128)(2,1)S(1)}, u32[]{:S(2)}, u32[]{:S(2)}) collective-permute-start(bf16[12,64,128]{2,1,0:T(8,128)(2,1)S(1)} %bitcast.33), channel_id=1, source_target_pairs={{0,16},{16,0},{1,17},{17,1},{2,18},{18,2},{3,19},{19,3},{4,20},{20... | collective-permute-start | bytes 589832 | tf_op jit(solution)/shard_map/ppermute | solution.py:384
  51.4 5.2 %collective-permute-start.12 = (bf16[4,64,128]{2,1,0:T(8,128)(2,1)S(1)}, bf16[4,64,128]{2,1,0:T(8,128)(2,1)S(1)}, u32[]{:S(2)}, u32[]{:S(2)}) collective-permute-start(bf16[4,64,128]{2,1,0:T(8,128)(2,1)S(1)} %bitcast.34), channel_id=1, source_target_pairs={{0,16},{16,0},{1,17},{17,1},{2,18},{18,2},{3,19},{19,3},{4,20},{20... | collective-permute-start | bytes 196616 | tf_op jit(solution)/shard_map/ppermute | solution.py:384

commit v5 on v4

v5 whole, which is shorter than its diff:
```python
import functools

import jax
import jax.numpy as jnp
from jax import lax
from jax.experimental import pallas as pl
from jax.experimental.pallas import tpu as pltpu
from jax.sharding import PartitionSpec as P

INTER_TILES = 32
PACK_UNROLL = 8
DEPTH = 8
LEFT_UNROLL = 32
RIGHT_UNROLL = 8


def vmem_params(size):
    return pltpu.CompilerParams(vmem_limit_bytes=min(size + (6 << 20), 60 << 20))


def round_up(value, step):
    return -(-value // step) * step


def swap(value, axis, mask):
    size = lax.axis_size(axis)
    return lax.ppermute(value, axis, [(i, i ^ mask) for i in range(size)])


def env_place(group, tile):
    sectors, terms = lax.axis_size("sector"), lax.axis_size("term")
    group = group ^ lax.axis_index("term")
    tile = tile ^ lax.axis_index("sector")
    far = sectors // 4
    place = (tile >> 2) + far * (((tile >> 1) & 1) + 2 * group)
    return place + far * 2 * terms * (tile & 1)


def column_kernel(count, *refs):
    tiles, sides = refs[:count], refs[count:]
    for place in range(count):
        for side in range(2):
            sides[side][place] = tiles[place][side]


def gather_far(env):
    count = lax.axis_size("sector") // 4
    vmem = pl.BlockSpec(memory_space=pltpu.VMEM)
    return pl.pallas_call(
        functools.partial(column_kernel, count),
        out_shape=[jax.ShapeDtypeStruct((count,) + env.shape[1:], env.dtype)] * 2,
        in_specs=[vmem] * count,
        out_specs=[vmem] * 2,
        compiler_params=vmem_params(4 * count * env.size),
        name="column",
    )(env, *[swap(env, "sector", mask << 2) for mask in range(1, count)])


def gather_env(column):
    terms = lax.axis_size("term")
    sides = []
    for side in range(2):
        across, over = swap(column[side], "sector", 2), swap(column[side], "term", 1)
        plane = jnp.concatenate([column[side], across, over, swap(across, "term", 1)])
        bit = 2
        while bit < terms:
            plane = jnp.concatenate([plane, swap(plane, "term", bit)])
            bit *= 2
        sides.append((plane, swap(plane, "sector", 1)))
    return sides


def pack_kernel(vectors, listed, wave, left, right, out, env, held, picks, sems):
    vector = lax.rem(lax.axis_index("term"), vectors)
    copies = [
        pltpu.make_async_copy(wave.at[:, vector], held, sems.at[0]),
        pltpu.make_async_copy(left.at[0, 0], env.at[0], sems.at[1]),
        pltpu.make_async_copy(right.at[0, 0], env.at[1], sems.at[2]),
        pltpu.make_async_copy(listed, picks, sems.at[3]),
    ]
    for copy in copies:
        copy.start()
    copies[0].wait()
    copies[3].wait()

    @pl.loop(0, out.shape[0] // PACK_UNROLL)
    def _(turn):
        for step in range(PACK_UNROLL):
            slot = turn * PACK_UNROLL + step
            tile = picks[0, slot]
            picked = held[jnp.maximum(tile, 0)]
            out[slot] = jnp.where(tile >= 0, picked, jnp.zeros_like(picked))

    copies[1].wait()
    copies[2].wait()


def schedule(first, second, target, targets, depth, turn, slots, idle):
    count = target.shape[0]
    index = jnp.arange(count, dtype=jnp.int32)
    same = target[:, None] == target[None, :]
    rank = jnp.sum(same & (index[None, :] < index[:, None]), axis=1, dtype=jnp.int32)
    names = jnp.arange(targets, dtype=jnp.int32)
    counts = jnp.sum(target[None, :] == names[:, None], axis=1, dtype=jnp.int32)
    padded = (counts + depth - 1) // depth * depth
    starts = jnp.sum(
        jnp.where(names[None, :] < target[:, None], padded[None, :], 0), axis=1, dtype=jnp.int32
    )
    place = starts + rank
    chosen = place[None, :] == jnp.arange(slots, dtype=jnp.int32)[:, None]

    def pick(values, rest):
        return rest + jnp.sum(jnp.where(chosen, values[None, :] - rest, 0), axis=1, dtype=jnp.int32)

    turns = (jnp.sum(padded) + turn - 1) // turn
    return jnp.concatenate([pick(first, idle), pick(second, 0), pick(target, 0), turns[None]])


def tasks_kernel(left, right, after, out):
    out[...] = jnp.zeros_like(out)
    out[0 : left.shape[0], 0 : left.shape[1]] = left[...]
    out[3 : 3 + right.shape[0], 0 : right.shape[1]] = right[...]


def right_products(right, slots, row, inter, env, total):
    rows = pl.ds(row, total.shape[1])

    @pl.loop(0, right[3 * slots])
    def _(turn):
        done = []
        for step in range(RIGHT_UNROLL):
            base = (turn * RIGHT_UNROLL + step) * DEPTH
            first = [inter[right[base + i], rows, :] for i in range(DEPTH)]
            second = [env[right[slots + base + i]] for i in range(DEPTH)]
            product = jnp.dot(
                jnp.concatenate(first, axis=1),
                jnp.concatenate(second, axis=0),
                preferred_element_type=jnp.float32,
            )
            done.append((right[2 * slots + base], product))
        for place, product in done:
            total[place] += product


def join(near, pieces, row, out, sems):
    copies = []
    for place, piece in enumerate(pieces):
        span = pl.ds(place * piece.shape[0], piece.shape[0])
        if near:
            out[span] = piece[:, row]
        else:
            copies.append(pltpu.make_async_copy(piece.at[:, row], out.at[span], sems.at[place]))
    for copy in copies:
        copy.start()
    for copy in copies:
        copy.wait()


def left_kernel(count, vectors, near, listed, wave, here, there, inter, env, acc, left, sems):
    inters, rows, dim = acc.shape
    lists = pltpu.make_async_copy(listed, left, sems.at[2])
    lists.start()
    first_row = 0
    if rows < dim:
        first_row = pl.multiple_of(lax.div(lax.axis_index("term"), vectors) * rows, rows)
    acc[...] = jnp.zeros_like(acc)
    join(near, (here, there), pl.ds(first_row, rows), env, sems)
    lists.wait()

    @pl.loop(0, count // LEFT_UNROLL)
    def _(turn):
        done = []
        for step in range(LEFT_UNROLL):
            at = turn * LEFT_UNROLL + step
            product = jnp.dot(
                env[left[at]], wave[left[count + at]], preferred_element_type=jnp.float32
            )
            done.append((left[2 * count + at], product))
        for place, product in done:
            acc[place] += product

    @pl.loop(0, inters // 8)
    def _(turn):
        for step in range(8):
            inter[turn * 8 + step] = acc[turn * 8 + step].astype(jnp.bfloat16)

    inter[inters] = jnp.zeros((rows, dim), jnp.bfloat16)


def theirs_kernel(slots, near, listed, inter, here, there, send, env, total, right, sems):
    lists = pltpu.make_async_copy(listed, right, sems.at[2])
    lists.start()
    join(near, (here, there), pl.ds(0, here.shape[1]), env, sems)
    total[...] = jnp.zeros_like(total)
    lists.wait()
    parts, share = send.shape[0] + 1, total.shape[1]
    vector = lax.rem(lax.axis_index("term"), parts)
    for hop in range(1, parts):
        if hop > 1:
            total[...] = jnp.zeros_like(total)
        part = lax.rem(vector + hop, parts)
        row = pl.multiple_of(part * share, share)
        right_products(right, slots, row, inter, env, total)
        send[hop - 1] = total[...].astype(jnp.bfloat16)


def own_kernel(slots, listed, inter, env, out, total, right, sems):
    lists = pltpu.make_async_copy(listed, right, sems.at[0])
    lists.start()
    total[...] = jnp.zeros_like(total)
    lists.wait()
    share = total.shape[1]
    vector = lax.rem(lax.axis_index("term"), out.shape[1])
    row = pl.multiple_of(vector * share, share)
    right_products(right, slots, row, inter, env, total)
    copy = pltpu.make_async_copy(total, out.at[:, vector], sems.at[1])
    copy.start()
    copy.wait()


def finish_kernel(vectors, *refs):
    received, (_, out, held, sems) = refs[: vectors - 1], refs[vectors - 1 :]
    vector = lax.rem(lax.axis_index("term"), vectors)
    copies = []
    for hop in range(1, vectors):
        held[hop - 1] = received[hop - 1][...].astype(jnp.float32)
        place = lax.rem(vector + vectors - hop, vectors)
        copies.append(
            pltpu.make_async_copy(held.at[hop - 1], out.at[:, place], sems.at[hop - 1])
        )
        copies[-1].start()
    for copy in copies:
        copy.wait()


def shards(wave_tiles, left_env, right_env, send_list, left_tasks, right_tasks):
    sectors, terms = lax.axis_size("sector"), lax.axis_size("term")
    tiles, vectors, dim, _ = wave_tiles.shape
    term = lax.axis_index("term")
    blocks = terms // vectors
    rows, share = dim // blocks, dim // terms
    vector, block = term % vectors, term // vectors

    vmem = pl.BlockSpec(memory_space=pltpu.VMEM)
    hbm = pl.BlockSpec(memory_space=pl.ANY)
    send_slots = send_list.shape[1]
    tile_bytes = dim * dim * 2
    outgoing, env = pl.pallas_call(
        functools.partial(pack_kernel, vectors),
        out_shape=(
            jax.ShapeDtypeStruct((send_slots, dim, dim), jnp.bfloat16),
            jax.ShapeDtypeStruct((2, dim, dim), jnp.bfloat16),
        ),
        in_specs=[hbm, hbm, hbm, hbm],
        out_specs=(vmem, vmem),
        scratch_shapes=[
            pltpu.VMEM((tiles, dim, dim), jnp.bfloat16),
            pltpu.SMEM(send_list.shape, jnp.int32),
            pltpu.SemaphoreType.DMA((4,)),
        ],
        compiler_params=vmem_params(54 << 20),
        name="pack",
    )(send_list, wave_tiles, left_env, right_env)
    column = gather_far(env)
    received = lax.all_to_all(outgoing, "sector", split_axis=0, concat_axis=0, tiled=True)
    sides = gather_env(column)

    left_count, right_count = left_tasks.shape[2], right_tasks.shape[2]
    tasks = pl.pallas_call(
        tasks_kernel,
        out_shape=jax.ShapeDtypeStruct((8, max(left_count, right_count)), jnp.int32),
        in_specs=[vmem, vmem, hbm],
        out_specs=vmem,
        compiler_params=vmem_params(0),
        name="tasks",
    )(left_tasks[0, 0].T, right_tasks[0, 0].T, column[0])[None]
    bit = 1
    while bit < terms:
        tasks = jnp.concatenate([tasks, swap(tasks, "term", bit)], axis=0)
        bit *= 2
    left_rows, right_rows = tasks[:, 0:3, :left_count], tasks[:, 3:6, :right_count]
    groups = jnp.arange(terms, dtype=jnp.int32)[:, None] ^ term
    left_count, right_count = terms * left_count, terms * right_count
    left = jnp.concatenate(
        [
            env_place(groups, left_rows[:, 0]).reshape(-1),
            left_rows[:, 1].reshape(-1),
            (groups * INTER_TILES + left_rows[:, 2]).reshape(-1),
        ]
    )
    turn = DEPTH * RIGHT_UNROLL
    slots = round_up(right_count + tiles * (DEPTH - 1), turn)
    inters = terms * INTER_TILES
    right = schedule(
        (groups * INTER_TILES + right_rows[:, 0]).reshape(-1),
        env_place(groups, right_rows[:, 1]).reshape(-1),
        right_rows[:, 2].reshape(-1),
        tiles,
        DEPTH,
        turn,
        slots,
        inters,
    )
    block_bytes = rows * dim * 2
    env_tiles = terms * sectors
    env_bytes = env_tiles * tile_bytes
    near = env_bytes <= 2 << 20
    env_spec = vmem if near else hbm
    left_bytes = send_slots * tile_bytes + (3 * inters + env_tiles) * block_bytes
    right_bytes = (tiles * 2 + inters) * block_bytes + env_bytes
    inter = pl.pallas_call(
        functools.partial(left_kernel, left_count, vectors, near),
        out_shape=jax.ShapeDtypeStruct((inters + 1, rows, dim), jnp.bfloat16),
        in_specs=[hbm, vmem, env_spec, env_spec],
        out_specs=vmem,
        scratch_shapes=[
            pltpu.VMEM((env_tiles, rows, dim), jnp.bfloat16),
            pltpu.VMEM((inters, rows, dim), jnp.float32),
            pltpu.SMEM(left.shape, jnp.int32),
            pltpu.SemaphoreType.DMA((3,)),
        ],
        compiler_params=vmem_params(left_bytes + near * env_bytes),
        cost_estimate=pl.CostEstimate(
            flops=2 * left_count * rows * dim * dim, bytes_accessed=8 << 20, transcendentals=0
        ),
        name="left_products",
    )(left, received, *sides[0])
    send, env_right = pl.pallas_call(
        functools.partial(theirs_kernel, slots, near),
        out_shape=(
            jax.ShapeDtypeStruct((vectors - 1, tiles, share, dim), jnp.bfloat16),
            jax.ShapeDtypeStruct((env_tiles, dim, dim), jnp.bfloat16),
        ),
        in_specs=[hbm, vmem, env_spec, env_spec],
        out_specs=(vmem, vmem),
        scratch_shapes=[
            pltpu.VMEM((tiles, share, dim), jnp.float32),
            pltpu.SMEM(right.shape, jnp.int32),
            pltpu.SemaphoreType.DMA((3,)),
        ],
        compiler_params=vmem_params(right_bytes + near * env_bytes),
        name="their_products",
    )(right, inter, *sides[1])
    result = pl.pallas_call(
        functools.partial(own_kernel, slots),
        out_shape=jax.ShapeDtypeStruct((tiles, vectors, share, dim), jnp.float32),
        in_specs=[hbm, vmem, vmem],
        out_specs=hbm,
        scratch_shapes=[
            pltpu.VMEM((tiles, share, dim), jnp.float32),
            pltpu.SMEM(right.shape, jnp.int32),
            pltpu.SemaphoreType.DMA((2,)),
        ],
        compiler_params=vmem_params(right_bytes),
        cost_estimate=pl.CostEstimate(
            flops=2 * right_count * share * dim * dim, bytes_accessed=12 << 20, transcendentals=0
        ),
        name="own_products",
    )(right, inter, env_right)
    moved = []
    for hop in range(1, vectors):
        pairs = [
            (i, i // vectors * vectors + (i % vectors + hop) % vectors) for i in range(terms)
        ]
        moved.append(lax.ppermute(send[hop - 1], "term", pairs))
    return pl.pallas_call(
        functools.partial(finish_kernel, vectors),
        out_shape=jax.ShapeDtypeStruct((tiles, vectors, share, dim), jnp.float32),
        in_specs=[vmem] * (vectors - 1) + [hbm],
        out_specs=hbm,
        scratch_shapes=[
            pltpu.VMEM((vectors - 1, tiles, share, dim), jnp.float32),
            pltpu.SemaphoreType.DMA((vectors - 1,)),
        ],
        compiler_params=vmem_params(2 * vectors * tiles * share * dim * 4),
        input_output_aliases={vectors - 1: 0},
        name="finish",
    )(*moved, result)


def solution(mesh):
    in_specs = (
        P("sector", None, None, None),
        P("term", "sector", None, None),
        P("term", "sector", None, None),
        P("sector", None),
        P("term", "sector", None, None),
        P("term", "sector", None, None),
    )
    out_specs = P("sector", None, "term", None)
    return jax.shard_map(shards, mesh=mesh, in_specs=in_specs, out_specs=out_specs, check_vma=False)
```

time: 58.2 us -> 57.1 us (0.981)
  Pallas kernels: 16.7 us -> 18.7 us
  waiting for transfers between devices: 12.6 us -> 11.3 us
  other arithmetic: 2.68 us -> 1.98 us
  starting transfers between devices: 22.8 us -> 22.2 us
  between operations: 1.55 us -> 0.95 us
    pallas_call x5 -> x4, Pallas kernels: 13.7 us -> 16.3 us  [the longest x1 6.27 us: shards(): pl.pallas_call(functools.partial(own_kernel, slots), out_shape=jax.ShapeD...]
    ppermute x2 -> x1, waiting for transfers between devices: 3.63 us -> 1.05 us  [shards(): moved.append(lax.ppermute(send[hop - 1], 'term', pairs))]
    ppermute x12, waiting for transfers between devices: 8.69 us -> 9.98 us  [swap(): return lax.ppermute(value, axis, [(i, i ^ mask) for i in range(size)])]
    pallas_call x1, Pallas kernels: 3.02 us -> 2.36 us  [shards(): pl.pallas_call(functools.partial(pack_kernel, vectors), out_shape=(jax.Sh...]
    reduce_sum x2 -> x1, other arithmetic: 1.34 us -> 0.72 us  [schedule(): turns = (jnp.sum(padded) + turn - 1) // turn]
    ppermute x2 -> x1, starting transfers between devices: 2.16 us -> 1.57 us  [shards(): moved.append(lax.ppermute(send[hop - 1], 'term', pairs))]
  transfers between devices with their start and end apart: 15 -> 14, of which waited for: 8 -> 7; matrix products, arithmetic and copies ran while one was open for 6% -> 5% of each run, Pallas kernels for 12% -> 18%
where the time goes in v5:
time: 57.1 us; the launch traced here: 56.1 us
  starting transfers between devices  22.2 us (39%)
  Pallas kernels  18.7 us (33%)
  waiting for transfers between devices  11.3 us (20%)
  other arithmetic  1.98 us (3%)
  local copies, waits for them, and re-layouts  1.01 us (2%)
  between operations  0.95 us (2%)
    ppermute x12, starting transfers between devices, swap(): return lax.ppermute(value, axis, [(i, i ^ mask) for i in range(size)])  14.5 us
    ppermute x12, waiting for transfers between devices, swap(): return lax.ppermute(value, axis, [(i, i ^ mask) for i in range(size)])  9.98 us
    pallas_call x1, Pallas kernels, shards(): pl.pallas_call(functools.partial(own_kernel, slots), out_shape=jax.ShapeD...  6.27 us
    all_to_all x1, starting transfers between devices, shards(): lax.all_to_all(outgoing, 'sector', split_axis=0, concat_axis=0, tiled=True)  6.16 us
    pallas_call x1, Pallas kernels, shards(): pl.pallas_call(functools.partial(theirs_kernel, slots, near), out_shape=(...  5.51 us
    pallas_call x1, Pallas kernels, shards(): pl.pallas_call(functools.partial(left_kernel, left_count, vectors, near),...  3.67 us
    pallas_call x1, Pallas kernels, shards(): pl.pallas_call(functools.partial(pack_kernel, vectors), out_shape=(jax.Sh...  2.36 us
    ppermute x1, starting transfers between devices, shards(): moved.append(lax.ppermute(send[hop - 1], 'term', pairs))  1.57 us
  transfers between devices with their start and end apart: 14, of which 7 were waited for; matrix products, arithmetic and copies ran while one was open for 5% of the time, Pallas kernels for 18%

profile of v5, /device:TPU:0, one launch (start us, length us, event | category | flops | bytes accessed | tf_op | source)
XLA Modules:
  0.0 56.1 jit_solution(10965275316213386727)
XLA Ops:
  0.0 2.4 %pack.1 = (bf16[32,128,128]{2,1,0:T(8,128)(2,1)}, bf16[2,128,128]{2,1,0:T(8,128)(2,1)}) custom-call(s32[1,32]{1,0:T(1,128)} %listed.1, bf16[16,2,128,128]{3,2,1,0:T(8,128)(2,1)} %wave.1, bf16[1,1,128,128]{3,2,1,0:T(8,128)(2,1)} %left.1, bf16[1,1,128,128]{3,2,1,0:T(8,128)(2,1)} %right.1), custom_call_target="tpu_custom_call" | custom-call | tf_op jit(solution)/shard_map/pack/pallas_call | solution.py:248
  2.4 0.0 copy-start.2
  2.4 0.0 copy-start.1
  2.4 0.0 copy-start
  2.4 3.1 %collective-permute-start = (bf16[2,128,128]{2,1,0:T(8,128)(2,1)}, bf16[2,128,128]{2,1,0:T(8,128)(2,1)S(1)}, u32[]{:S(2)}, u32[]{:S(2)}) collective-permute-start(bf16[2,128,128]{2,1,0:T(8,128)(2,1)} %get-tuple-element.11.refs_0_), channel_id=1, source_target_pairs={{0,4},{1,5},{2,6},{3,7},{4,0},{5,1},{6,2},{7,3},{8,12},{9,13},{10,... | collective-permute-start | bytes 196616 | tf_op jit(solution)/shard_map/ppermute | solution.py:27
  5.5 2.6 %collective-permute-start.1 = (bf16[2,128,128]{2,1,0:T(8,128)(2,1)}, bf16[2,128,128]{2,1,0:T(8,128)(2,1)S(1)}, u32[]{:S(2)}, u32[]{:S(2)}) collective-permute-start(bf16[2,128,128]{2,1,0:T(8,128)(2,1)} %get-tuple-element.11.refs_0_), channel_id=1, source_target_pairs={{0,8},{1,9},{2,10},{3,11},{4,12},{5,13},{6,14},{7,15},{8,0},{9,1},... | collective-permute-start | bytes 196616 | tf_op jit(solution)/shard_map/ppermute | solution.py:27
  8.1 0.0 collective-permute-start.2
  8.1 6.2 %all-to-all-start = ((bf16[32,128,128]{2,1,0:T(8,128)(2,1)}), bf16[32,128,128]{2,1,0:T(8,128)(2,1)S(1)}, u32[]{:S(2)}, u32[]{:S(2)}) async-start(bf16[32,128,128]{2,1,0:T(8,128)(2,1)} %get-tuple-element.13), calls=%async_computation | async-start | bytes 2097152 | tf_op jit(solution)/shard_map/all_to_all | solution.py:265
  14.3 0.1 broadcast_bitcast_fusion.1
  14.3 0.1 broadcast_bitcast_fusion
  14.4 0.0 copy-done.2
  14.4 0.0 copy-done.1
  14.4 0.1 add.129
  14.5 0.1 add.130
  14.6 0.1 add.124
  14.7 0.1 add.125
  14.8 0.0 collective-permute-done.refs_1_
  14.8 0.0 collective-permute-done.1.refs_2_
  14.8 0.0 collective-permute-done.2.refs_3_
  14.8 0.0 copy-done
  14.8 2.0 %collective-permute-start.4 = (bf16[4,128,128]{2,1,0:T(8,128)(2,1)S(1)}, bf16[4,128,128]{2,1,0:T(8,128)(2,1)S(1)}, u32[]{:S(2)}, u32[]{:S(2)}) collective-permute-start(bf16[4,128,128]{2,1,0:T(8,128)(2,1)S(1)} %get-tuple-element.12.after), channel_id=1, source_target_pairs={{0,2},{1,3},{2,0},{3,1},{4,6},{5,7},{6,4},{7,5},{8,10},{9,11},{10,... | collective-permute-start | bytes 393224 | tf_op jit(solution)/shard_map/ppermute | solution.py:27
  16.8 1.5 %collective-permute-start.5 = (bf16[4,128,128]{2,1,0:T(8,128)(2,1)S(1)}, bf16[4,128,128]{2,1,0:T(8,128)(2,1)S(1)}, u32[]{:S(2)}, u32[]{:S(2)}) collective-permute-start(bf16[4,128,128]{2,1,0:T(8,128)(2,1)S(1)} %get-tuple-element.12.after), channel_id=1, source_target_pairs={{0,16},{16,0},{1,17},{17,1},{2,18},{18,2},{3,19},{19,3},{4,20},{20... | collective-permute-start | bytes 393224 | tf_op jit(solution)/shard_map/ppermute | solution.py:27
  18.3 0.5 collective-permute-start.3
  18.8 0.2 collective-permute-start.8
  19.0 1.5 %collective-permute-start.9 = (bf16[4,128,128]{2,1,0:T(8,128)(2,1)S(1)}, bf16[4,128,128]{2,1,0:T(8,128)(2,1)S(1)}, u32[]{:S(2)}, u32[]{:S(2)}) collective-permute-start(bf16[4,128,128]{2,1,0:T(8,128)(2,1)S(1)} %get-tuple-element.14), channel_id=1, source_target_pairs={{0,16},{16,0},{1,17},{17,1},{2,18},{18,2},{3,19},{19,3},{4,20},{20... | collective-permute-start | bytes 393224 | tf_op jit(solution)/shard_map/ppermute | solution.py:27
  20.5 2.8 %collective-permute-done.3 = s32[1,8,256]{2,1,0:T(8,128)S(1)} collective-permute-done((s32[1,8,256]{2,1,0:T(8,128)S(1)}, s32[1,8,256]{2,1,0:T(8,128)S(1)}, u32[]{:S(2)}, u32[]{:S(2)}) %collective-permute-start.3) | collective-permute-done | bytes 8224 | tf_op jit(solution)/shard_map/ppermute | solution.py:27
  23.4 0.1 convert_reduce_fusion.1
  23.5 0.3 convert_reduce_fusion
  23.7 0.7 %fusion.4 = (s32[]{:T(128)}, s32[16]{0:T(128)S(1)}) fusion(s32[16]{0:T(128)S(1)} %convert_reduce_fusion.1), kind=kLoop, calls=%fused_computation.50 | loop fusion | flops 287 | bytes 132 | tf_op jit(solution)/shard_map/reduce_sum | solution.py:115
  24.4 0.1 select_reduce_fusion.3
  24.6 0.1 mul.77
  24.7 0.1 shift_right_arithmetic.42
  24.8 0.1 and.60
  24.9 0.6 %select_reduce_fusion.2 = (s32[640]{0:T(1024)S(1)}, s32[640]{0:T(1024)S(1)}, s32[640]{0:T(1024)S(1)}) fusion(s32[512]{0:T(512)S(1)} %add_add_fusion.1, s32[512]{0:T(512)S(1)} %add.113, s32[512]{0:T(512)S(1)} %bitcast.33, s32[512]{0:T(512)S(1)} %add_add_fusion), kind=kLoop, calls=%fused_computation.2 | loop fusion | flops 2291840 | bytes 15872 | tf_op jit(solution)/shard_map/reduce_sum | solution.py:113
  26.2 0.1 squeeze.20
  26.3 0.1 reshape_squeeze.3
  26.4 2.6 %collective-permute-done.4 = bf16[4,128,128]{2,1,0:T(8,128)(2,1)S(1)} collective-permute-done((bf16[4,128,128]{2,1,0:T(8,128)(2,1)S(1)}, bf16[4,128,128]{2,1,0:T(8,128)(2,1)S(1)}, u32[]{:S(2)}, u32[]{:S(2)}) %collective-permute-start.4) | collective-permute-done | bytes 131104 | tf_op jit(solution)/shard_map/ppermute | solution.py:27
  28.9 1.5 %collective-permute-start.6 = (bf16[4,128,128]{2,1,0:T(8,128)(2,1)S(1)}, bf16[4,128,128]{2,1,0:T(8,128)(2,1)S(1)}, u32[]{:S(2)}, u32[]{:S(2)}) collective-permute-start(bf16[4,128,128]{2,1,0:T(8,128)(2,1)S(1)} %collective-permute-done.4), channel_id=1, source_target_pairs={{0,16},{16,0},{1,17},{17,1},{2,18},{18,2},{3,19},{19,3},{4,20},{20... | collective-permute-start | bytes 393224 | tf_op jit(solution)/shard_map/ppermute | solution.py:27
  30.4 1.0 %collective-permute-done.8 = bf16[4,128,128]{2,1,0:T(8,128)(2,1)S(1)} collective-permute-done((bf16[4,128,128]{2,1,0:T(8,128)(2,1)S(1)}, bf16[4,128,128]{2,1,0:T(8,128)(2,1)S(1)}, u32[]{:S(2)}, u32[]{:S(2)}) %collective-permute-start.8) | collective-permute-done | bytes 131104 | tf_op jit(solution)/shard_map/ppermute | solution.py:27
  31.4 1.5 %collective-permute-start.10 = (bf16[4,128,128]{2,1,0:T(8,128)(2,1)S(1)}, bf16[4,128,128]{2,1,0:T(8,128)(2,1)S(1)}, u32[]{:S(2)}, u32[]{:S(2)}) collective-permute-start(bf16[4,128,128]{2,1,0:T(8,128)(2,1)S(1)} %collective-permute-done.8), channel_id=1, source_target_pairs={{0,16},{16,0},{1,17},{17,1},{2,18},{18,2},{3,19},{19,3},{4,20},{20... | collective-permute-start | bytes 393224 | tf_op jit(solution)/shard_map/ppermute | solution.py:27
  32.9 0.0 collective-permute-done.5
  33.0 0.0 collective-permute-done.9
  33.0 1.1 %collective-permute-done.6 = bf16[4,128,128]{2,1,0:T(8,128)(2,1)S(1)} collective-permute-done((bf16[4,128,128]{2,1,0:T(8,128)(2,1)S(1)}, bf16[4,128,128]{2,1,0:T(8,128)(2,1)S(1)}, u32[]{:S(2)}, u32[]{:S(2)}) %collective-permute-start.6) | collective-permute-done | bytes 131104 | tf_op jit(solution)/shard_map/ppermute | solution.py:27
  34.1 0.1 collective-permute-start.7
  34.2 2.5 %collective-permute-done.10 = bf16[4,128,128]{2,1,0:T(8,128)(2,1)S(1)} collective-permute-done((bf16[4,128,128]{2,1,0:T(8,128)(2,1)S(1)}, bf16[4,128,128]{2,1,0:T(8,128)(2,1)S(1)}, u32[]{:S(2)}, u32[]{:S(2)}) %collective-permute-start.10) | collective-permute-done | bytes 131104 | tf_op jit(solution)/shard_map/ppermute | solution.py:27
  36.7 0.1 collective-permute-start.11
  36.8 0.1 pad_add_fusion.1.listed
  36.9 0.0 collective-permute-done.7.there
  36.9 0.3 all-to-all-done.wave
  37.2 3.7 %left_products.1.inter = bf16[65,128,128]{2,1,0:T(8,128)(2,1)S(1)} custom-call(s32[576]{0:T(1024)S(1)} %pad_add_fusion.1.listed, bf16[32,128,128]{2,1,0:T(8,128)(2,1)S(1)} %all-to-all-done.wave, bf16[16,128,128]{2,1,0:T(8,128)(2,1)S(1)} %constant_dynamic-update-slice_fusion.here, bf16[16,128,128]{2,1,0:T(8,128)(2,1)S(1)} %collective-permute-done.7.there), custom_call_target="tpu_custom_call" | custom-call | flops 805306368 | bytes 8388608 | tf_op jit(solution)/shard_map/left_products/pallas_call | solution.py:311
  40.9 0.0 collective-permute-done.11.there
  40.9 5.5 %their_products.1 = (bf16[1,16,64,128]{3,2,1,0:T(8,128)(2,1)S(1)}, bf16[32,128,128]{2,1,0:T(8,128)(2,1)S(1)}) custom-call(s32[1921]{0:T(1024)S(1)} %pad_add_fusion.listed, bf16[65,128,128]{2,1,0:T(8,128)(2,1)S(1)} %left_products.1.inter, bf16[16,128,128]{2,1,0:T(8,128)(2,1)S(1)} %constant_dynamic-update-slice_fusion.4.here, ...), custom_call_target="tpu_custom_call" | custom-call | tf_op jit(solution)/shard_map/their_products/pallas_call | solution.py:328
  46.4 1.6 %collective-permute-start.12 = (bf16[16,64,128]{2,1,0:T(8,128)(2,1)S(1)}, bf16[16,64,128]{2,1,0:T(8,128)(2,1)S(1)}, u32[]{:S(2)}, u32[]{:S(2)}) collective-permute-start(bf16[16,64,128]{2,1,0:T(8,128)(2,1)S(1)} %bitcast.29), channel_id=1, source_target_pairs={{0,16},{16,0},{1,17},{17,1},{2,18},{18,2},{3,19},{19,3},{4,20},{20... | collective-permute-start | bytes 786440 | tf_op jit(solution)/shard_map/ppermute | solution.py:365
  48.0 6.3 %own_products.1.refs_1_ = f32[16,2,64,128]{3,2,1,0:T(8,128)} custom-call(s32[1921]{0:T(1024)S(1)} %pad_add_fusion.listed, bf16[65,128,128]{2,1,0:T(8,128)(2,1)S(1)} %left_products.1.inter, bf16[32,128,128]{2,1,0:T(8,128)(2,1)S(1)} %get-tuple-element.16.env), custom_call_target="tpu_custom_call" | custom-call | flops 1073741824 | bytes 12582912 | tf_op jit(solution)/shard_map/own_products/pallas_call | solution.py:344
  54.2 1.0 %collective-permute-done.12.refs_0_ = bf16[16,64,128]{2,1,0:T(8,128)(2,1)S(1)} collective-permute-done((bf16[16,64,128]{2,1,0:T(8,128)(2,1)S(1)}, bf16[16,64,128]{2,1,0:T(8,128)(2,1)S(1)}, u32[]{:S(2)}, u32[]{:S(2)}) %collective-permute-start.12) | collective-permute-done | bytes 262176 | tf_op jit(solution)/shard_map/ppermute | solution.py:365
  55.3 0.8 %finish.1 = f32[16,2,64,128]{3,2,1,0:T(8,128)} custom-call(bf16[16,64,128]{2,1,0:T(8,128)(2,1)S(1)} %collective-permute-done.12.refs_0_, f32[16,2,64,128]{3,2,1,0:T(8,128)} %own_products.1.refs_1_), custom_call_target="tpu_custom_call", output_to_operand_aliasing={{}: (1, {})} | custom-call | tf_op jit(solution)/shard_map/finish/pallas_call | solution.py:366
  (25 shorter events, 0.3 us)
Async XLA Ops:
  2.4 12.0 %copy-start.2 = (s32[1,1,96,3]{2,1,3,0:T(1,128)S(1)}, s32[1,1,96,3]{2,1,3,0:T(1,128)}, u32[]{:S(2)}) copy-start(s32[1,1,96,3]{2,1,3,0:T(1,128)} %param.10) | copy-start | bytes 3460
  2.4 12.0 %copy-start.1 = (s32[1,1,256,3]{2,1,3,0:T(1,128)S(1)}, s32[1,1,256,3]{2,1,3,0:T(1,128)}, u32[]{:S(2)}) copy-start(s32[1,1,256,3]{2,1,3,0:T(1,128)} %param.11) | copy-start | bytes 9220
  2.4 12.4 %copy-start = (bf16[2,128,128]{2,1,0:T(8,128)(2,1)S(1)}, bf16[2,128,128]{2,1,0:T(8,128)(2,1)}, u32[]{:S(2)}) copy-start(bf16[2,128,128]{2,1,0:T(8,128)(2,1)} %get-tuple-element.11.refs_0_) | copy-start | bytes 196612
  2.4 12.4 %collective-permute-start = (bf16[2,128,128]{2,1,0:T(8,128)(2,1)}, bf16[2,128,128]{2,1,0:T(8,128)(2,1)S(1)}, u32[]{:S(2)}, u32[]{:S(2)}) collective-permute-start(bf16[2,128,128]{2,1,0:T(8,128)(2,1)} %get-tuple-element.11.refs_0_), channel_id=1, source_target_pairs={{0,4},{1,5},{2,6},{3,7},{4,0},{5,1},{6,2},{7,3},{8,12},{9,13},{10,... | collective-permute-start | bytes 196616 | tf_op jit(solution)/shard_map/ppermute | solution.py:27
  5.5 9.3 %collective-permute-start.1 = (bf16[2,128,128]{2,1,0:T(8,128)(2,1)}, bf16[2,128,128]{2,1,0:T(8,128)(2,1)S(1)}, u32[]{:S(2)}, u32[]{:S(2)}) collective-permute-start(bf16[2,128,128]{2,1,0:T(8,128)(2,1)} %get-tuple-element.11.refs_0_), channel_id=1, source_target_pairs={{0,8},{1,9},{2,10},{3,11},{4,12},{5,13},{6,14},{7,15},{8,0},{9,1},... | collective-permute-start | bytes 196616 | tf_op jit(solution)/shard_map/ppermute | solution.py:27
  8.1 6.7 %collective-permute-start.2 = (bf16[2,128,128]{2,1,0:T(8,128)(2,1)}, bf16[2,128,128]{2,1,0:T(8,128)(2,1)S(1)}, u32[]{:S(2)}, u32[]{:S(2)}) collective-permute-start(bf16[2,128,128]{2,1,0:T(8,128)(2,1)} %get-tuple-element.11.refs_0_), channel_id=1, source_target_pairs={{0,12},{1,13},{2,14},{3,15},{4,8},{5,9},{6,10},{7,11},{8,4},{9,5},... | collective-permute-start | bytes 196616 | tf_op jit(solution)/shard_map/ppermute | solution.py:27
  8.1 29.1 %all-to-all-start = ((bf16[32,128,128]{2,1,0:T(8,128)(2,1)}), bf16[32,128,128]{2,1,0:T(8,128)(2,1)S(1)}, u32[]{:S(2)}, u32[]{:S(2)}) async-start(bf16[32,128,128]{2,1,0:T(8,128)(2,1)} %get-tuple-element.13), calls=%async_computation | async-start | bytes 2097152 | tf_op jit(solution)/shard_map/all_to_all | solution.py:265
  14.8 14.1 %collective-permute-start.4 = (bf16[4,128,128]{2,1,0:T(8,128)(2,1)S(1)}, bf16[4,128,128]{2,1,0:T(8,128)(2,1)S(1)}, u32[]{:S(2)}, u32[]{:S(2)}) collective-permute-start(bf16[4,128,128]{2,1,0:T(8,128)(2,1)S(1)} %get-tuple-element.12.after), channel_id=1, source_target_pairs={{0,2},{1,3},{2,0},{3,1},{4,6},{5,7},{6,4},{7,5},{8,10},{9,11},{10,... | collective-permute-start | bytes 393224 | tf_op jit(solution)/shard_map/ppermute | solution.py:27
  16.8 16.2 %collective-permute-start.5 = (bf16[4,128,128]{2,1,0:T(8,128)(2,1)S(1)}, bf16[4,128,128]{2,1,0:T(8,128)(2,1)S(1)}, u32[]{:S(2)}, u32[]{:S(2)}) collective-permute-start(bf16[4,128,128]{2,1,0:T(8,128)(2,1)S(1)} %get-tuple-element.12.after), channel_id=1, source_target_pairs={{0,16},{16,0},{1,17},{17,1},{2,18},{18,2},{3,19},{19,3},{4,20},{20... | collective-permute-start | bytes 393224 | tf_op jit(solution)/shard_map/ppermute | solution.py:27
  18.3 5.1 %collective-permute-start.3 = (s32[1,8,256]{2,1,0:T(8,128)S(1)}, s32[1,8,256]{2,1,0:T(8,128)S(1)}, u32[]{:S(2)}, u32[]{:S(2)}) collective-permute-start(s32[1,8,256]{2,1,0:T(8,128)S(1)} %bitcast.24), channel_id=1, source_target_pairs={{0,16},{16,0},{1,17},{17,1},{2,18},{18,2},{3,19},{19,3},{4,20},{20... | collective-permute-start | bytes 24584 | tf_op jit(solution)/shard_map/ppermute | solution.py:27
  18.8 12.6 %collective-permute-start.8 = (bf16[4,128,128]{2,1,0:T(8,128)(2,1)S(1)}, bf16[4,128,128]{2,1,0:T(8,128)(2,1)S(1)}, u32[]{:S(2)}, u32[]{:S(2)}) collective-permute-start(bf16[4,128,128]{2,1,0:T(8,128)(2,1)S(1)} %get-tuple-element.14), channel_id=1, source_target_pairs={{0,2},{1,3},{2,0},{3,1},{4,6},{5,7},{6,4},{7,5},{8,10},{9,11},{10,... | collective-permute-start | bytes 393224 | tf_op jit(solution)/shard_map/ppermute | solution.py:27
  19.0 14.0 %collective-permute-start.9 = (bf16[4,128,128]{2,1,0:T(8,128)(2,1)S(1)}, bf16[4,128,128]{2,1,0:T(8,128)(2,1)S(1)}, u32[]{:S(2)}, u32[]{:S(2)}) collective-permute-start(bf16[4,128,128]{2,1,0:T(8,128)(2,1)S(1)} %get-tuple-element.14), channel_id=1, source_target_pairs={{0,16},{16,0},{1,17},{17,1},{2,18},{18,2},{3,19},{19,3},{4,20},{20... | collective-permute-start | bytes 393224 | tf_op jit(solution)/shard_map/ppermute | solution.py:27
  28.9 5.2 %collective-permute-start.6 = (bf16[4,128,128]{2,1,0:T(8,128)(2,1)S(1)}, bf16[4,128,128]{2,1,0:T(8,128)(2,1)S(1)}, u32[]{:S(2)}, u32[]{:S(2)}) collective-permute-start(bf16[4,128,128]{2,1,0:T(8,128)(2,1)S(1)} %collective-permute-done.4), channel_id=1, source_target_pairs={{0,16},{16,0},{1,17},{17,1},{2,18},{18,2},{3,19},{19,3},{4,20},{20... | collective-permute-start | bytes 393224 | tf_op jit(solution)/shard_map/ppermute | solution.py:27
  31.4 5.3 %collective-permute-start.10 = (bf16[4,128,128]{2,1,0:T(8,128)(2,1)S(1)}, bf16[4,128,128]{2,1,0:T(8,128)(2,1)S(1)}, u32[]{:S(2)}, u32[]{:S(2)}) collective-permute-start(bf16[4,128,128]{2,1,0:T(8,128)(2,1)S(1)} %collective-permute-done.8), channel_id=1, source_target_pairs={{0,16},{16,0},{1,17},{17,1},{2,18},{18,2},{3,19},{19,3},{4,20},{20... | collective-permute-start | bytes 393224 | tf_op jit(solution)/shard_map/ppermute | solution.py:27
  34.1 2.8 %collective-permute-start.7 = (bf16[16,128,128]{2,1,0:T(8,128)(2,1)S(1)}, bf16[16,128,128]{2,1,0:T(8,128)(2,1)S(1)}, u32[]{:S(2)}, u32[]{:S(2)}) collective-permute-start(bf16[16,128,128]{2,1,0:T(8,128)(2,1)S(1)} %constant_dynamic-update-slice_fusion.here), channel_id=1, source_target_pairs={{0,1},{1,0},{2,3},{3,2},{4,5},{5,4},{6,7},{7,6},{8,9},{9,8},{10,11... | collective-permute-start | bytes 1572872 | tf_op jit(solution)/shard_map/ppermute | solution.py:27
  36.7 4.1 %collective-permute-start.11 = (bf16[16,128,128]{2,1,0:T(8,128)(2,1)S(1)}, bf16[16,128,128]{2,1,0:T(8,128)(2,1)S(1)}, u32[]{:S(2)}, u32[]{:S(2)}) collective-permute-start(bf16[16,128,128]{2,1,0:T(8,128)(2,1)S(1)} %constant_dynamic-update-slice_fusion.4.here), channel_id=1, source_target_pairs={{0,1},{1,0},{2,3},{3,2},{4,5},{5,4},{6,7},{7,6},{8,9},{9,8},{10,11... | collective-permute-start | bytes 1572872 | tf_op jit(solution)/shard_map/ppermute | solution.py:27
  46.4 8.9 %collective-permute-start.12 = (bf16[16,64,128]{2,1,0:T(8,128)(2,1)S(1)}, bf16[16,64,128]{2,1,0:T(8,128)(2,1)S(1)}, u32[]{:S(2)}, u32[]{:S(2)}) collective-permute-start(bf16[16,64,128]{2,1,0:T(8,128)(2,1)S(1)} %bitcast.29), channel_id=1, source_target_pairs={{0,16},{16,0},{1,17},{17,1},{2,18},{18,2},{3,19},{19,3},{4,20},{20... | collective-permute-start | bytes 786440 | tf_op jit(solution)/shard_map/ppermute | solution.py:365

commit v6 on v5

v6 whole, which is shorter than its diff:
```python
import functools

import jax
import jax.numpy as jnp
from jax import lax
from jax.experimental import pallas as pl
from jax.experimental.pallas import tpu as pltpu
from jax.sharding import PartitionSpec as P

INTER_TILES = 32
PACK_UNROLL = 8
DEPTH = 8
LEFT_UNROLL = 64
RIGHT_UNROLL = 4


def vmem_params(size):
    return pltpu.CompilerParams(vmem_limit_bytes=min(size + (6 << 20), 60 << 20))


def round_up(value, step):
    return -(-value // step) * step


def swap(value, axis, mask):
    size = lax.axis_size(axis)
    return lax.ppermute(value, axis, [(i, i ^ mask) for i in range(size)])


def cross(value, first):
    sectors, terms = lax.axis_size("sector"), lax.axis_size("term")
    pairs = []
    for i in range(terms * sectors):
        pairs.append((i, i ^ (sectors if (i & 1) == first else 2)))
    return lax.ppermute(value, ("term", "sector"), pairs)


def env_place(group, tile):
    sectors, terms = lax.axis_size("sector"), lax.axis_size("term")
    core = tile & 1
    group = group ^ lax.axis_index("term")
    tile = tile ^ lax.axis_index("sector")
    far = sectors // 4
    over, across = group & 1, (tile >> 1) & 1
    square = jnp.where(core == 0, over + 2 * across, across + 2 * over)
    place = (tile >> 2) + far * (square + 4 * (group >> 1))
    return place + far * 2 * terms * (tile & 1)


def column_kernel(count, *refs):
    tiles, sides = refs[:count], refs[count:]
    for place in range(count):
        for side in range(2):
            sides[side][place] = tiles[place][side]


def gather_far(env):
    count = lax.axis_size("sector") // 4
    vmem = pl.BlockSpec(memory_space=pltpu.VMEM)
    return pl.pallas_call(
        functools.partial(column_kernel, count),
        out_shape=[jax.ShapeDtypeStruct((count,) + env.shape[1:], env.dtype)] * 2,
        in_specs=[vmem] * count,
        out_specs=[vmem] * 2,
        compiler_params=vmem_params(4 * count * env.size),
        name="column",
    )(env, *[swap(env, "sector", mask << 2) for mask in range(1, count)])


def gather_env(column):
    terms = lax.axis_size("term")
    sides = []
    for side in range(2):
        one, two = cross(column[side], 0), cross(column[side], 1)
        plane = jnp.concatenate([column[side], one, two, cross(one, 1)])
        bit = 2
        while bit < terms:
            plane = jnp.concatenate([plane, swap(plane, "term", bit)])
            bit *= 2
        sides.append((plane, swap(plane, "sector", 1)))
    return sides


def pack_kernel(vectors, listed, wave, left, right, out, env, held, picks, sems):
    vector = lax.rem(lax.axis_index("term"), vectors)
    copies = [
        pltpu.make_async_copy(wave.at[:, vector], held, sems.at[0]),
        pltpu.make_async_copy(left.at[0, 0], env.at[0], sems.at[1]),
        pltpu.make_async_copy(right.at[0, 0], env.at[1], sems.at[2]),
        pltpu.make_async_copy(listed, picks, sems.at[3]),
    ]
    for copy in copies:
        copy.start()
    copies[0].wait()
    copies[3].wait()

    @pl.loop(0, out.shape[0] // PACK_UNROLL)
    def _(turn):
        for step in range(PACK_UNROLL):
            slot = turn * PACK_UNROLL + step
            tile = picks[0, slot]
            picked = held[jnp.maximum(tile, 0)]
            out[slot] = jnp.where(tile >= 0, picked, jnp.zeros_like(picked))

    copies[1].wait()
    copies[2].wait()


def schedule(first, second, target, targets, cut, depth, turn, slots, idle):
    count = target.shape[0]
    index = jnp.arange(count, dtype=jnp.int32)
    same = target[:, None] == target[None, :]
    rank = jnp.sum(same & (index[None, :] < index[:, None]), axis=1, dtype=jnp.int32)
    names = jnp.arange(targets, dtype=jnp.int32)
    counts = jnp.sum(target[None, :] == names[:, None], axis=1, dtype=jnp.int32)
    padded = (counts + depth - 1) // depth * depth

    def before(bounds):
        lower = names[None, :] < bounds[:, None]
        return jnp.sum(jnp.where(lower, padded[None, :], 0), axis=1, dtype=jnp.int32)

    head = before(jnp.full((targets,), cut, jnp.int32))
    padded = padded + jnp.where(names == cut - 1, -head & (turn - 1), 0)
    starts = before(target)
    place = starts + rank
    chosen = place[None, :] == jnp.arange(slots, dtype=jnp.int32)[:, None]

    def pick(values, rest):
        return rest + jnp.sum(jnp.where(chosen, values[None, :] - rest, 0), axis=1, dtype=jnp.int32)

    ends = before(cut + (targets - cut) * jnp.arange(2, dtype=jnp.int32))
    return jnp.concatenate([pick(first, idle), pick(second, 0), pick(target, cut), ends])


def tasks_kernel(left, right, after, out):
    out[...] = jnp.zeros_like(out)
    out[0 : left.shape[0], 0 : left.shape[1]] = left[...]
    out[3 : 3 + right.shape[0], 0 : right.shape[1]] = right[...]


def right_products(right, slots, begin, end, rows, lowest, inter, env, total):
    def chunks(at, unroll):
        done = []
        for step in range(unroll):
            base = at + step * DEPTH
            first = [inter[right[base + i], rows, :] for i in range(DEPTH)]
            second = [env[right[slots + base + i]] for i in range(DEPTH)]
            product = jnp.dot(
                jnp.concatenate(first, axis=1),
                jnp.concatenate(second, axis=0),
                preferred_element_type=jnp.float32,
            )
            place = jnp.minimum(right[2 * slots + base] - lowest, total.shape[0] - 1)
            done.append((place, product))
        for place, product in done:
            total[place] += product

    turn = RIGHT_UNROLL * DEPTH
    for width in (4, 2, 1):
        rounds = (end - begin) // width

        @pl.loop(0, rounds)
        def _(step, begin=begin, width=width):
            chunks((begin + step * width) * turn, width * RIGHT_UNROLL)

        begin = begin + rounds * width


def turn_of(right, slots, which):
    turn = RIGHT_UNROLL * DEPTH
    return lax.div(right[3 * slots + which] + turn - 1, turn)


def part_rows(part, share):
    return pl.ds(pl.multiple_of(part * share, share), share)


def join(near, pieces, row, out, sems):
    copies = []
    for place, piece in enumerate(pieces):
        span = pl.ds(place * piece.shape[0], piece.shape[0])
        if near:
            out[span] = piece[:, row]
        else:
            copies.append(pltpu.make_async_copy(piece.at[:, row], out.at[span], sems.at[place]))
    for copy in copies:
        copy.start()
    for copy in copies:
        copy.wait()


def first_kernel(
    count,
    slots,
    near,
    listed_left,
    listed_right,
    wave,
    here_left,
    there_left,
    here_right,
    there_right,
    inter,
    send,
    env_right,
    env_left,
    acc,
    total,
    left,
    right,
    sems,
):
    lists = [
        pltpu.make_async_copy(listed_left, left, sems.at[2]),
        pltpu.make_async_copy(listed_right, right, sems.at[3]),
    ]
    for copy in lists:
        copy.start()
    inters, rows, dim = acc.shape
    acc[...] = jnp.zeros_like(acc)
    total[...] = jnp.zeros_like(total)
    inter[inters] = jnp.zeros((rows, dim), jnp.bfloat16)
    parts, share = send.shape[0] + 1, total.shape[1]
    term = lax.axis_index("term")
    vector = lax.rem(term, parts)
    first_row = 0 if rows == dim else pl.multiple_of(lax.div(term, parts) * rows, rows)
    join(near, (here_left, there_left), pl.ds(first_row, rows), env_left, sems)
    join(near, (here_right, there_right), pl.ds(0, dim), env_right, sems)
    for copy in lists:
        copy.wait()

    @pl.loop(0, count // LEFT_UNROLL)
    def _(turn):
        done = []
        for step in range(LEFT_UNROLL):
            at = turn * LEFT_UNROLL + step
            product = jnp.dot(
                env_left[left[at]], wave[left[count + at]], preferred_element_type=jnp.float32
            )
            done.append((left[2 * count + at], product))
        for place, product in done:
            acc[place] += product

    @pl.loop(0, inters // 8)
    def _(turn):
        for step in range(8):
            inter[turn * 8 + step] = acc[turn * 8 + step].astype(jnp.bfloat16)

    for hop in range(1, parts):
        if hop > 1:
            total[...] = jnp.zeros_like(total)
        own = part_rows(lax.rem(vector + hop, parts), share)
        right_products(right, slots, 0, turn_of(right, slots, 0), own, 0, inter, env_right, total)
        send[hop - 1] = total[...].astype(jnp.bfloat16)


def both_kernel(slots, cut, listed, inter, env, send, keep, total, right, sem):
    lists = pltpu.make_async_copy(listed, right, sem)
    lists.start()
    total[...] = jnp.zeros_like(total)
    lists.wait()
    parts, share = send.shape[0] + 1, keep.shape[1]
    vector = lax.rem(lax.axis_index("term"), parts)
    begin, end = turn_of(right, slots, 0), turn_of(right, slots, 1)
    right_products(right, slots, begin, end, pl.ds(0, total.shape[1]), cut, inter, env, total)
    for hop in range(1, parts):
        rows = part_rows(lax.rem(vector + hop, parts), share)
        send[hop - 1] = total[:, rows, :].astype(jnp.bfloat16)
    keep[...] = total[:, part_rows(vector, share), :]


def own_kernel(slots, parts, listed, inter, env, keep, right, sem):
    lists = pltpu.make_async_copy(listed, right, sem)
    lists.start()
    keep[...] = jnp.zeros_like(keep)
    lists.wait()
    rows = part_rows(lax.rem(lax.axis_index("term"), parts), keep.shape[1])
    right_products(right, slots, 0, turn_of(right, slots, 0), rows, 0, inter, env, keep)


def finish_kernel(vectors, *refs):
    pieces, (out, held, sems) = refs[: 2 * vectors], refs[2 * vectors :]
    vector = lax.rem(lax.axis_index("term"), vectors)
    copies = []
    for hop in range(vectors):
        place = lax.rem(vector + vectors - hop, vectors)
        first = 0
        for part in range(2):
            source = pieces[2 * hop + part]
            span = pl.ds(first, source.shape[0])
            if hop > 0:
                held[hop - 1, span] = source[...].astype(jnp.float32)
                source = held.at[hop - 1, span]
            copies.append(
                pltpu.make_async_copy(source, out.at[span, place], sems.at[2 * hop + part])
            )
            copies[-1].start()
            first += span.size
    for copy in copies:
        copy.wait()


def shards(wave_tiles, left_env, right_env, send_list, left_tasks, right_tasks):
    sectors, terms = lax.axis_size("sector"), lax.axis_size("term")
    tiles, vectors, dim, _ = wave_tiles.shape
    term = lax.axis_index("term")
    blocks = terms // vectors
    rows, share = dim // blocks, dim // terms
    vector, block = term % vectors, term // vectors

    vmem = pl.BlockSpec(memory_space=pltpu.VMEM)
    hbm = pl.BlockSpec(memory_space=pl.ANY)
    send_slots = send_list.shape[1]
    tile_bytes = dim * dim * 2
    outgoing, env = pl.pallas_call(
        functools.partial(pack_kernel, vectors),
        out_shape=(
            jax.ShapeDtypeStruct((send_slots, dim, dim), jnp.bfloat16),
            jax.ShapeDtypeStruct((2, dim, dim), jnp.bfloat16),
        ),
        in_specs=[hbm, hbm, hbm, hbm],
        out_specs=(vmem, vmem),
        scratch_shapes=[
            pltpu.VMEM((tiles, dim, dim), jnp.bfloat16),
            pltpu.SMEM(send_list.shape, jnp.int32),
            pltpu.SemaphoreType.DMA((4,)),
        ],
        compiler_params=vmem_params(54 << 20),
        name="pack",
    )(send_list, wave_tiles, left_env, right_env)
    column = gather_far(env)
    received = lax.all_to_all(outgoing, "sector", split_axis=0, concat_axis=0, tiled=True)
    sides = gather_env(column)

    left_count, right_count = left_tasks.shape[2], right_tasks.shape[2]
    tasks = pl.pallas_call(
        tasks_kernel,
        out_shape=jax.ShapeDtypeStruct((8, max(left_count, right_count)), jnp.int32),
        in_specs=[vmem, vmem, hbm],
        out_specs=vmem,
        compiler_params=vmem_params(0),
        name="tasks",
    )(left_tasks[0, 0].T, right_tasks[0, 0].T, column[0])[None]
    bit = 1
    while bit < terms:
        tasks = jnp.concatenate([tasks, swap(tasks, "term", bit)], axis=0)
        bit *= 2

    def listed(first_row, count):
        rows = jnp.swapaxes(tasks[:, first_row : first_row + 3, :count], 0, 1).reshape(3, -1)
        group = (jnp.arange(terms * count, dtype=jnp.int32) // count) ^ term
        return rows[0], rows[1], rows[2], group

    left_env_tile, left_slot, left_inter, left_group = listed(0, left_count)
    right_inter, right_env_tile, right_sigma, right_group = listed(3, right_count)
    left_count, right_count = terms * left_count, terms * right_count
    left = jnp.concatenate(
        [
            env_place(left_group, left_env_tile),
            left_slot,
            left_group * INTER_TILES + left_inter,
        ]
    )
    turn = DEPTH * RIGHT_UNROLL
    slots = round_up(right_count + tiles * (DEPTH - 1), turn) + turn
    cut = tiles * 11 // 16
    inters = terms * INTER_TILES
    right = schedule(
        right_group * INTER_TILES + right_inter,
        env_place(right_group, right_env_tile),
        right_sigma,
        tiles,
        cut,
        DEPTH,
        turn,
        slots,
        inters,
    )
    block_bytes = rows * dim * 2
    env_tiles = terms * sectors
    env_bytes = env_tiles * tile_bytes
    near = env_bytes <= 2 << 20
    env_spec = vmem if near else hbm
    right_bytes = (tiles * 2 + inters) * block_bytes + env_bytes
    first_bytes = right_bytes + send_slots * tile_bytes + (2 * inters + env_tiles) * block_bytes
    right_params = vmem_params(right_bytes)

    def sent(count):
        return jax.ShapeDtypeStruct((vectors - 1, count, share, dim), jnp.bfloat16)

    def cost(part):
        flops = 2 * right_count * rows * dim * dim // part
        return pl.CostEstimate(flops=flops, bytes_accessed=12 << 20, transcendentals=0)

    inter, send_one, env_right = pl.pallas_call(
        functools.partial(first_kernel, left_count, slots, near),
        out_shape=(
            jax.ShapeDtypeStruct((inters + 1, rows, dim), jnp.bfloat16),
            sent(cut),
            jax.ShapeDtypeStruct((env_tiles, dim, dim), jnp.bfloat16),
        ),
        in_specs=[hbm, hbm, vmem] + [env_spec] * 4,
        out_specs=(vmem, vmem, vmem),
        scratch_shapes=[
            pltpu.VMEM((env_tiles, rows, dim), jnp.bfloat16),
            pltpu.VMEM((inters, rows, dim), jnp.float32),
            pltpu.VMEM((cut, share, dim), jnp.float32),
            pltpu.SMEM(left.shape, jnp.int32),
            pltpu.SMEM(right.shape, jnp.int32),
            pltpu.SemaphoreType.DMA((4,)),
        ],
        compiler_params=vmem_params(first_bytes + near * 2 * env_bytes),
        name="first_products",
    )(left, right, received, *sides[0], *sides[1])
    send_two, keep_two = pl.pallas_call(
        functools.partial(both_kernel, slots, cut),
        out_shape=(
            sent(tiles - cut),
            jax.ShapeDtypeStruct((tiles - cut, share, dim), jnp.float32),
        ),
        in_specs=[hbm, vmem, vmem],
        out_specs=(vmem, vmem),
        scratch_shapes=[
            pltpu.VMEM((tiles - cut, rows, dim), jnp.float32),
            pltpu.SMEM(right.shape, jnp.int32),
            pltpu.SemaphoreType.DMA,
        ],
        compiler_params=right_params,
        cost_estimate=cost(2),
        name="both_products",
    )(right, inter, env_right)
    keep_one = pl.pallas_call(
        functools.partial(own_kernel, slots, vectors),
        out_shape=jax.ShapeDtypeStruct((cut, share, dim), jnp.float32),
        in_specs=[hbm, vmem, vmem],
        out_specs=vmem,
        scratch_shapes=[pltpu.SMEM(right.shape, jnp.int32), pltpu.SemaphoreType.DMA],
        compiler_params=right_params,
        cost_estimate=cost(vectors),
        name="own_products",
    )(right, inter, env_right)
    pieces = [keep_one, keep_two]
    for hop in range(1, vectors):
        pairs = [
            (i, i // vectors * vectors + (i % vectors + hop) % vectors) for i in range(terms)
        ]
        pieces += [lax.ppermute(send[hop - 1], "term", pairs) for send in (send_one, send_two)]
    return pl.pallas_call(
        functools.partial(finish_kernel, vectors),
        out_shape=jax.ShapeDtypeStruct((tiles, vectors, share, dim), jnp.float32),
        in_specs=[vmem] * (2 * vectors),
        out_specs=hbm,
        scratch_shapes=[
            pltpu.VMEM((vectors - 1, tiles, share, dim), jnp.float32),
            pltpu.SemaphoreType.DMA((2 * vectors,)),
        ],
        compiler_params=vmem_params(3 * vectors * tiles * share * dim * 4),
        name="finish",
    )(*pieces)


def solution(mesh):
    in_specs = (
        P("sector", None, None, None),
        P("term", "sector", None, None),
        P("term", "sector", None, None),
        P("sector", None),
        P("term", "sector", None, None),
        P("term", "sector", None, None),
    )
    out_specs = P("sector", None, "term", None)
    return jax.shard_map(shards, mesh=mesh, in_specs=in_specs, out_specs=out_specs, check_vma=False)
```

time: 57.1 us -> 54.9 us (0.961)
  Pallas kernels: 18.7 us -> 16.6 us
  between operations: 0.95 us -> 0.26 us
  starting transfers between devices: 22.2 us -> 22.8 us
    ppermute x1 -> x8, starting transfers between devices: 1.57 us -> 8.36 us  [the longest x6 6.21 us: cross(): return lax.ppermute(value, ('term', 'sector'), pairs)]
    ppermute x12 -> x6, starting transfers between devices: 14.5 us -> 8.34 us  [swap(): return lax.ppermute(value, axis, [(i, i ^ mask) for i in range(size)])]
    ppermute x1 -> x8, waiting for transfers between devices: 1.05 us -> 5.77 us  [the longest x6 5.49 us: cross(): return lax.ppermute(value, ('term', 'sector'), pairs)]
    ppermute x12 -> x6, waiting for transfers between devices: 9.98 us -> 5.65 us  [swap(): return lax.ppermute(value, axis, [(i, i ^ mask) for i in range(size)])]
    pallas_call x3, Pallas kernels: 15.4 us -> 13.2 us  [the longest x1 6.64 us: shards(): pl.pallas_call(functools.partial(first_kernel, left_count, slots, near),...]
  transfers between devices with their start and end apart: 14 -> 15, of which waited for: 7 -> 7; matrix products, arithmetic and copies ran while one was open for 5% -> 4% of each run, Pallas kernels for 18% -> 12%
where the time goes in v6:
time: 54.9 us; the launch traced here: 53.9 us
  starting transfers between devices  22.8 us (42%)
  Pallas kernels  16.6 us (30%)
  waiting for transfers between devices  11.8 us (21%)
  other arithmetic  1.67 us (3%)
  local copies, waits for them, and re-layouts  0.74 us (1%)
    ppermute x6, starting transfers between devices, swap(): return lax.ppermute(value, axis, [(i, i ^ mask) for i in range(size)])  8.34 us
    pallas_call x1, Pallas kernels, shards(): pl.pallas_call(functools.partial(first_kernel, left_count, slots, near),...  6.64 us
    ppermute x6, starting transfers between devices, cross(): return lax.ppermute(value, ('term', 'sector'), pairs)  6.21 us
    all_to_all x1, starting transfers between devices, shards(): lax.all_to_all(outgoing, 'sector', split_axis=0, concat_axis=0, tiled=True)  6.08 us
    ppermute x6, waiting for transfers between devices, swap(): return lax.ppermute(value, axis, [(i, i ^ mask) for i in range(size)])  5.65 us
    ppermute x6, waiting for transfers between devices, cross(): return lax.ppermute(value, ('term', 'sector'), pairs)  5.49 us
    pallas_call x1, Pallas kernels, shards(): pl.pallas_call(functools.partial(own_kernel, slots, vectors), out_shape=j...  3.88 us
    pallas_call x1, Pallas kernels, shards(): pl.pallas_call(functools.partial(both_kernel, slots, cut), out_shape=(sen...  2.71 us
  transfers between devices with their start and end apart: 15, of which 7 were waited for; matrix products, arithmetic and copies ran while one was open for 4% of the time, Pallas kernels for 12%

profile of v6, /device:TPU:0, one launch (start us, length us, event | category | flops | bytes accessed | tf_op | source)
XLA Modules:
  0.0 53.9 jit_solution(11046331175063996333)
XLA Ops:
  0.0 0.0 copy-start.2
  0.0 0.0 copy-start.1
  0.0 2.4 %pack.1 = (bf16[32,128,128]{2,1,0:T(8,128)(2,1)}, bf16[2,128,128]{2,1,0:T(8,128)(2,1)}) custom-call(s32[1,32]{1,0:T(1,128)} %listed.1, bf16[16,2,128,128]{3,2,1,0:T(8,128)(2,1)} %wave.1, bf16[1,1,128,128]{3,2,1,0:T(8,128)(2,1)} %left.1, bf16[1,1,128,128]{3,2,1,0:T(8,128)(2,1)} %right.1), custom_call_target="tpu_custom_call" | custom-call | tf_op jit(solution)/shard_map/pack/pallas_call | solution.py:315
  2.4 0.0 copy-start
  2.4 5.1 %collective-permute-start.2 = (bf16[2,128,128]{2,1,0:T(8,128)(2,1)}, bf16[2,128,128]{2,1,0:T(8,128)(2,1)S(1)}, u32[]{:S(2)}, u32[]{:S(2)}) collective-permute-start(bf16[2,128,128]{2,1,0:T(8,128)(2,1)} %get-tuple-element.14.refs_0_), channel_id=1, source_target_pairs={{0,12},{1,13},{2,14},{3,15},{4,8},{5,9},{6,10},{7,11},{8,4},{9,5},... | collective-permute-start | bytes 196616 | tf_op jit(solution)/shard_map/ppermute | solution.py:27
  7.5 0.0 collective-permute-start.1
  7.5 0.6 %collective-permute-start = (bf16[2,128,128]{2,1,0:T(8,128)(2,1)}, bf16[2,128,128]{2,1,0:T(8,128)(2,1)S(1)}, u32[]{:S(2)}, u32[]{:S(2)}) collective-permute-start(bf16[2,128,128]{2,1,0:T(8,128)(2,1)} %get-tuple-element.14.refs_0_), channel_id=1, source_target_pairs={{0,4},{1,5},{2,6},{3,7},{4,0},{5,1},{6,2},{7,3},{8,12},{9,13},{10,... | collective-permute-start | bytes 196616 | tf_op jit(solution)/shard_map/ppermute | solution.py:27
  8.2 6.1 %all-to-all-start = ((bf16[32,128,128]{2,1,0:T(8,128)(2,1)}), bf16[32,128,128]{2,1,0:T(8,128)(2,1)S(1)}, u32[]{:S(2)}, u32[]{:S(2)}) async-start(bf16[32,128,128]{2,1,0:T(8,128)(2,1)} %get-tuple-element.16), calls=%async_computation | async-start | bytes 2097152 | tf_op jit(solution)/shard_map/all_to_all | solution.py:332
  14.3 0.0 copy-done.2
  14.3 0.0 copy-done.1
  14.3 0.0 collective-permute-done.2.refs_3_
  14.3 0.0 collective-permute-done.1.refs_2_
  14.4 0.0 collective-permute-done.refs_1_
  14.4 0.0 copy-done
  14.4 2.0 %collective-permute-start.9 = (bf16[4,128,128]{2,1,0:T(8,128)(2,1)S(1)}, bf16[4,128,128]{2,1,0:T(8,128)(2,1)S(1)}, u32[]{:S(2)}, u32[]{:S(2)}) collective-permute-start(bf16[4,128,128]{2,1,0:T(8,128)(2,1)S(1)} %get-tuple-element.17), channel_id=1, source_target_pairs={{0,2},{1,17},{2,0},{3,19},{4,6},{5,21},{6,4},{7,23},{8,10},{9,25},... | collective-permute-start | bytes 393224 | tf_op jit(solution)/shard_map/ppermute | solution.py:35
  16.4 1.5 %collective-permute-start.8 = (bf16[4,128,128]{2,1,0:T(8,128)(2,1)S(1)}, bf16[4,128,128]{2,1,0:T(8,128)(2,1)S(1)}, u32[]{:S(2)}, u32[]{:S(2)}) collective-permute-start(bf16[4,128,128]{2,1,0:T(8,128)(2,1)S(1)} %get-tuple-element.17), channel_id=1, source_target_pairs={{0,16},{1,3},{2,18},{3,1},{4,20},{5,7},{6,22},{7,5},{8,24},{9,11},... | collective-permute-start | bytes 393224 | tf_op jit(solution)/shard_map/ppermute | solution.py:35
  17.9 0.1 collective-permute-start.5
  18.0 0.5 collective-permute-start.4
  18.5 1.5 %collective-permute-start.3 = (s32[1,8,256]{2,1,0:T(8,128)S(1)}, s32[1,8,256]{2,1,0:T(8,128)S(1)}, u32[]{:S(2)}, u32[]{:S(2)}) collective-permute-start(s32[1,8,256]{2,1,0:T(8,128)S(1)} %bitcast.22), channel_id=1, source_target_pairs={{0,16},{16,0},{1,17},{17,1},{2,18},{18,2},{3,19},{19,3},{4,20},{20... | collective-permute-start | bytes 24584 | tf_op jit(solution)/shard_map/ppermute | solution.py:27
  20.1 4.3 %collective-permute-done.3 = s32[1,8,256]{2,1,0:T(8,128)S(1)} collective-permute-done((s32[1,8,256]{2,1,0:T(8,128)S(1)}, s32[1,8,256]{2,1,0:T(8,128)S(1)}, u32[]{:S(2)}, u32[]{:S(2)}) %collective-permute-start.3) | collective-permute-done | bytes 8224 | tf_op jit(solution)/shard_map/ppermute | solution.py:27
  24.4 0.1 convert_reduce_fusion.1
  24.5 0.3 convert_reduce_fusion
  24.8 0.1 select_reduce_fusion.4
  24.9 0.1 select_reduce_fusion.3
  25.1 0.6 %select_reduce_fusion = (s32[672]{0:T(1024)S(1)}, s32[672]{0:T(1024)S(1)}, s32[672]{0:T(1024)S(1)}) fusion(s32[512]{0:T(512)S(1)} %broadcast_add_fusion.2, s32[512]{0:T(512)S(1)} %add.136, s32[512]{0:T(512)S(1)} %get-tuple-element.38, s32[512]{0:T(512)S(1)} %get-tuple-element.39), kind=kLoop, calls=%fused_computation | loop fusion | flops 2406432 | bytes 16256 | tf_op jit(solution)/shard_map/reduce_sum | solution.py:129
  25.8 0.1 eq.82
  25.9 0.1 and.117
  25.9 0.1 squeeze.27
  26.0 0.1 squeeze.26
  26.1 0.1 mul.112
  26.2 0.1 shift_right_arithmetic.43
  26.3 0.2 fusion.8
  26.5 0.0 collective-permute-done.8
  26.5 0.7 %collective-permute-start.10 = (bf16[4,128,128]{2,1,0:T(8,128)(2,1)S(1)}, bf16[4,128,128]{2,1,0:T(8,128)(2,1)S(1)}, u32[]{:S(2)}, u32[]{:S(2)}) collective-permute-start(bf16[4,128,128]{2,1,0:T(8,128)(2,1)S(1)} %collective-permute-done.8), channel_id=1, source_target_pairs={{0,2},{1,17},{2,0},{3,19},{4,6},{5,21},{6,4},{7,23},{8,10},{9,25},... | collective-permute-start | bytes 393224 | tf_op jit(solution)/shard_map/ppermute | solution.py:35
  27.1 0.0 collective-permute-done.4
  27.1 1.4 %collective-permute-start.6 = (bf16[4,128,128]{2,1,0:T(8,128)(2,1)S(1)}, bf16[4,128,128]{2,1,0:T(8,128)(2,1)S(1)}, u32[]{:S(2)}, u32[]{:S(2)}) collective-permute-start(bf16[4,128,128]{2,1,0:T(8,128)(2,1)S(1)} %collective-permute-done.4), channel_id=1, source_target_pairs={{0,2},{1,17},{2,0},{3,19},{4,6},{5,21},{6,4},{7,23},{8,10},{9,25},... | collective-permute-start | bytes 393224 | tf_op jit(solution)/shard_map/ppermute | solution.py:35
  28.6 2.8 %collective-permute-done.5 = bf16[4,128,128]{2,1,0:T(8,128)(2,1)S(1)} collective-permute-done((bf16[4,128,128]{2,1,0:T(8,128)(2,1)S(1)}, bf16[4,128,128]{2,1,0:T(8,128)(2,1)S(1)}, u32[]{:S(2)}, u32[]{:S(2)}) %collective-permute-start.5) | collective-permute-done | bytes 131104 | tf_op jit(solution)/shard_map/ppermute | solution.py:35
  31.5 0.0 collective-permute-done.9
  31.5 1.3 %collective-permute-done.10 = bf16[4,128,128]{2,1,0:T(8,128)(2,1)S(1)} collective-permute-done((bf16[4,128,128]{2,1,0:T(8,128)(2,1)S(1)}, bf16[4,128,128]{2,1,0:T(8,128)(2,1)S(1)}, u32[]{:S(2)}, u32[]{:S(2)}) %collective-permute-start.10) | collective-permute-done | bytes 131104 | tf_op jit(solution)/shard_map/ppermute | solution.py:35
  32.9 0.1 collective-permute-start.11
  32.9 1.3 %collective-permute-done.6 = bf16[4,128,128]{2,1,0:T(8,128)(2,1)S(1)} collective-permute-done((bf16[4,128,128]{2,1,0:T(8,128)(2,1)S(1)}, bf16[4,128,128]{2,1,0:T(8,128)(2,1)S(1)}, u32[]{:S(2)}, u32[]{:S(2)}) %collective-permute-start.6) | collective-permute-done | bytes 131104 | tf_op jit(solution)/shard_map/ppermute | solution.py:35
  34.3 1.0 %collective-permute-start.7 = (bf16[16,128,128]{2,1,0:T(8,128)(2,1)S(1)}, bf16[16,128,128]{2,1,0:T(8,128)(2,1)S(1)}, u32[]{:S(2)}, u32[]{:S(2)}) collective-permute-start(bf16[16,128,128]{2,1,0:T(8,128)(2,1)S(1)} %constant_dynamic-update-slice_fusion.here_left), channel_id=1, source_target_pairs={{0,1},{1,0},{2,3},{3,2},{4,5},{5,4},{6,7},{7,6},{8,9},{9,8},{10,11... | collective-permute-start | bytes 1572872 | tf_op jit(solution)/shard_map/ppermute | solution.py:27
  35.3 0.1 concatenate.16.listed_right.listed
  35.4 0.1 pad_add_fusion.1.listed_left
  35.5 0.0 collective-permute-done.11.there_right
  35.5 1.4 %collective-permute-done.7.there_left = bf16[16,128,128]{2,1,0:T(8,128)(2,1)S(1)} collective-permute-done((bf16[16,128,128]{2,1,0:T(8,128)(2,1)S(1)}, bf16[16,128,128]{2,1,0:T(8,128)(2,1)S(1)}, u32[]{:S(2)}, u32[]{:S(2)}) %collective-permute-start.7) | collective-permute-done | bytes 524320 | tf_op jit(solution)/shard_map/ppermute | solution.py:27
  36.8 0.4 all-to-all-done.wave
  37.2 6.6 %first_products.1 = (bf16[65,128,128]{2,1,0:T(8,128)(2,1)S(1)}, bf16[1,11,64,128]{3,2,1,0:T(8,128)(2,1)S(1)}, bf16[32,128,128]{2,1,0:T(8,128)(2,1)S(1)}) custom-call(s32[576]{0:T(1024)S(1)} %pad_add_fusion.1.listed_left, s32[2018]{0:T(1024)S(1)} %concatenate.16.listed_right.listed, bf16[32,128,128]{2,1,0:T(8,128)(2,1)S(1)} %all-to-all-done.wave, ...), custom_call_target="tpu_custom_call" | custom-call | tf_op jit(solution)/shard_map/first_products/pallas_call | solution.py:395
  43.8 1.6 %collective-permute-start.12 = (bf16[11,64,128]{2,1,0:T(8,128)(2,1)S(1)}, bf16[11,64,128]{2,1,0:T(8,128)(2,1)S(1)}, u32[]{:S(2)}, u32[]{:S(2)}) collective-permute-start(bf16[11,64,128]{2,1,0:T(8,128)(2,1)S(1)} %bitcast.27), channel_id=1, source_target_pairs={{0,16},{16,0},{1,17},{17,1},{2,18},{18,2},{3,19},{19,3},{4,20},{20... | collective-permute-start | bytes 540680 | tf_op jit(solution)/shard_map/ppermute | solution.py:447
  45.4 2.7 %both_products.1 = (bf16[1,5,64,128]{3,2,1,0:T(8,128)(2,1)S(1)}, f32[5,64,128]{2,1,0:T(8,128)S(1)}) custom-call(s32[2018]{0:T(1024)S(1)} %concatenate.16.listed_right.listed, bf16[65,128,128]{2,1,0:T(8,128)(2,1)S(1)} %get-tuple-element.18.inter, bf16[32,128,128]{2,1,0:T(8,128)(2,1)S(1)} %get-tuple-element.19.env), custom_call_target="tpu_custom_call" | custom-call | flops 1073741824 | bytes 12582912 | tf_op jit(solution)/shard_map/both_products/pallas_call | solution.py:415
  48.1 0.6 %collective-permute-start.13 = (bf16[5,64,128]{2,1,0:T(8,128)(2,1)S(1)}, bf16[5,64,128]{2,1,0:T(8,128)(2,1)S(1)}, u32[]{:S(2)}, u32[]{:S(2)}) collective-permute-start(bf16[5,64,128]{2,1,0:T(8,128)(2,1)S(1)} %bitcast.28), channel_id=1, source_target_pairs={{0,16},{16,0},{1,17},{17,1},{2,18},{18,2},{3,19},{19,3},{4,20},{20... | collective-permute-start | bytes 245768 | tf_op jit(solution)/shard_map/ppermute | solution.py:447
  48.7 3.9 %own_products.1.refs_0_ = f32[11,64,128]{2,1,0:T(8,128)S(1)} custom-call(s32[2018]{0:T(1024)S(1)} %concatenate.16.listed_right.listed, bf16[65,128,128]{2,1,0:T(8,128)(2,1)S(1)} %get-tuple-element.18.inter, bf16[32,128,128]{2,1,0:T(8,128)(2,1)S(1)} %get-tuple-element.19.env), custom_call_target="tpu_custom_call" | custom-call | flops 1073741824 | bytes 12582912 | tf_op jit(solution)/shard_map/own_products/pallas_call | solution.py:432
  52.6 0.3 collective-permute-done.13.refs_3_
  52.9 0.0 collective-permute-done.12.refs_2_
  52.9 1.0 %finish.1 = f32[16,2,64,128]{3,2,1,0:T(8,128)} custom-call(f32[11,64,128]{2,1,0:T(8,128)S(1)} %own_products.1.refs_0_, f32[5,64,128]{2,1,0:T(8,128)S(1)} %get-tuple-element.20.refs_1_, bf16[11,64,128]{2,1,0:T(8,128)(2,1)S(1)} %collective-permute-done.12.refs_2_, bf16[5,64,128]{2,1,0:T(8,128)(2,1)S(1)} %collective-permute-done.13.refs_3_), custom_call_target="tpu_custom_call" | custom-call | tf_op jit(solution)/shard_map/finish/pallas_call | solution.py:448
  (28 shorter events, 0.4 us)
Async XLA Ops:
  0.0 14.3 %copy-start.2 = (s32[1,1,96,3]{2,1,3,0:T(1,128)S(1)}, s32[1,1,96,3]{2,1,3,0:T(1,128)}, u32[]{:S(2)}) copy-start(s32[1,1,96,3]{2,1,3,0:T(1,128)} %param.10) | copy-start | bytes 3460
  0.0 14.3 %copy-start.1 = (s32[1,1,256,3]{2,1,3,0:T(1,128)S(1)}, s32[1,1,256,3]{2,1,3,0:T(1,128)}, u32[]{:S(2)}) copy-start(s32[1,1,256,3]{2,1,3,0:T(1,128)} %param.11) | copy-start | bytes 9220
  2.4 12.0 %copy-start = (bf16[2,128,128]{2,1,0:T(8,128)(2,1)S(1)}, bf16[2,128,128]{2,1,0:T(8,128)(2,1)}, u32[]{:S(2)}) copy-start(bf16[2,128,128]{2,1,0:T(8,128)(2,1)} %get-tuple-element.14.refs_0_) | copy-start | bytes 196612
  2.4 11.9 %collective-permute-start.2 = (bf16[2,128,128]{2,1,0:T(8,128)(2,1)}, bf16[2,128,128]{2,1,0:T(8,128)(2,1)S(1)}, u32[]{:S(2)}, u32[]{:S(2)}) collective-permute-start(bf16[2,128,128]{2,1,0:T(8,128)(2,1)} %get-tuple-element.14.refs_0_), channel_id=1, source_target_pairs={{0,12},{1,13},{2,14},{3,15},{4,8},{5,9},{6,10},{7,11},{8,4},{9,5},... | collective-permute-start | bytes 196616 | tf_op jit(solution)/shard_map/ppermute | solution.py:27
  7.5 6.8 %collective-permute-start.1 = (bf16[2,128,128]{2,1,0:T(8,128)(2,1)}, bf16[2,128,128]{2,1,0:T(8,128)(2,1)S(1)}, u32[]{:S(2)}, u32[]{:S(2)}) collective-permute-start(bf16[2,128,128]{2,1,0:T(8,128)(2,1)} %get-tuple-element.14.refs_0_), channel_id=1, source_target_pairs={{0,8},{1,9},{2,10},{3,11},{4,12},{5,13},{6,14},{7,15},{8,0},{9,1},... | collective-permute-start | bytes 196616 | tf_op jit(solution)/shard_map/ppermute | solution.py:27
  7.5 6.8 %collective-permute-start = (bf16[2,128,128]{2,1,0:T(8,128)(2,1)}, bf16[2,128,128]{2,1,0:T(8,128)(2,1)S(1)}, u32[]{:S(2)}, u32[]{:S(2)}) collective-permute-start(bf16[2,128,128]{2,1,0:T(8,128)(2,1)} %get-tuple-element.14.refs_0_), channel_id=1, source_target_pairs={{0,4},{1,5},{2,6},{3,7},{4,0},{5,1},{6,2},{7,3},{8,12},{9,13},{10,... | collective-permute-start | bytes 196616 | tf_op jit(solution)/shard_map/ppermute | solution.py:27
  8.2 29.0 %all-to-all-start = ((bf16[32,128,128]{2,1,0:T(8,128)(2,1)}), bf16[32,128,128]{2,1,0:T(8,128)(2,1)S(1)}, u32[]{:S(2)}, u32[]{:S(2)}) async-start(bf16[32,128,128]{2,1,0:T(8,128)(2,1)} %get-tuple-element.16), calls=%async_computation | async-start | bytes 2097152 | tf_op jit(solution)/shard_map/all_to_all | solution.py:332
  14.4 17.1 %collective-permute-start.9 = (bf16[4,128,128]{2,1,0:T(8,128)(2,1)S(1)}, bf16[4,128,128]{2,1,0:T(8,128)(2,1)S(1)}, u32[]{:S(2)}, u32[]{:S(2)}) collective-permute-start(bf16[4,128,128]{2,1,0:T(8,128)(2,1)S(1)} %get-tuple-element.17), channel_id=1, source_target_pairs={{0,2},{1,17},{2,0},{3,19},{4,6},{5,21},{6,4},{7,23},{8,10},{9,25},... | collective-permute-start | bytes 393224 | tf_op jit(solution)/shard_map/ppermute | solution.py:35
  16.4 10.1 %collective-permute-start.8 = (bf16[4,128,128]{2,1,0:T(8,128)(2,1)S(1)}, bf16[4,128,128]{2,1,0:T(8,128)(2,1)S(1)}, u32[]{:S(2)}, u32[]{:S(2)}) collective-permute-start(bf16[4,128,128]{2,1,0:T(8,128)(2,1)S(1)} %get-tuple-element.17), channel_id=1, source_target_pairs={{0,16},{1,3},{2,18},{3,1},{4,20},{5,7},{6,22},{7,5},{8,24},{9,11},... | collective-permute-start | bytes 393224 | tf_op jit(solution)/shard_map/ppermute | solution.py:35
  17.9 13.6 %collective-permute-start.5 = (bf16[4,128,128]{2,1,0:T(8,128)(2,1)S(1)}, bf16[4,128,128]{2,1,0:T(8,128)(2,1)S(1)}, u32[]{:S(2)}, u32[]{:S(2)}) collective-permute-start(bf16[4,128,128]{2,1,0:T(8,128)(2,1)S(1)} %get-tuple-element.15.after), channel_id=1, source_target_pairs={{0,2},{1,17},{2,0},{3,19},{4,6},{5,21},{6,4},{7,23},{8,10},{9,25},... | collective-permute-start | bytes 393224 | tf_op jit(solution)/shard_map/ppermute | solution.py:35
  18.0 9.1 %collective-permute-start.4 = (bf16[4,128,128]{2,1,0:T(8,128)(2,1)S(1)}, bf16[4,128,128]{2,1,0:T(8,128)(2,1)S(1)}, u32[]{:S(2)}, u32[]{:S(2)}) collective-permute-start(bf16[4,128,128]{2,1,0:T(8,128)(2,1)S(1)} %get-tuple-element.15.after), channel_id=1, source_target_pairs={{0,16},{1,3},{2,18},{3,1},{4,20},{5,7},{6,22},{7,5},{8,24},{9,11},... | collective-permute-start | bytes 393224 | tf_op jit(solution)/shard_map/ppermute | solution.py:35
  18.5 5.8 %collective-permute-start.3 = (s32[1,8,256]{2,1,0:T(8,128)S(1)}, s32[1,8,256]{2,1,0:T(8,128)S(1)}, u32[]{:S(2)}, u32[]{:S(2)}) collective-permute-start(s32[1,8,256]{2,1,0:T(8,128)S(1)} %bitcast.22), channel_id=1, source_target_pairs={{0,16},{16,0},{1,17},{17,1},{2,18},{18,2},{3,19},{19,3},{4,20},{20... | collective-permute-start | bytes 24584 | tf_op jit(solution)/shard_map/ppermute | solution.py:27
  26.5 6.4 %collective-permute-start.10 = (bf16[4,128,128]{2,1,0:T(8,128)(2,1)S(1)}, bf16[4,128,128]{2,1,0:T(8,128)(2,1)S(1)}, u32[]{:S(2)}, u32[]{:S(2)}) collective-permute-start(bf16[4,128,128]{2,1,0:T(8,128)(2,1)S(1)} %collective-permute-done.8), channel_id=1, source_target_pairs={{0,2},{1,17},{2,0},{3,19},{4,6},{5,21},{6,4},{7,23},{8,10},{9,25},... | collective-permute-start | bytes 393224 | tf_op jit(solution)/shard_map/ppermute | solution.py:35
  27.1 7.1 %collective-permute-start.6 = (bf16[4,128,128]{2,1,0:T(8,128)(2,1)S(1)}, bf16[4,128,128]{2,1,0:T(8,128)(2,1)S(1)}, u32[]{:S(2)}, u32[]{:S(2)}) collective-permute-start(bf16[4,128,128]{2,1,0:T(8,128)(2,1)S(1)} %collective-permute-done.4), channel_id=1, source_target_pairs={{0,2},{1,17},{2,0},{3,19},{4,6},{5,21},{6,4},{7,23},{8,10},{9,25},... | collective-permute-start | bytes 393224 | tf_op jit(solution)/shard_map/ppermute | solution.py:35
  32.9 2.6 %collective-permute-start.11 = (bf16[16,128,128]{2,1,0:T(8,128)(2,1)S(1)}, bf16[16,128,128]{2,1,0:T(8,128)(2,1)S(1)}, u32[]{:S(2)}, u32[]{:S(2)}) collective-permute-start(bf16[16,128,128]{2,1,0:T(8,128)(2,1)S(1)} %constant_dynamic-update-slice_fusion.4.here_right), channel_id=1, source_target_pairs={{0,1},{1,0},{2,3},{3,2},{4,5},{5,4},{6,7},{7,6},{8,9},{9,8},{10,11... | collective-permute-start | bytes 1572872 | tf_op jit(solution)/shard_map/ppermute | solution.py:27
  34.3 2.5 %collective-permute-start.7 = (bf16[16,128,128]{2,1,0:T(8,128)(2,1)S(1)}, bf16[16,128,128]{2,1,0:T(8,128)(2,1)S(1)}, u32[]{:S(2)}, u32[]{:S(2)}) collective-permute-start(bf16[16,128,128]{2,1,0:T(8,128)(2,1)S(1)} %constant_dynamic-update-slice_fusion.here_left), channel_id=1, source_target_pairs={{0,1},{1,0},{2,3},{3,2},{4,5},{5,4},{6,7},{7,6},{8,9},{9,8},{10,11... | collective-permute-start | bytes 1572872 | tf_op jit(solution)/shard_map/ppermute | solution.py:27
  43.8 9.0 %collective-permute-start.12 = (bf16[11,64,128]{2,1,0:T(8,128)(2,1)S(1)}, bf16[11,64,128]{2,1,0:T(8,128)(2,1)S(1)}, u32[]{:S(2)}, u32[]{:S(2)}) collective-permute-start(bf16[11,64,128]{2,1,0:T(8,128)(2,1)S(1)} %bitcast.27), channel_id=1, source_target_pairs={{0,16},{16,0},{1,17},{17,1},{2,18},{18,2},{3,19},{19,3},{4,20},{20... | collective-permute-start | bytes 540680 | tf_op jit(solution)/shard_map/ppermute | solution.py:447
  48.1 4.7 %collective-permute-start.13 = (bf16[5,64,128]{2,1,0:T(8,128)(2,1)S(1)}, bf16[5,64,128]{2,1,0:T(8,128)(2,1)S(1)}, u32[]{:S(2)}, u32[]{:S(2)}) collective-permute-start(bf16[5,64,128]{2,1,0:T(8,128)(2,1)S(1)} %bitcast.28), channel_id=1, source_target_pairs={{0,16},{16,0},{1,17},{17,1},{2,18},{18,2},{3,19},{19,3},{4,20},{20... | collective-permute-start | bytes 245768 | tf_op jit(solution)/shard_map/ppermute | solution.py:447

commit v7 on v6

--- a/solution.py
+++ b/solution.py
@@ -10,7 +10,7 @@
 INTER_TILES = 32
 PACK_UNROLL = 8
 DEPTH = 8
-LEFT_UNROLL = 64
+LEFT_UNROLL = 96
 RIGHT_UNROLL = 4
 
 
@@ -226,8 +226,7 @@
     first_row = 0 if rows == dim else pl.multiple_of(lax.div(term, parts) * rows, rows)
     join(near, (here_left, there_left), pl.ds(first_row, rows), env_left, sems)
     join(near, (here_right, there_right), pl.ds(0, dim), env_right, sems)
-    for copy in lists:
-        copy.wait()
+    lists[0].wait()
 
     @pl.loop(0, count // LEFT_UNROLL)
     def _(turn):
@@ -246,6 +245,7 @@
         for step in range(8):
             inter[turn * 8 + step] = acc[turn * 8 + step].astype(jnp.bfloat16)
 
+    lists[1].wait()
     for hop in range(1, parts):
         if hop > 1:
             total[...] = jnp.zeros_like(total)

time: 54.9 us -> 54.5 us (level)
  no operation moved by 1% of the time
where the time goes in v7:
time: 54.5 us; the launch traced here: 53.5 us
  starting transfers between devices  22.8 us (42%)
  Pallas kernels  16.4 us (30%)
  waiting for transfers between devices  11.6 us (21%)
  other arithmetic  1.67 us (3%)
  local copies, waits for them, and re-layouts  0.74 us (1%)
    ppermute x6, starting transfers between devices, swap(): return lax.ppermute(value, axis, [(i, i ^ mask) for i in range(size)])  8.34 us
    pallas_call x1, Pallas kernels, shards(): pl.pallas_call(functools.partial(first_kernel, left_count, slots, near),...  6.38 us
    ppermute x6, starting transfers between devices, cross(): return lax.ppermute(value, ('term', 'sector'), pairs)  6.21 us
    all_to_all x1, starting transfers between devices, shards(): lax.all_to_all(outgoing, 'sector', split_axis=0, concat_axis=0, tiled=True)  6.08 us
    ppermute x6, waiting for transfers between devices, swap(): return lax.ppermute(value, axis, [(i, i ^ mask) for i in range(size)])  5.65 us
    ppermute x6, waiting for transfers between devices, cross(): return lax.ppermute(value, ('term', 'sector'), pairs)  5.49 us
    pallas_call x1, Pallas kernels, shards(): pl.pallas_call(functools.partial(own_kernel, slots, vectors), out_shape=j...  3.9 us
    pallas_call x1, Pallas kernels, shards(): pl.pallas_call(functools.partial(both_kernel, slots, cut), out_shape=(sen...  2.71 us
  transfers between devices with their start and end apart: 15, of which 7 were waited for; matrix products, arithmetic and copies ran while one was open for 4% of the time, Pallas kernels for 12%

profile of v7, /device:TPU:0, one launch (start us, length us, event | category | flops | bytes accessed | tf_op | source)
XLA Modules:
  0.0 53.5 jit_solution(5935699834985388685)
XLA Ops:
  0.0 0.0 copy-start.2
  0.0 0.0 copy-start.1
  0.0 2.4 %pack.1 = (bf16[32,128,128]{2,1,0:T(8,128)(2,1)}, bf16[2,128,128]{2,1,0:T(8,128)(2,1)}) custom-call(s32[1,32]{1,0:T(1,128)} %listed.1, bf16[16,2,128,128]{3,2,1,0:T(8,128)(2,1)} %wave.1, bf16[1,1,128,128]{3,2,1,0:T(8,128)(2,1)} %left.1, bf16[1,1,128,128]{3,2,1,0:T(8,128)(2,1)} %right.1), custom_call_target="tpu_custom_call" | custom-call | tf_op jit(solution)/shard_map/pack/pallas_call | solution.py:315
  2.4 0.0 copy-start
  2.4 5.1 %collective-permute-start.2 = (bf16[2,128,128]{2,1,0:T(8,128)(2,1)}, bf16[2,128,128]{2,1,0:T(8,128)(2,1)S(1)}, u32[]{:S(2)}, u32[]{:S(2)}) collective-permute-start(bf16[2,128,128]{2,1,0:T(8,128)(2,1)} %get-tuple-element.14.refs_0_), channel_id=1, source_target_pairs={{0,12},{1,13},{2,14},{3,15},{4,8},{5,9},{6,10},{7,11},{8,4},{9,5},... | collective-permute-start | bytes 196616 | tf_op jit(solution)/shard_map/ppermute | solution.py:27
  7.5 0.0 collective-permute-start.1
  7.5 0.6 %collective-permute-start = (bf16[2,128,128]{2,1,0:T(8,128)(2,1)}, bf16[2,128,128]{2,1,0:T(8,128)(2,1)S(1)}, u32[]{:S(2)}, u32[]{:S(2)}) collective-permute-start(bf16[2,128,128]{2,1,0:T(8,128)(2,1)} %get-tuple-element.14.refs_0_), channel_id=1, source_target_pairs={{0,4},{1,5},{2,6},{3,7},{4,0},{5,1},{6,2},{7,3},{8,12},{9,13},{10,... | collective-permute-start | bytes 196616 | tf_op jit(solution)/shard_map/ppermute | solution.py:27
  8.2 6.1 %all-to-all-start = ((bf16[32,128,128]{2,1,0:T(8,128)(2,1)}), bf16[32,128,128]{2,1,0:T(8,128)(2,1)S(1)}, u32[]{:S(2)}, u32[]{:S(2)}) async-start(bf16[32,128,128]{2,1,0:T(8,128)(2,1)} %get-tuple-element.16), calls=%async_computation | async-start | bytes 2097152 | tf_op jit(solution)/shard_map/all_to_all | solution.py:332
  14.3 0.0 copy-done.2
  14.3 0.0 copy-done.1
  14.3 0.0 collective-permute-done.2.refs_3_
  14.3 0.0 collective-permute-done.1.refs_2_
  14.4 0.0 collective-permute-done.refs_1_
  14.4 0.0 copy-done
  14.4 2.0 %collective-permute-start.9 = (bf16[4,128,128]{2,1,0:T(8,128)(2,1)S(1)}, bf16[4,128,128]{2,1,0:T(8,128)(2,1)S(1)}, u32[]{:S(2)}, u32[]{:S(2)}) collective-permute-start(bf16[4,128,128]{2,1,0:T(8,128)(2,1)S(1)} %get-tuple-element.17), channel_id=1, source_target_pairs={{0,2},{1,17},{2,0},{3,19},{4,6},{5,21},{6,4},{7,23},{8,10},{9,25},... | collective-permute-start | bytes 393224 | tf_op jit(solution)/shard_map/ppermute | solution.py:35
  16.4 1.5 %collective-permute-start.8 = (bf16[4,128,128]{2,1,0:T(8,128)(2,1)S(1)}, bf16[4,128,128]{2,1,0:T(8,128)(2,1)S(1)}, u32[]{:S(2)}, u32[]{:S(2)}) collective-permute-start(bf16[4,128,128]{2,1,0:T(8,128)(2,1)S(1)} %get-tuple-element.17), channel_id=1, source_target_pairs={{0,16},{1,3},{2,18},{3,1},{4,20},{5,7},{6,22},{7,5},{8,24},{9,11},... | collective-permute-start | bytes 393224 | tf_op jit(solution)/shard_map/ppermute | solution.py:35
  17.9 0.1 collective-permute-start.5
  18.0 0.5 collective-permute-start.4
  18.5 1.5 %collective-permute-start.3 = (s32[1,8,256]{2,1,0:T(8,128)S(1)}, s32[1,8,256]{2,1,0:T(8,128)S(1)}, u32[]{:S(2)}, u32[]{:S(2)}) collective-permute-start(s32[1,8,256]{2,1,0:T(8,128)S(1)} %bitcast.22), channel_id=1, source_target_pairs={{0,16},{16,0},{1,17},{17,1},{2,18},{18,2},{3,19},{19,3},{4,20},{20... | collective-permute-start | bytes 24584 | tf_op jit(solution)/shard_map/ppermute | solution.py:27
  20.1 4.3 %collective-permute-done.3 = s32[1,8,256]{2,1,0:T(8,128)S(1)} collective-permute-done((s32[1,8,256]{2,1,0:T(8,128)S(1)}, s32[1,8,256]{2,1,0:T(8,128)S(1)}, u32[]{:S(2)}, u32[]{:S(2)}) %collective-permute-start.3) | collective-permute-done | bytes 8224 | tf_op jit(solution)/shard_map/ppermute | solution.py:27
  24.4 0.1 convert_reduce_fusion.1
  24.5 0.3 convert_reduce_fusion
  24.8 0.1 select_reduce_fusion.4
  24.9 0.1 select_reduce_fusion.3
  25.1 0.6 %select_reduce_fusion = (s32[672]{0:T(1024)S(1)}, s32[672]{0:T(1024)S(1)}, s32[672]{0:T(1024)S(1)}) fusion(s32[512]{0:T(512)S(1)} %broadcast_add_fusion.2, s32[512]{0:T(512)S(1)} %add.136, s32[512]{0:T(512)S(1)} %get-tuple-element.38, s32[512]{0:T(512)S(1)} %get-tuple-element.39), kind=kLoop, calls=%fused_computation | loop fusion | flops 2406432 | bytes 16256 | tf_op jit(solution)/shard_map/reduce_sum | solution.py:129
  25.8 0.1 eq.82
  25.9 0.1 and.117
  25.9 0.1 squeeze.27
  26.0 0.1 squeeze.26
  26.1 0.1 mul.112
  26.2 0.1 shift_right_arithmetic.43
  26.3 0.2 fusion.8
  26.5 0.0 collective-permute-done.8
  26.5 0.7 %collective-permute-start.10 = (bf16[4,128,128]{2,1,0:T(8,128)(2,1)S(1)}, bf16[4,128,128]{2,1,0:T(8,128)(2,1)S(1)}, u32[]{:S(2)}, u32[]{:S(2)}) collective-permute-start(bf16[4,128,128]{2,1,0:T(8,128)(2,1)S(1)} %collective-permute-done.8), channel_id=1, source_target_pairs={{0,2},{1,17},{2,0},{3,19},{4,6},{5,21},{6,4},{7,23},{8,10},{9,25},... | collective-permute-start | bytes 393224 | tf_op jit(solution)/shard_map/ppermute | solution.py:35
  27.1 0.0 collective-permute-done.4
  27.1 1.4 %collective-permute-start.6 = (bf16[4,128,128]{2,1,0:T(8,128)(2,1)S(1)}, bf16[4,128,128]{2,1,0:T(8,128)(2,1)S(1)}, u32[]{:S(2)}, u32[]{:S(2)}) collective-permute-start(bf16[4,128,128]{2,1,0:T(8,128)(2,1)S(1)} %collective-permute-done.4), channel_id=1, source_target_pairs={{0,2},{1,17},{2,0},{3,19},{4,6},{5,21},{6,4},{7,23},{8,10},{9,25},... | collective-permute-start | bytes 393224 | tf_op jit(solution)/shard_map/ppermute | solution.py:35
  28.6 2.8 %collective-permute-done.5 = bf16[4,128,128]{2,1,0:T(8,128)(2,1)S(1)} collective-permute-done((bf16[4,128,128]{2,1,0:T(8,128)(2,1)S(1)}, bf16[4,128,128]{2,1,0:T(8,128)(2,1)S(1)}, u32[]{:S(2)}, u32[]{:S(2)}) %collective-permute-start.5) | collective-permute-done | bytes 131104 | tf_op jit(solution)/shard_map/ppermute | solution.py:35
  31.5 0.0 collective-permute-done.9
  31.5 1.3 %collective-permute-done.10 = bf16[4,128,128]{2,1,0:T(8,128)(2,1)S(1)} collective-permute-done((bf16[4,128,128]{2,1,0:T(8,128)(2,1)S(1)}, bf16[4,128,128]{2,1,0:T(8,128)(2,1)S(1)}, u32[]{:S(2)}, u32[]{:S(2)}) %collective-permute-start.10) | collective-permute-done | bytes 131104 | tf_op jit(solution)/shard_map/ppermute | solution.py:35
  32.9 0.1 collective-permute-start.11
  32.9 1.3 %collective-permute-done.6 = bf16[4,128,128]{2,1,0:T(8,128)(2,1)S(1)} collective-permute-done((bf16[4,128,128]{2,1,0:T(8,128)(2,1)S(1)}, bf16[4,128,128]{2,1,0:T(8,128)(2,1)S(1)}, u32[]{:S(2)}, u32[]{:S(2)}) %collective-permute-start.6) | collective-permute-done | bytes 131104 | tf_op jit(solution)/shard_map/ppermute | solution.py:35
  34.3 1.0 %collective-permute-start.7 = (bf16[16,128,128]{2,1,0:T(8,128)(2,1)S(1)}, bf16[16,128,128]{2,1,0:T(8,128)(2,1)S(1)}, u32[]{:S(2)}, u32[]{:S(2)}) collective-permute-start(bf16[16,128,128]{2,1,0:T(8,128)(2,1)S(1)} %constant_dynamic-update-slice_fusion.here_left), channel_id=1, source_target_pairs={{0,1},{1,0},{2,3},{3,2},{4,5},{5,4},{6,7},{7,6},{8,9},{9,8},{10,11... | collective-permute-start | bytes 1572872 | tf_op jit(solution)/shard_map/ppermute | solution.py:27
  35.3 0.1 concatenate.16.listed_right.listed
  35.4 0.1 pad_add_fusion.1.listed_left
  35.5 0.0 collective-permute-done.11.there_right
  35.5 1.4 %collective-permute-done.7.there_left = bf16[16,128,128]{2,1,0:T(8,128)(2,1)S(1)} collective-permute-done((bf16[16,128,128]{2,1,0:T(8,128)(2,1)S(1)}, bf16[16,128,128]{2,1,0:T(8,128)(2,1)S(1)}, u32[]{:S(2)}, u32[]{:S(2)}) %collective-permute-start.7) | collective-permute-done | bytes 524320 | tf_op jit(solution)/shard_map/ppermute | solution.py:27
  36.8 0.4 all-to-all-done.wave
  37.2 6.4 %first_products.1 = (bf16[65,128,128]{2,1,0:T(8,128)(2,1)S(1)}, bf16[1,11,64,128]{3,2,1,0:T(8,128)(2,1)S(1)}, bf16[32,128,128]{2,1,0:T(8,128)(2,1)S(1)}) custom-call(s32[576]{0:T(1024)S(1)} %pad_add_fusion.1.listed_left, s32[2018]{0:T(1024)S(1)} %concatenate.16.listed_right.listed, bf16[32,128,128]{2,1,0:T(8,128)(2,1)S(1)} %all-to-all-done.wave, ...), custom_call_target="tpu_custom_call" | custom-call | tf_op jit(solution)/shard_map/first_products/pallas_call | solution.py:395
  43.6 1.6 %collective-permute-start.12 = (bf16[11,64,128]{2,1,0:T(8,128)(2,1)S(1)}, bf16[11,64,128]{2,1,0:T(8,128)(2,1)S(1)}, u32[]{:S(2)}, u32[]{:S(2)}) collective-permute-start(bf16[11,64,128]{2,1,0:T(8,128)(2,1)S(1)} %bitcast.27), channel_id=1, source_target_pairs={{0,16},{16,0},{1,17},{17,1},{2,18},{18,2},{3,19},{19,3},{4,20},{20... | collective-permute-start | bytes 540680 | tf_op jit(solution)/shard_map/ppermute | solution.py:447
  45.2 2.7 %both_products.1 = (bf16[1,5,64,128]{3,2,1,0:T(8,128)(2,1)S(1)}, f32[5,64,128]{2,1,0:T(8,128)S(1)}) custom-call(s32[2018]{0:T(1024)S(1)} %concatenate.16.listed_right.listed, bf16[65,128,128]{2,1,0:T(8,128)(2,1)S(1)} %get-tuple-element.18.inter, bf16[32,128,128]{2,1,0:T(8,128)(2,1)S(1)} %get-tuple-element.19.env), custom_call_target="tpu_custom_call" | custom-call | flops 1073741824 | bytes 12582912 | tf_op jit(solution)/shard_map/both_products/pallas_call | solution.py:415
  47.9 0.6 %collective-permute-start.13 = (bf16[5,64,128]{2,1,0:T(8,128)(2,1)S(1)}, bf16[5,64,128]{2,1,0:T(8,128)(2,1)S(1)}, u32[]{:S(2)}, u32[]{:S(2)}) collective-permute-start(bf16[5,64,128]{2,1,0:T(8,128)(2,1)S(1)} %bitcast.28), channel_id=1, source_target_pairs={{0,16},{16,0},{1,17},{17,1},{2,18},{18,2},{3,19},{19,3},{4,20},{20... | collective-permute-start | bytes 245768 | tf_op jit(solution)/shard_map/ppermute | solution.py:447
  48.5 3.9 %own_products.1.refs_0_ = f32[11,64,128]{2,1,0:T(8,128)S(1)} custom-call(s32[2018]{0:T(1024)S(1)} %concatenate.16.listed_right.listed, bf16[65,128,128]{2,1,0:T(8,128)(2,1)S(1)} %get-tuple-element.18.inter, bf16[32,128,128]{2,1,0:T(8,128)(2,1)S(1)} %get-tuple-element.19.env), custom_call_target="tpu_custom_call" | custom-call | flops 1073741824 | bytes 12582912 | tf_op jit(solution)/shard_map/own_products/pallas_call | solution.py:432
  52.4 0.1 collective-permute-done.13.refs_3_
  52.5 0.0 collective-permute-done.12.refs_2_
  52.5 1.0 %finish.1 = f32[16,2,64,128]{3,2,1,0:T(8,128)} custom-call(f32[11,64,128]{2,1,0:T(8,128)S(1)} %own_products.1.refs_0_, f32[5,64,128]{2,1,0:T(8,128)S(1)} %get-tuple-element.20.refs_1_, bf16[11,64,128]{2,1,0:T(8,128)(2,1)S(1)} %collective-permute-done.12.refs_2_, bf16[5,64,128]{2,1,0:T(8,128)(2,1)S(1)} %collective-permute-done.13.refs_3_), custom_call_target="tpu_custom_call" | custom-call | tf_op jit(solution)/shard_map/finish/pallas_call | solution.py:448
  (28 shorter events, 0.4 us)
Async XLA Ops:
  0.0 14.3 %copy-start.2 = (s32[1,1,96,3]{2,1,3,0:T(1,128)S(1)}, s32[1,1,96,3]{2,1,3,0:T(1,128)}, u32[]{:S(2)}) copy-start(s32[1,1,96,3]{2,1,3,0:T(1,128)} %param.10) | copy-start | bytes 3460
  0.0 14.3 %copy-start.1 = (s32[1,1,256,3]{2,1,3,0:T(1,128)S(1)}, s32[1,1,256,3]{2,1,3,0:T(1,128)}, u32[]{:S(2)}) copy-start(s32[1,1,256,3]{2,1,3,0:T(1,128)} %param.11) | copy-start | bytes 9220
  2.4 12.0 %copy-start = (bf16[2,128,128]{2,1,0:T(8,128)(2,1)S(1)}, bf16[2,128,128]{2,1,0:T(8,128)(2,1)}, u32[]{:S(2)}) copy-start(bf16[2,128,128]{2,1,0:T(8,128)(2,1)} %get-tuple-element.14.refs_0_) | copy-start | bytes 196612
  2.4 11.9 %collective-permute-start.2 = (bf16[2,128,128]{2,1,0:T(8,128)(2,1)}, bf16[2,128,128]{2,1,0:T(8,128)(2,1)S(1)}, u32[]{:S(2)}, u32[]{:S(2)}) collective-permute-start(bf16[2,128,128]{2,1,0:T(8,128)(2,1)} %get-tuple-element.14.refs_0_), channel_id=1, source_target_pairs={{0,12},{1,13},{2,14},{3,15},{4,8},{5,9},{6,10},{7,11},{8,4},{9,5},... | collective-permute-start | bytes 196616 | tf_op jit(solution)/shard_map/ppermute | solution.py:27
  7.5 6.8 %collective-permute-start.1 = (bf16[2,128,128]{2,1,0:T(8,128)(2,1)}, bf16[2,128,128]{2,1,0:T(8,128)(2,1)S(1)}, u32[]{:S(2)}, u32[]{:S(2)}) collective-permute-start(bf16[2,128,128]{2,1,0:T(8,128)(2,1)} %get-tuple-element.14.refs_0_), channel_id=1, source_target_pairs={{0,8},{1,9},{2,10},{3,11},{4,12},{5,13},{6,14},{7,15},{8,0},{9,1},... | collective-permute-start | bytes 196616 | tf_op jit(solution)/shard_map/ppermute | solution.py:27
  7.5 6.8 %collective-permute-start = (bf16[2,128,128]{2,1,0:T(8,128)(2,1)}, bf16[2,128,128]{2,1,0:T(8,128)(2,1)S(1)}, u32[]{:S(2)}, u32[]{:S(2)}) collective-permute-start(bf16[2,128,128]{2,1,0:T(8,128)(2,1)} %get-tuple-element.14.refs_0_), channel_id=1, source_target_pairs={{0,4},{1,5},{2,6},{3,7},{4,0},{5,1},{6,2},{7,3},{8,12},{9,13},{10,... | collective-permute-start | bytes 196616 | tf_op jit(solution)/shard_map/ppermute | solution.py:27
  8.2 29.0 %all-to-all-start = ((bf16[32,128,128]{2,1,0:T(8,128)(2,1)}), bf16[32,128,128]{2,1,0:T(8,128)(2,1)S(1)}, u32[]{:S(2)}, u32[]{:S(2)}) async-start(bf16[32,128,128]{2,1,0:T(8,128)(2,1)} %get-tuple-element.16), calls=%async_computation | async-start | bytes 2097152 | tf_op jit(solution)/shard_map/all_to_all | solution.py:332
  14.4 17.1 %collective-permute-start.9 = (bf16[4,128,128]{2,1,0:T(8,128)(2,1)S(1)}, bf16[4,128,128]{2,1,0:T(8,128)(2,1)S(1)}, u32[]{:S(2)}, u32[]{:S(2)}) collective-permute-start(bf16[4,128,128]{2,1,0:T(8,128)(2,1)S(1)} %get-tuple-element.17), channel_id=1, source_target_pairs={{0,2},{1,17},{2,0},{3,19},{4,6},{5,21},{6,4},{7,23},{8,10},{9,25},... | collective-permute-start | bytes 393224 | tf_op jit(solution)/shard_map/ppermute | solution.py:35
  16.4 10.1 %collective-permute-start.8 = (bf16[4,128,128]{2,1,0:T(8,128)(2,1)S(1)}, bf16[4,128,128]{2,1,0:T(8,128)(2,1)S(1)}, u32[]{:S(2)}, u32[]{:S(2)}) collective-permute-start(bf16[4,128,128]{2,1,0:T(8,128)(2,1)S(1)} %get-tuple-element.17), channel_id=1, source_target_pairs={{0,16},{1,3},{2,18},{3,1},{4,20},{5,7},{6,22},{7,5},{8,24},{9,11},... | collective-permute-start | bytes 393224 | tf_op jit(solution)/shard_map/ppermute | solution.py:35
  17.9 13.6 %collective-permute-start.5 = (bf16[4,128,128]{2,1,0:T(8,128)(2,1)S(1)}, bf16[4,128,128]{2,1,0:T(8,128)(2,1)S(1)}, u32[]{:S(2)}, u32[]{:S(2)}) collective-permute-start(bf16[4,128,128]{2,1,0:T(8,128)(2,1)S(1)} %get-tuple-element.15.after), channel_id=1, source_target_pairs={{0,2},{1,17},{2,0},{3,19},{4,6},{5,21},{6,4},{7,23},{8,10},{9,25},... | collective-permute-start | bytes 393224 | tf_op jit(solution)/shard_map/ppermute | solution.py:35
  18.0 9.1 %collective-permute-start.4 = (bf16[4,128,128]{2,1,0:T(8,128)(2,1)S(1)}, bf16[4,128,128]{2,1,0:T(8,128)(2,1)S(1)}, u32[]{:S(2)}, u32[]{:S(2)}) collective-permute-start(bf16[4,128,128]{2,1,0:T(8,128)(2,1)S(1)} %get-tuple-element.15.after), channel_id=1, source_target_pairs={{0,16},{1,3},{2,18},{3,1},{4,20},{5,7},{6,22},{7,5},{8,24},{9,11},... | collective-permute-start | bytes 393224 | tf_op jit(solution)/shard_map/ppermute | solution.py:35
  18.5 5.8 %collective-permute-start.3 = (s32[1,8,256]{2,1,0:T(8,128)S(1)}, s32[1,8,256]{2,1,0:T(8,128)S(1)}, u32[]{:S(2)}, u32[]{:S(2)}) collective-permute-start(s32[1,8,256]{2,1,0:T(8,128)S(1)} %bitcast.22), channel_id=1, source_target_pairs={{0,16},{16,0},{1,17},{17,1},{2,18},{18,2},{3,19},{19,3},{4,20},{20... | collective-permute-start | bytes 24584 | tf_op jit(solution)/shard_map/ppermute | solution.py:27
  26.5 6.4 %collective-permute-start.10 = (bf16[4,128,128]{2,1,0:T(8,128)(2,1)S(1)}, bf16[4,128,128]{2,1,0:T(8,128)(2,1)S(1)}, u32[]{:S(2)}, u32[]{:S(2)}) collective-permute-start(bf16[4,128,128]{2,1,0:T(8,128)(2,1)S(1)} %collective-permute-done.8), channel_id=1, source_target_pairs={{0,2},{1,17},{2,0},{3,19},{4,6},{5,21},{6,4},{7,23},{8,10},{9,25},... | collective-permute-start | bytes 393224 | tf_op jit(solution)/shard_map/ppermute | solution.py:35
  27.1 7.1 %collective-permute-start.6 = (bf16[4,128,128]{2,1,0:T(8,128)(2,1)S(1)}, bf16[4,128,128]{2,1,0:T(8,128)(2,1)S(1)}, u32[]{:S(2)}, u32[]{:S(2)}) collective-permute-start(bf16[4,128,128]{2,1,0:T(8,128)(2,1)S(1)} %collective-permute-done.4), channel_id=1, source_target_pairs={{0,2},{1,17},{2,0},{3,19},{4,6},{5,21},{6,4},{7,23},{8,10},{9,25},... | collective-permute-start | bytes 393224 | tf_op jit(solution)/shard_map/ppermute | solution.py:35
  32.9 2.6 %collective-permute-start.11 = (bf16[16,128,128]{2,1,0:T(8,128)(2,1)S(1)}, bf16[16,128,128]{2,1,0:T(8,128)(2,1)S(1)}, u32[]{:S(2)}, u32[]{:S(2)}) collective-permute-start(bf16[16,128,128]{2,1,0:T(8,128)(2,1)S(1)} %constant_dynamic-update-slice_fusion.4.here_right), channel_id=1, source_target_pairs={{0,1},{1,0},{2,3},{3,2},{4,5},{5,4},{6,7},{7,6},{8,9},{9,8},{10,11... | collective-permute-start | bytes 1572872 | tf_op jit(solution)/shard_map/ppermute | solution.py:27
  34.3 2.5 %collective-permute-start.7 = (bf16[16,128,128]{2,1,0:T(8,128)(2,1)S(1)}, bf16[16,128,128]{2,1,0:T(8,128)(2,1)S(1)}, u32[]{:S(2)}, u32[]{:S(2)}) collective-permute-start(bf16[16,128,128]{2,1,0:T(8,128)(2,1)S(1)} %constant_dynamic-update-slice_fusion.here_left), channel_id=1, source_target_pairs={{0,1},{1,0},{2,3},{3,2},{4,5},{5,4},{6,7},{7,6},{8,9},{9,8},{10,11... | collective-permute-start | bytes 1572872 | tf_op jit(solution)/shard_map/ppermute | solution.py:27
  43.6 8.9 %collective-permute-start.12 = (bf16[11,64,128]{2,1,0:T(8,128)(2,1)S(1)}, bf16[11,64,128]{2,1,0:T(8,128)(2,1)S(1)}, u32[]{:S(2)}, u32[]{:S(2)}) collective-permute-start(bf16[11,64,128]{2,1,0:T(8,128)(2,1)S(1)} %bitcast.27), channel_id=1, source_target_pairs={{0,16},{16,0},{1,17},{17,1},{2,18},{18,2},{3,19},{19,3},{4,20},{20... | collective-permute-start | bytes 540680 | tf_op jit(solution)/shard_map/ppermute | solution.py:447
  47.9 4.6 %collective-permute-start.13 = (bf16[5,64,128]{2,1,0:T(8,128)(2,1)S(1)}, bf16[5,64,128]{2,1,0:T(8,128)(2,1)S(1)}, u32[]{:S(2)}, u32[]{:S(2)}) collective-permute-start(bf16[5,64,128]{2,1,0:T(8,128)(2,1)S(1)} %bitcast.28), channel_id=1, source_target_pairs={{0,16},{16,0},{1,17},{17,1},{2,18},{18,2},{3,19},{19,3},{4,20},{20... | collective-permute-start | bytes 245768 | tf_op jit(solution)/shard_map/ppermute | solution.py:447

commit v8 on v7

--- a/solution.py
+++ b/solution.py
@@ -156,7 +156,7 @@
             total[place] += product
 
     turn = RIGHT_UNROLL * DEPTH
-    for width in (4, 2, 1):
+    for width in (8, 4, 2, 1):
         rounds = (end - begin) // width
 
         @pl.loop(0, rounds)

time: 54.5 us -> 54.5 us (level)
  no operation moved by 1% of the time
where the time goes in v8:
time: 54.5 us; the launch traced here: 53.9 us
  starting transfers between devices  22.8 us (42%)
  Pallas kernels  16.3 us (30%)
  waiting for transfers between devices  11.9 us (22%)
  other arithmetic  1.67 us (3%)
  local copies, waits for them, and re-layouts  0.74 us (1%)
    ppermute x6, starting transfers between devices, swap(): return lax.ppermute(value, axis, [(i, i ^ mask) for i in range(size)])  8.34 us
    pallas_call x1, Pallas kernels, shards(): pl.pallas_call(functools.partial(first_kernel, left_count, slots, near),...  6.28 us
    ppermute x6, starting transfers between devices, cross(): return lax.ppermute(value, ('term', 'sector'), pairs)  6.21 us
    all_to_all x1, starting transfers between devices, shards(): lax.all_to_all(outgoing, 'sector', split_axis=0, concat_axis=0, tiled=True)  6.08 us
    ppermute x6, waiting for transfers between devices, swap(): return lax.ppermute(value, axis, [(i, i ^ mask) for i in range(size)])  5.65 us
    ppermute x6, waiting for transfers between devices, cross(): return lax.ppermute(value, ('term', 'sector'), pairs)  5.49 us
    pallas_call x1, Pallas kernels, shards(): pl.pallas_call(functools.partial(own_kernel, slots, vectors), out_shape=j...  3.74 us
    pallas_call x1, Pallas kernels, shards(): pl.pallas_call(functools.partial(both_kernel, slots, cut), out_shape=(sen...  2.9 us
  transfers between devices with their start and end apart: 15, of which 7 were waited for; matrix products, arithmetic and copies ran while one was open for 4% of the time, Pallas kernels for 12%

profile of v8, /device:TPU:0, one launch (start us, length us, event | category | flops | bytes accessed | tf_op | source)
XLA Modules:
  0.0 53.9 jit_solution(1075545553601775578)
XLA Ops:
  0.0 0.0 copy-start.2
  0.0 0.0 copy-start.1
  0.0 2.4 %pack.1 = (bf16[32,128,128]{2,1,0:T(8,128)(2,1)}, bf16[2,128,128]{2,1,0:T(8,128)(2,1)}) custom-call(s32[1,32]{1,0:T(1,128)} %listed.1, bf16[16,2,128,128]{3,2,1,0:T(8,128)(2,1)} %wave.1, bf16[1,1,128,128]{3,2,1,0:T(8,128)(2,1)} %left.1, bf16[1,1,128,128]{3,2,1,0:T(8,128)(2,1)} %right.1), custom_call_target="tpu_custom_call" | custom-call | tf_op jit(solution)/shard_map/pack/pallas_call | solution.py:315
  2.4 0.0 copy-start
  2.4 5.1 %collective-permute-start.2 = (bf16[2,128,128]{2,1,0:T(8,128)(2,1)}, bf16[2,128,128]{2,1,0:T(8,128)(2,1)S(1)}, u32[]{:S(2)}, u32[]{:S(2)}) collective-permute-start(bf16[2,128,128]{2,1,0:T(8,128)(2,1)} %get-tuple-element.14.refs_0_), channel_id=1, source_target_pairs={{0,12},{1,13},{2,14},{3,15},{4,8},{5,9},{6,10},{7,11},{8,4},{9,5},... | collective-permute-start | bytes 196616 | tf_op jit(solution)/shard_map/ppermute | solution.py:27
  7.5 0.0 collective-permute-start.1
  7.5 0.6 %collective-permute-start = (bf16[2,128,128]{2,1,0:T(8,128)(2,1)}, bf16[2,128,128]{2,1,0:T(8,128)(2,1)S(1)}, u32[]{:S(2)}, u32[]{:S(2)}) collective-permute-start(bf16[2,128,128]{2,1,0:T(8,128)(2,1)} %get-tuple-element.14.refs_0_), channel_id=1, source_target_pairs={{0,4},{1,5},{2,6},{3,7},{4,0},{5,1},{6,2},{7,3},{8,12},{9,13},{10,... | collective-permute-start | bytes 196616 | tf_op jit(solution)/shard_map/ppermute | solution.py:27
  8.2 6.1 %all-to-all-start = ((bf16[32,128,128]{2,1,0:T(8,128)(2,1)}), bf16[32,128,128]{2,1,0:T(8,128)(2,1)S(1)}, u32[]{:S(2)}, u32[]{:S(2)}) async-start(bf16[32,128,128]{2,1,0:T(8,128)(2,1)} %get-tuple-element.16), calls=%async_computation | async-start | bytes 2097152 | tf_op jit(solution)/shard_map/all_to_all | solution.py:332
  14.3 0.0 copy-done.2
  14.3 0.0 copy-done.1
  14.3 0.0 collective-permute-done.2.refs_3_
  14.3 0.0 collective-permute-done.1.refs_2_
  14.4 0.0 collective-permute-done.refs_1_
  14.4 0.0 copy-done
  14.4 2.0 %collective-permute-start.9 = (bf16[4,128,128]{2,1,0:T(8,128)(2,1)S(1)}, bf16[4,128,128]{2,1,0:T(8,128)(2,1)S(1)}, u32[]{:S(2)}, u32[]{:S(2)}) collective-permute-start(bf16[4,128,128]{2,1,0:T(8,128)(2,1)S(1)} %get-tuple-element.17), channel_id=1, source_target_pairs={{0,2},{1,17},{2,0},{3,19},{4,6},{5,21},{6,4},{7,23},{8,10},{9,25},... | collective-permute-start | bytes 393224 | tf_op jit(solution)/shard_map/ppermute | solution.py:35
  16.4 1.5 %collective-permute-start.8 = (bf16[4,128,128]{2,1,0:T(8,128)(2,1)S(1)}, bf16[4,128,128]{2,1,0:T(8,128)(2,1)S(1)}, u32[]{:S(2)}, u32[]{:S(2)}) collective-permute-start(bf16[4,128,128]{2,1,0:T(8,128)(2,1)S(1)} %get-tuple-element.17), channel_id=1, source_target_pairs={{0,16},{1,3},{2,18},{3,1},{4,20},{5,7},{6,22},{7,5},{8,24},{9,11},... | collective-permute-start | bytes 393224 | tf_op jit(solution)/shard_map/ppermute | solution.py:35
  17.9 0.1 collective-permute-start.5
  18.0 0.5 collective-permute-start.4
  18.5 1.5 %collective-permute-start.3 = (s32[1,8,256]{2,1,0:T(8,128)S(1)}, s32[1,8,256]{2,1,0:T(8,128)S(1)}, u32[]{:S(2)}, u32[]{:S(2)}) collective-permute-start(s32[1,8,256]{2,1,0:T(8,128)S(1)} %bitcast.22), channel_id=1, source_target_pairs={{0,16},{16,0},{1,17},{17,1},{2,18},{18,2},{3,19},{19,3},{4,20},{20... | collective-permute-start | bytes 24584 | tf_op jit(solution)/shard_map/ppermute | solution.py:27
  20.1 4.3 %collective-permute-done.3 = s32[1,8,256]{2,1,0:T(8,128)S(1)} collective-permute-done((s32[1,8,256]{2,1,0:T(8,128)S(1)}, s32[1,8,256]{2,1,0:T(8,128)S(1)}, u32[]{:S(2)}, u32[]{:S(2)}) %collective-permute-start.3) | collective-permute-done | bytes 8224 | tf_op jit(solution)/shard_map/ppermute | solution.py:27
  24.4 0.1 convert_reduce_fusion.1
  24.5 0.3 convert_reduce_fusion
  24.8 0.1 select_reduce_fusion.4
  24.9 0.1 select_reduce_fusion.3
  25.1 0.6 %select_reduce_fusion = (s32[672]{0:T(1024)S(1)}, s32[672]{0:T(1024)S(1)}, s32[672]{0:T(1024)S(1)}) fusion(s32[512]{0:T(512)S(1)} %broadcast_add_fusion.2, s32[512]{0:T(512)S(1)} %add.136, s32[512]{0:T(512)S(1)} %get-tuple-element.38, s32[512]{0:T(512)S(1)} %get-tuple-element.39), kind=kLoop, calls=%fused_computation | loop fusion | flops 2406432 | bytes 16256 | tf_op jit(solution)/shard_map/reduce_sum | solution.py:129
  25.8 0.1 eq.82
  25.9 0.1 and.117
  25.9 0.1 squeeze.27
  26.0 0.1 squeeze.26
  26.1 0.1 mul.112
  26.2 0.1 shift_right_arithmetic.43
  26.3 0.2 fusion.8
  26.5 0.0 collective-permute-done.8
  26.5 0.7 %collective-permute-start.10 = (bf16[4,128,128]{2,1,0:T(8,128)(2,1)S(1)}, bf16[4,128,128]{2,1,0:T(8,128)(2,1)S(1)}, u32[]{:S(2)}, u32[]{:S(2)}) collective-permute-start(bf16[4,128,128]{2,1,0:T(8,128)(2,1)S(1)} %collective-permute-done.8), channel_id=1, source_target_pairs={{0,2},{1,17},{2,0},{3,19},{4,6},{5,21},{6,4},{7,23},{8,10},{9,25},... | collective-permute-start | bytes 393224 | tf_op jit(solution)/shard_map/ppermute | solution.py:35
  27.1 0.0 collective-permute-done.4
  27.1 1.4 %collective-permute-start.6 = (bf16[4,128,128]{2,1,0:T(8,128)(2,1)S(1)}, bf16[4,128,128]{2,1,0:T(8,128)(2,1)S(1)}, u32[]{:S(2)}, u32[]{:S(2)}) collective-permute-start(bf16[4,128,128]{2,1,0:T(8,128)(2,1)S(1)} %collective-permute-done.4), channel_id=1, source_target_pairs={{0,2},{1,17},{2,0},{3,19},{4,6},{5,21},{6,4},{7,23},{8,10},{9,25},... | collective-permute-start | bytes 393224 | tf_op jit(solution)/shard_map/ppermute | solution.py:35
  28.6 2.8 %collective-permute-done.5 = bf16[4,128,128]{2,1,0:T(8,128)(2,1)S(1)} collective-permute-done((bf16[4,128,128]{2,1,0:T(8,128)(2,1)S(1)}, bf16[4,128,128]{2,1,0:T(8,128)(2,1)S(1)}, u32[]{:S(2)}, u32[]{:S(2)}) %collective-permute-start.5) | collective-permute-done | bytes 131104 | tf_op jit(solution)/shard_map/ppermute | solution.py:35
  31.5 0.0 collective-permute-done.9
  31.5 1.3 %collective-permute-done.10 = bf16[4,128,128]{2,1,0:T(8,128)(2,1)S(1)} collective-permute-done((bf16[4,128,128]{2,1,0:T(8,128)(2,1)S(1)}, bf16[4,128,128]{2,1,0:T(8,128)(2,1)S(1)}, u32[]{:S(2)}, u32[]{:S(2)}) %collective-permute-start.10) | collective-permute-done | bytes 131104 | tf_op jit(solution)/shard_map/ppermute | solution.py:35
  32.9 0.1 collective-permute-start.11
  32.9 1.3 %collective-permute-done.6 = bf16[4,128,128]{2,1,0:T(8,128)(2,1)S(1)} collective-permute-done((bf16[4,128,128]{2,1,0:T(8,128)(2,1)S(1)}, bf16[4,128,128]{2,1,0:T(8,128)(2,1)S(1)}, u32[]{:S(2)}, u32[]{:S(2)}) %collective-permute-start.6) | collective-permute-done | bytes 131104 | tf_op jit(solution)/shard_map/ppermute | solution.py:35
  34.3 1.0 %collective-permute-start.7 = (bf16[16,128,128]{2,1,0:T(8,128)(2,1)S(1)}, bf16[16,128,128]{2,1,0:T(8,128)(2,1)S(1)}, u32[]{:S(2)}, u32[]{:S(2)}) collective-permute-start(bf16[16,128,128]{2,1,0:T(8,128)(2,1)S(1)} %constant_dynamic-update-slice_fusion.here_left), channel_id=1, source_target_pairs={{0,1},{1,0},{2,3},{3,2},{4,5},{5,4},{6,7},{7,6},{8,9},{9,8},{10,11... | collective-permute-start | bytes 1572872 | tf_op jit(solution)/shard_map/ppermute | solution.py:27
  35.3 0.1 concatenate.16.listed_right.listed
  35.4 0.1 pad_add_fusion.1.listed_left
  35.5 0.0 collective-permute-done.11.there_right
  35.5 1.4 %collective-permute-done.7.there_left = bf16[16,128,128]{2,1,0:T(8,128)(2,1)S(1)} collective-permute-done((bf16[16,128,128]{2,1,0:T(8,128)(2,1)S(1)}, bf16[16,128,128]{2,1,0:T(8,128)(2,1)S(1)}, u32[]{:S(2)}, u32[]{:S(2)}) %collective-permute-start.7) | collective-permute-done | bytes 524320 | tf_op jit(solution)/shard_map/ppermute | solution.py:27
  36.8 0.4 all-to-all-done.wave
  37.2 6.3 %first_products.1 = (bf16[65,128,128]{2,1,0:T(8,128)(2,1)S(1)}, bf16[1,11,64,128]{3,2,1,0:T(8,128)(2,1)S(1)}, bf16[32,128,128]{2,1,0:T(8,128)(2,1)S(1)}) custom-call(s32[576]{0:T(1024)S(1)} %pad_add_fusion.1.listed_left, s32[2018]{0:T(1024)S(1)} %concatenate.16.listed_right.listed, bf16[32,128,128]{2,1,0:T(8,128)(2,1)S(1)} %all-to-all-done.wave, ...), custom_call_target="tpu_custom_call" | custom-call | tf_op jit(solution)/shard_map/first_products/pallas_call | solution.py:395
  43.5 1.6 %collective-permute-start.12 = (bf16[11,64,128]{2,1,0:T(8,128)(2,1)S(1)}, bf16[11,64,128]{2,1,0:T(8,128)(2,1)S(1)}, u32[]{:S(2)}, u32[]{:S(2)}) collective-permute-start(bf16[11,64,128]{2,1,0:T(8,128)(2,1)S(1)} %bitcast.27), channel_id=1, source_target_pairs={{0,16},{16,0},{1,17},{17,1},{2,18},{18,2},{3,19},{19,3},{4,20},{20... | collective-permute-start | bytes 540680 | tf_op jit(solution)/shard_map/ppermute | solution.py:447
  45.1 2.9 %both_products.1 = (bf16[1,5,64,128]{3,2,1,0:T(8,128)(2,1)S(1)}, f32[5,64,128]{2,1,0:T(8,128)S(1)}) custom-call(s32[2018]{0:T(1024)S(1)} %concatenate.16.listed_right.listed, bf16[65,128,128]{2,1,0:T(8,128)(2,1)S(1)} %get-tuple-element.18.inter, bf16[32,128,128]{2,1,0:T(8,128)(2,1)S(1)} %get-tuple-element.19.env), custom_call_target="tpu_custom_call" | custom-call | flops 1073741824 | bytes 12582912 | tf_op jit(solution)/shard_map/both_products/pallas_call | solution.py:415
  48.0 0.6 %collective-permute-start.13 = (bf16[5,64,128]{2,1,0:T(8,128)(2,1)S(1)}, bf16[5,64,128]{2,1,0:T(8,128)(2,1)S(1)}, u32[]{:S(2)}, u32[]{:S(2)}) collective-permute-start(bf16[5,64,128]{2,1,0:T(8,128)(2,1)S(1)} %bitcast.28), channel_id=1, source_target_pairs={{0,16},{16,0},{1,17},{17,1},{2,18},{18,2},{3,19},{19,3},{4,20},{20... | collective-permute-start | bytes 245768 | tf_op jit(solution)/shard_map/ppermute | solution.py:447
  48.6 3.7 %own_products.1.refs_0_ = f32[11,64,128]{2,1,0:T(8,128)S(1)} custom-call(s32[2018]{0:T(1024)S(1)} %concatenate.16.listed_right.listed, bf16[65,128,128]{2,1,0:T(8,128)(2,1)S(1)} %get-tuple-element.18.inter, bf16[32,128,128]{2,1,0:T(8,128)(2,1)S(1)} %get-tuple-element.19.env), custom_call_target="tpu_custom_call" | custom-call | flops 1073741824 | bytes 12582912 | tf_op jit(solution)/shard_map/own_products/pallas_call | solution.py:432
  52.3 0.4 collective-permute-done.13.refs_3_
  52.7 0.0 collective-permute-done.12.refs_2_
  52.7 1.0 %finish.1 = f32[16,2,64,128]{3,2,1,0:T(8,128)} custom-call(f32[11,64,128]{2,1,0:T(8,128)S(1)} %own_products.1.refs_0_, f32[5,64,128]{2,1,0:T(8,128)S(1)} %get-tuple-element.20.refs_1_, bf16[11,64,128]{2,1,0:T(8,128)(2,1)S(1)} %collective-permute-done.12.refs_2_, bf16[5,64,128]{2,1,0:T(8,128)(2,1)S(1)} %collective-permute-done.13.refs_3_), custom_call_target="tpu_custom_call" | custom-call | tf_op jit(solution)/shard_map/finish/pallas_call | solution.py:448
  (28 shorter events, 0.4 us)
Async XLA Ops:
  0.0 14.3 %copy-start.2 = (s32[1,1,96,3]{2,1,3,0:T(1,128)S(1)}, s32[1,1,96,3]{2,1,3,0:T(1,128)}, u32[]{:S(2)}) copy-start(s32[1,1,96,3]{2,1,3,0:T(1,128)} %param.10) | copy-start | bytes 3460
  0.0 14.3 %copy-start.1 = (s32[1,1,256,3]{2,1,3,0:T(1,128)S(1)}, s32[1,1,256,3]{2,1,3,0:T(1,128)}, u32[]{:S(2)}) copy-start(s32[1,1,256,3]{2,1,3,0:T(1,128)} %param.11) | copy-start | bytes 9220
  2.4 12.0 %copy-start = (bf16[2,128,128]{2,1,0:T(8,128)(2,1)S(1)}, bf16[2,128,128]{2,1,0:T(8,128)(2,1)}, u32[]{:S(2)}) copy-start(bf16[2,128,128]{2,1,0:T(8,128)(2,1)} %get-tuple-element.14.refs_0_) | copy-start | bytes 196612
  2.4 11.9 %collective-permute-start.2 = (bf16[2,128,128]{2,1,0:T(8,128)(2,1)}, bf16[2,128,128]{2,1,0:T(8,128)(2,1)S(1)}, u32[]{:S(2)}, u32[]{:S(2)}) collective-permute-start(bf16[2,128,128]{2,1,0:T(8,128)(2,1)} %get-tuple-element.14.refs_0_), channel_id=1, source_target_pairs={{0,12},{1,13},{2,14},{3,15},{4,8},{5,9},{6,10},{7,11},{8,4},{9,5},... | collective-permute-start | bytes 196616 | tf_op jit(solution)/shard_map/ppermute | solution.py:27
  7.5 6.8 %collective-permute-start.1 = (bf16[2,128,128]{2,1,0:T(8,128)(2,1)}, bf16[2,128,128]{2,1,0:T(8,128)(2,1)S(1)}, u32[]{:S(2)}, u32[]{:S(2)}) collective-permute-start(bf16[2,128,128]{2,1,0:T(8,128)(2,1)} %get-tuple-element.14.refs_0_), channel_id=1, source_target_pairs={{0,8},{1,9},{2,10},{3,11},{4,12},{5,13},{6,14},{7,15},{8,0},{9,1},... | collective-permute-start | bytes 196616 | tf_op jit(solution)/shard_map/ppermute | solution.py:27
  7.5 6.8 %collective-permute-start = (bf16[2,128,128]{2,1,0:T(8,128)(2,1)}, bf16[2,128,128]{2,1,0:T(8,128)(2,1)S(1)}, u32[]{:S(2)}, u32[]{:S(2)}) collective-permute-start(bf16[2,128,128]{2,1,0:T(8,128)(2,1)} %get-tuple-element.14.refs_0_), channel_id=1, source_target_pairs={{0,4},{1,5},{2,6},{3,7},{4,0},{5,1},{6,2},{7,3},{8,12},{9,13},{10,... | collective-permute-start | bytes 196616 | tf_op jit(solution)/shard_map/ppermute | solution.py:27
  8.2 29.0 %all-to-all-start = ((bf16[32,128,128]{2,1,0:T(8,128)(2,1)}), bf16[32,128,128]{2,1,0:T(8,128)(2,1)S(1)}, u32[]{:S(2)}, u32[]{:S(2)}) async-start(bf16[32,128,128]{2,1,0:T(8,128)(2,1)} %get-tuple-element.16), calls=%async_computation | async-start | bytes 2097152 | tf_op jit(solution)/shard_map/all_to_all | solution.py:332
  14.4 17.1 %collective-permute-start.9 = (bf16[4,128,128]{2,1,0:T(8,128)(2,1)S(1)}, bf16[4,128,128]{2,1,0:T(8,128)(2,1)S(1)}, u32[]{:S(2)}, u32[]{:S(2)}) collective-permute-start(bf16[4,128,128]{2,1,0:T(8,128)(2,1)S(1)} %get-tuple-element.17), channel_id=1, source_target_pairs={{0,2},{1,17},{2,0},{3,19},{4,6},{5,21},{6,4},{7,23},{8,10},{9,25},... | collective-permute-start | bytes 393224 | tf_op jit(solution)/shard_map/ppermute | solution.py:35
  16.4 10.1 %collective-permute-start.8 = (bf16[4,128,128]{2,1,0:T(8,128)(2,1)S(1)}, bf16[4,128,128]{2,1,0:T(8,128)(2,1)S(1)}, u32[]{:S(2)}, u32[]{:S(2)}) collective-permute-start(bf16[4,128,128]{2,1,0:T(8,128)(2,1)S(1)} %get-tuple-element.17), channel_id=1, source_target_pairs={{0,16},{1,3},{2,18},{3,1},{4,20},{5,7},{6,22},{7,5},{8,24},{9,11},... | collective-permute-start | bytes 393224 | tf_op jit(solution)/shard_map/ppermute | solution.py:35
  17.9 13.6 %collective-permute-start.5 = (bf16[4,128,128]{2,1,0:T(8,128)(2,1)S(1)}, bf16[4,128,128]{2,1,0:T(8,128)(2,1)S(1)}, u32[]{:S(2)}, u32[]{:S(2)}) collective-permute-start(bf16[4,128,128]{2,1,0:T(8,128)(2,1)S(1)} %get-tuple-element.15.after), channel_id=1, source_target_pairs={{0,2},{1,17},{2,0},{3,19},{4,6},{5,21},{6,4},{7,23},{8,10},{9,25},... | collective-permute-start | bytes 393224 | tf_op jit(solution)/shard_map/ppermute | solution.py:35
  18.0 9.1 %collective-permute-start.4 = (bf16[4,128,128]{2,1,0:T(8,128)(2,1)S(1)}, bf16[4,128,128]{2,1,0:T(8,128)(2,1)S(1)}, u32[]{:S(2)}, u32[]{:S(2)}) collective-permute-start(bf16[4,128,128]{2,1,0:T(8,128)(2,1)S(1)} %get-tuple-element.15.after), channel_id=1, source_target_pairs={{0,16},{1,3},{2,18},{3,1},{4,20},{5,7},{6,22},{7,5},{8,24},{9,11},... | collective-permute-start | bytes 393224 | tf_op jit(solution)/shard_map/ppermute | solution.py:35
  18.5 5.8 %collective-permute-start.3 = (s32[1,8,256]{2,1,0:T(8,128)S(1)}, s32[1,8,256]{2,1,0:T(8,128)S(1)}, u32[]{:S(2)}, u32[]{:S(2)}) collective-permute-start(s32[1,8,256]{2,1,0:T(8,128)S(1)} %bitcast.22), channel_id=1, source_target_pairs={{0,16},{16,0},{1,17},{17,1},{2,18},{18,2},{3,19},{19,3},{4,20},{20... | collective-permute-start | bytes 24584 | tf_op jit(solution)/shard_map/ppermute | solution.py:27
  26.5 6.4 %collective-permute-start.10 = (bf16[4,128,128]{2,1,0:T(8,128)(2,1)S(1)}, bf16[4,128,128]{2,1,0:T(8,128)(2,1)S(1)}, u32[]{:S(2)}, u32[]{:S(2)}) collective-permute-start(bf16[4,128,128]{2,1,0:T(8,128)(2,1)S(1)} %collective-permute-done.8), channel_id=1, source_target_pairs={{0,2},{1,17},{2,0},{3,19},{4,6},{5,21},{6,4},{7,23},{8,10},{9,25},... | collective-permute-start | bytes 393224 | tf_op jit(solution)/shard_map/ppermute | solution.py:35
  27.1 7.1 %collective-permute-start.6 = (bf16[4,128,128]{2,1,0:T(8,128)(2,1)S(1)}, bf16[4,128,128]{2,1,0:T(8,128)(2,1)S(1)}, u32[]{:S(2)}, u32[]{:S(2)}) collective-permute-start(bf16[4,128,128]{2,1,0:T(8,128)(2,1)S(1)} %collective-permute-done.4), channel_id=1, source_target_pairs={{0,2},{1,17},{2,0},{3,19},{4,6},{5,21},{6,4},{7,23},{8,10},{9,25},... | collective-permute-start | bytes 393224 | tf_op jit(solution)/shard_map/ppermute | solution.py:35
  32.9 2.6 %collective-permute-start.11 = (bf16[16,128,128]{2,1,0:T(8,128)(2,1)S(1)}, bf16[16,128,128]{2,1,0:T(8,128)(2,1)S(1)}, u32[]{:S(2)}, u32[]{:S(2)}) collective-permute-start(bf16[16,128,128]{2,1,0:T(8,128)(2,1)S(1)} %constant_dynamic-update-slice_fusion.4.here_right), channel_id=1, source_target_pairs={{0,1},{1,0},{2,3},{3,2},{4,5},{5,4},{6,7},{7,6},{8,9},{9,8},{10,11... | collective-permute-start | bytes 1572872 | tf_op jit(solution)/shard_map/ppermute | solution.py:27
  34.3 2.5 %collective-permute-start.7 = (bf16[16,128,128]{2,1,0:T(8,128)(2,1)S(1)}, bf16[16,128,128]{2,1,0:T(8,128)(2,1)S(1)}, u32[]{:S(2)}, u32[]{:S(2)}) collective-permute-start(bf16[16,128,128]{2,1,0:T(8,128)(2,1)S(1)} %constant_dynamic-update-slice_fusion.here_left), channel_id=1, source_target_pairs={{0,1},{1,0},{2,3},{3,2},{4,5},{5,4},{6,7},{7,6},{8,9},{9,8},{10,11... | collective-permute-start | bytes 1572872 | tf_op jit(solution)/shard_map/ppermute | solution.py:27
  43.5 9.2 %collective-permute-start.12 = (bf16[11,64,128]{2,1,0:T(8,128)(2,1)S(1)}, bf16[11,64,128]{2,1,0:T(8,128)(2,1)S(1)}, u32[]{:S(2)}, u32[]{:S(2)}) collective-permute-start(bf16[11,64,128]{2,1,0:T(8,128)(2,1)S(1)} %bitcast.27), channel_id=1, source_target_pairs={{0,16},{16,0},{1,17},{17,1},{2,18},{18,2},{3,19},{19,3},{4,20},{20... | collective-permute-start | bytes 540680 | tf_op jit(solution)/shard_map/ppermute | solution.py:447
  48.0 4.7 %collective-permute-start.13 = (bf16[5,64,128]{2,1,0:T(8,128)(2,1)S(1)}, bf16[5,64,128]{2,1,0:T(8,128)(2,1)S(1)}, u32[]{:S(2)}, u32[]{:S(2)}) collective-permute-start(bf16[5,64,128]{2,1,0:T(8,128)(2,1)S(1)} %bitcast.28), channel_id=1, source_target_pairs={{0,16},{16,0},{1,17},{17,1},{2,18},{18,2},{3,19},{19,3},{4,20},{20... | collective-permute-start | bytes 245768 | tf_op jit(solution)/shard_map/ppermute | solution.py:447
